TPU v7x, 32 devices: a whole 2x2x4 slice. The times are simulated.
32 devices in a mesh: gen: 8 (over z, y), dat: 4 (over x, core).
Axes of the slice: x: 2, y: 2, z: 4, core: 2. Of those that a mesh axis runs over, the one named last changes fastest.
Arguments:
- gen_samples: bfloat16 [32768, 256], P(('gen', 'dat')), may hold values from -6 to 6
- data_samples: bfloat16 [3072, 256], P(('dat', 'gen')), may hold values from -6 to 6
- data_potential: float32 [3072], P(('dat', 'gen')), may hold values from -1 to 10
Outputs:
- gen_potential: float32 [32768], P(('gen', 'dat'))
- new_data_potential: float32 [3072], P(('dat', 'gen'))
All inputs are finite; a program needn't handle non-finite values.
Results may differ from a plain program's by a relative error of at most 0.0003.
Values may be sent and summed in bfloat16 or wider, within the bound.
No kernel may reach another device: no remote copies, remote signals or barrier semaphores. Data moves between devices by JAX's collectives and lax.ppermute only.
A program may use at most 64 MiB of HBM per device.

v0:
```python
import jax
import jax.numpy as jnp
from jax import lax
from jax.sharding import PartitionSpec as P

EPS = 0.05


def combined_all(shard, axis, combine):
    everything = jax.tree.map(lambda part: lax.all_gather(part, axis), shard)
    initial = jax.tree.map(lambda part: part[0], everything)

    def turn(k, so_far):
        return combine(so_far, jax.tree.map(lambda part: part[k], everything))

    return lax.fori_loop(1, lax.axis_size(axis), turn, initial)


def pair_combine(first, second):
    top = jnp.maximum(first[0], second[0])
    return (top, first[1] * jnp.exp(first[0] - top) + second[1] * jnp.exp(second[0] - top))


def per_device(gen_samples, data_samples, data_potential):
    gen_rows = lax.all_gather(gen_samples, "dat", axis=0, tiled=True)
    data_rows = lax.all_gather(data_samples, "gen", axis=0, tiled=True)
    potential = lax.all_gather(data_potential, "gen", axis=0, tiled=True)
    width = gen_rows.shape[1]
    rows = gen_rows.shape[0]
    cols = data_rows.shape[0]
    n_dat = lax.axis_size("dat")
    n_gen = lax.axis_size("gen")
    sq_cols = jnp.sum(data_rows.astype(jnp.float32) ** 2, axis=1)
    block = min(512, rows)
    count = rows // block
    gen_blocks = gen_rows.reshape(count, block, width)

    def block_cost(tile_rows):
        sq_rows = jnp.sum(tile_rows.astype(jnp.float32) ** 2, axis=1)
        cross = lax.dot_general(
            tile_rows, data_rows, (((1,), (1,)), ((), ())), preferred_element_type=jnp.float32
        )
        return (sq_rows[:, None] + sq_cols[None, :] - 2.0 * cross) / width

    def row_pass(tile_rows):
        scores = (potential[None, :] - block_cost(tile_rows)) / EPS
        top = jnp.max(scores, axis=1)
        return (top, jnp.sum(jnp.exp(scores - top[:, None]), axis=1))

    row_max, row_sum = lax.map(row_pass, gen_blocks)
    row_max = row_max.reshape(rows)
    row_sum = row_sum.reshape(rows)
    log_cols = jnp.log(jnp.float32(cols * n_dat))
    share = rows // n_dat
    whole_max, whole_sum = combined_all((row_max, row_sum), "dat", pair_combine)
    gen_full = -EPS * (whole_max + jnp.log(whole_sum) - log_cols)
    gen_potential = lax.dynamic_slice_in_dim(gen_full, lax.axis_index("dat") * share, share, 0)

    def column_pass(carry, item):
        tile_rows, pot = item
        run_max, run_sum = carry
        scores = (pot[:, None] - block_cost(tile_rows)) / EPS
        top = jnp.maximum(run_max, jnp.max(scores, axis=0))
        run_sum = run_sum * jnp.exp(run_max - top) + jnp.sum(jnp.exp(scores - top[None, :]), axis=0)
        return ((top, run_sum), None)

    start = (jnp.full((cols,), -1e30, jnp.float32), jnp.zeros((cols,), jnp.float32))
    (col_max, col_sum), _ = lax.scan(
        column_pass, start, (gen_blocks, gen_full.reshape(count, block))
    )
    log_rows = jnp.log(jnp.float32(rows * n_gen))
    col_share = cols // n_gen
    all_max, all_sum = combined_all((col_max, col_sum), "gen", pair_combine)
    own_max = lax.dynamic_slice_in_dim(all_max, lax.axis_index("gen") * col_share, col_share, 0)
    own_sum = lax.dynamic_slice_in_dim(all_sum, lax.axis_index("gen") * col_share, col_share, 0)
    new_data_potential = -EPS * (own_max + jnp.log(own_sum) - log_rows)
    return (gen_potential, new_data_potential)


def solution(mesh):
    in_specs = (P(("gen", "dat"), None), P(("dat", "gen"), None), P(("dat", "gen")))
    out_specs = (P(("gen", "dat")), P(("dat", "gen")))
    return jax.shard_map(
        per_device, mesh=mesh, in_specs=in_specs, out_specs=out_specs, check_vma=False
    )
```

profile of v0, /device:TPU:0, one launch (start us, length us, event | category | flops | bytes accessed | tf_op | source)
XLA Modules:
  0.0 195.1 jit_solution(7556670408598343798)
XLA Ops:
  7.2 0.7 all-gather.8.cloned.1.call-update
  8.0 1.3 dynamic-slice
  9.8 0.9 dynamic-update-slice
  10.7 23.1 %all-reduce = f32[768]{0:T(1024)S(1)} all-reduce(f32[768]{0:T(1024)S(1)} %dynamic-update-slice), channel_id=1, replica_groups=mesh['gen'=8,'dat'=4] {'gen'}, use_global_device_ids=true, to_apply=%add | all-reduce | flops 768 | bytes 6144
  33.8 31.2 %all_gather.29 = bf16[768,256]{1,0:T(8,128)(2,1)S(1)} all-gather(bf16[96,256]{1,0:T(8,128)(2,1)} %param.12), channel_id=1, replica_groups=mesh['gen'=8,'dat'=4] {'gen'}, dimensions={0}, use_global_device_ids=true | all-gather | bytes 442368 | tf_op jit(solution)/shard_map/all_gather | solution.py:26
  65.0 0.2 multiply_reduce_fusion.2
  65.2 26.0 %while.59 = (s32[]{:T(128)}, f32[8,512]{1,0:T(8,128)S(1)}, f32[8,512]{1,0:T(8,128)S(1)}, f32[768]{0:T(1024)S(1)}, bf16[8,512,256]{2,1,0:T(8,128)(2,1)}, /*index=...) while((s32[]{:T(128)}, f32[8,512]{1,0:T(8,128)S(1)}, f32[8,512]{1,0:T(8,128)S(1)}, ...), condition=%wide.region_5.6_spmd, body=%wide.region_1.5_spmd.sunk | while | flops 205257216 | bytes 4088425 | solution.py:50
  65.2 1.1 multiply_reduce_fusion.5
  66.3 1.6 fusion.17
  67.9 0.4 exponential_reduce_fusion.4
  68.5 1.1 multiply_reduce_fusion.5
  69.6 1.6 fusion.17
  71.2 0.4 exponential_reduce_fusion.4
  71.7 1.1 multiply_reduce_fusion.5
  72.8 1.6 fusion.17
  74.4 0.4 exponential_reduce_fusion.4
  75.0 1.1 multiply_reduce_fusion.5
  76.1 1.6 fusion.17
  77.7 0.4 exponential_reduce_fusion.4
  78.2 1.1 multiply_reduce_fusion.5
  79.3 1.6 fusion.17
  80.9 0.4 exponential_reduce_fusion.4
  81.5 1.1 multiply_reduce_fusion.5
  82.6 1.6 fusion.17
  84.2 0.4 exponential_reduce_fusion.4
  84.7 1.1 multiply_reduce_fusion.5
  85.8 1.6 fusion.17
  87.4 0.4 exponential_reduce_fusion.4
  88.0 1.1 multiply_reduce_fusion.5
  89.1 1.6 fusion.17
  90.7 0.4 exponential_reduce_fusion.4
  91.2 5.2 %all-gather.2 = f32[4,1,4096]{2,1,0:T(1,128)S(1)} all-gather(f32[1,1,4096]{2,1,0:T(1,128)S(1)} %reshape.30), channel_id=1, replica_groups=mesh['gen'=8,'dat'=4] {'dat'}, dimensions={0}, use_global_device_ids=true | all-gather | bytes 81920 | tf_op jit(solution)/shard_map/all_gather | solution.py:10
  96.6 5.2 %all-gather.3 = f32[4,1,4096]{2,1,0:T(1,128)S(1)} all-gather(f32[1,1,4096]{2,1,0:T(1,128)S(1)} %reshape.32), channel_id=1, replica_groups=mesh['gen'=8,'dat'=4] {'dat'}, dimensions={0}, use_global_device_ids=true | all-gather | bytes 81920 | tf_op jit(solution)/shard_map/all_gather | solution.py:10
  101.9 0.3 while.60
  102.2 23.7 %while.62 = (s32[]{:T(128)}, f32[768]{0:T(1024)S(1)}, f32[768]{0:T(1024)S(1)}, f32[8,512]{1,0:T(8,128)S(1)}, bf16[8,512,256]{2,1,0:T(8,128)(2,1)}, /*index=5*/f3...) while((s32[]{:T(128)}, f32[768]{0:T(1024)S(1)}, f32[768]{0:T(1024)S(1)}, ...), condition=%wide.region_12.13_spmd.clone, body=%wide.region_8.12_spmd.clone.sunk | while | flops 205262080 | bytes 4117104 | solution.py:68
  102.2 1.1 multiply_reduce_fusion.6
  103.3 1.5 fusion.19
  104.9 0.3 exponential_reduce_fusion.5
  105.2 1.1 multiply_reduce_fusion.6
  106.3 1.5 fusion.19
  107.8 0.3 exponential_reduce_fusion.5
  108.1 1.1 multiply_reduce_fusion.6
  109.2 1.5 fusion.19
  110.8 0.3 exponential_reduce_fusion.5
  111.1 1.1 multiply_reduce_fusion.6
  112.2 1.5 fusion.19
  113.7 0.3 exponential_reduce_fusion.5
  114.0 1.1 multiply_reduce_fusion.6
  115.2 1.5 fusion.19
  116.7 0.3 exponential_reduce_fusion.5
  117.0 1.1 multiply_reduce_fusion.6
  118.1 1.5 fusion.19
  119.7 0.3 exponential_reduce_fusion.5
  119.9 1.1 multiply_reduce_fusion.6
  121.1 1.5 fusion.19
  122.6 0.3 exponential_reduce_fusion.5
  122.9 1.1 multiply_reduce_fusion.6
  124.0 1.5 fusion.19
  125.6 0.3 exponential_reduce_fusion.5
  125.9 30.3 %all-gather.5 = f32[8,1,768]{2,1,0:T(1,128)S(1)} all-gather(f32[1,1,768]{2,1,0:T(1,128)S(1)} %reshape.36), channel_id=3, replica_groups=mesh['gen'=8,'dat'=4] {'gen'}, dimensions={0}, use_global_device_ids=true | all-gather | bytes 27648 | tf_op jit(solution)/shard_map/all_gather | solution.py:10
  156.2 30.3 %all-gather.4 = f32[8,1,768]{2,1,0:T(1,128)S(1)} all-gather(f32[1,1,768]{2,1,0:T(1,128)S(1)} %reshape.34), channel_id=2, replica_groups=mesh['gen'=8,'dat'=4] {'gen'}, dimensions={0}, use_global_device_ids=true | all-gather | bytes 27648 | tf_op jit(solution)/shard_map/all_gather | solution.py:10
  186.6 0.5 while.61
  187.1 0.6 dynamic_slice.60
  187.7 0.6 add_multiply_fusion.1
  (89 shorter events, 1.9 us)
Async XLA Ops:
  7.2 58.0 %all-gather.8.cloned.1.call-start = ((), (), s32[]{:S(2)}) async-start(), calls=%async_computation | async-start | bytes 2621440 | tf_op jit(solution)/shard_map/all_gather | solution.py:25
Sparse Core Ops, SparseCore 0:
  9.6 25.2 all-gather.7
where the time goes:
time: 196 us; the launch traced here: 195 us
  blocking collectives  125 us (64%)
  matrix products  25 us (13%)
  other arithmetic  23.9 us (12%)
  between operations  14.8 us (8%)
  local copies, waits for them, and re-layouts  4.26 us (2%)
    all_gather x4, blocking collectives, combined_all(): everything = jax.tree.map(lambda part: lax.all_gather(part, axis), shard)  71.2 us
    all_gather x1, blocking collectives, per_device(): data_rows = lax.all_gather(data_samples, 'gen', axis=0, tiled=True)  31.2 us
    dot_general x16, matrix products, block_cost(): lax.dot_general(tile_rows, data_rows, (((1,), (1,)), ((), ())), preferred...  25 us
    unnamed x1, blocking collectives  23.1 us
    reduce_sum x16, other arithmetic, block_cost(): sq_rows = jnp.sum(tile_rows.astype(jnp.float32) ** 2, axis=1)  17.6 us
  transfers between devices with their start and end apart: 1, of which 0 were waited for; matrix products, arithmetic and copies ran while one was open for 1% of the time, Pallas kernels for 0%

commit v1 on v0

v1 whole, which is shorter than its diff:
```python
import functools
import math

import jax
import jax.numpy as jnp
from jax import lax
from jax.experimental import pallas as pl
from jax.experimental.pallas import tpu as pltpu
from jax.sharding import PartitionSpec as P

EPS = 0.05
LOG2E = 1.4426950408889634
LN2 = 0.6931471805599453
SCALE = LOG2E / EPS
ALL = ("dat", "gen")
LANES = 128


def lane_chunks(width, step):
    return [(start, min(step, width - start)) for start in range(0, width, step)]


def sinkhorn_kernel(x_ref, y_ref, b_ref, f_ref, col_ref, t_ref, max_ref, sum_ref, *, block, chunk, shares):
    rows, width = x_ref.shape
    cols = y_ref.shape[0]
    alpha = 2.0 * SCALE / width
    max_ref[...] = jnp.full(max_ref.shape, -jnp.inf, jnp.float32)
    sum_ref[...] = jnp.zeros(sum_ref.shape, jnp.float32)

    def fold(values, op):
        out = values[:, :LANES]
        for start in range(LANES, values.shape[1], LANES):
            out = op(out, values[:, start : start + LANES])
        return out

    def step(index, carry):
        x = x_ref[pl.ds(pl.multiple_of(index * block, block), block), :]
        top = None
        for start, size in lane_chunks(cols, chunk):
            dots = lax.dot_general(
                x, y_ref[start : start + size, :], (((1,), (1,)), ((), ())), preferred_element_type=jnp.float32
            )
            t = alpha * dots + b_ref[:, start : start + size]
            t_ref[:, start : start + size] = t
            part = fold(t, jnp.maximum)
            top = part if top is None else jnp.maximum(top, part)
        row_top = jnp.max(top, axis=1, keepdims=True)
        total = None
        for start, size in lane_chunks(cols, chunk):
            part = fold(jnp.exp2(t_ref[:, start : start + size] - row_top), jnp.add)
            total = part if total is None else total + part
        row_lse = row_top + jnp.log2(jnp.sum(total, axis=1, keepdims=True))
        x32 = x.astype(jnp.float32)
        sq = jnp.sum(x32 * x32, axis=1, keepdims=True)
        f = sq / width - (EPS * LN2) * row_lse + EPS * math.log(cols)
        wide = jnp.broadcast_to(f, (block, LANES))
        for part in range(block // LANES):
            turned = wide[part * LANES : (part + 1) * LANES, :].T
            f_ref[pl.ds(index * (block // LANES) + part, 1), :] = turned[0:1, :]
        for start, size in lane_chunks(cols, chunk):
            here = slice(start, start + size)
            u = t_ref[:, here] - row_lse
            old = max_ref[:, here]
            new = jnp.maximum(old, jnp.max(u, axis=0, keepdims=True))
            max_ref[:, here] = new
            sum_ref[:, here] = sum_ref[:, here] * jnp.exp2(old - new) + jnp.sum(
                jnp.exp2(u - new), axis=0, keepdims=True
            )
        return carry

    lax.fori_loop(0, rows // block, step, 0)
    max_ref[...] = max_ref[...] + jnp.log2(sum_ref[...]) - b_ref[...]
    share = cols // shares
    for k in range(shares):
        col_ref[k : k + 1, :] = max_ref[:, k * share : (k + 1) * share]


def per_device(gen_samples, data_samples, data_potential):
    rows, width = gen_samples.shape
    shares = lax.axis_size("dat") * lax.axis_size("gen")
    share = data_samples.shape[0]
    cols = share * shares
    wide = data_samples.astype(jnp.float32)
    sq_own = jnp.sum(wide * wide, axis=1)
    bias = SCALE * (data_potential - sq_own / width)
    everything = lax.all_gather(data_samples, ALL, axis=0, tiled=True)
    biases = lax.all_gather(bias, ALL, axis=0, tiled=True).reshape(1, cols)
    block = min(256, rows)
    kernel = functools.partial(sinkhorn_kernel, block=block, chunk=256, shares=shares)
    f, col = pl.pallas_call(
        kernel,
        out_shape=(
            jax.ShapeDtypeStruct((rows // LANES, LANES), jnp.float32),
            jax.ShapeDtypeStruct((shares, share), jnp.float32),
        ),
        scratch_shapes=[
            pltpu.VMEM((block, cols), jnp.float32),
            pltpu.VMEM((1, cols), jnp.float32),
            pltpu.VMEM((1, cols), jnp.float32),
        ],
        compiler_params=pltpu.CompilerParams(vmem_limit_bytes=48 * 1024 * 1024),
        cost_estimate=pl.CostEstimate(
            flops=2 * rows * cols * width, bytes_accessed=2 * (rows + cols) * width, transcendentals=2 * rows * cols
        ),
    )(gen_samples, everything, biases)
    parts = lax.all_to_all(col, ALL, 0, 0, tiled=True)
    top = jnp.max(parts, axis=0)
    total = top + jnp.log2(jnp.sum(jnp.exp2(parts - top[None, :]), axis=0))
    new_data = sq_own / width - (EPS * LN2) * total + EPS * math.log(rows * shares / cols)
    return f.reshape(rows), new_data


def solution(mesh):
    in_specs = (P(("gen", "dat"), None), P(("dat", "gen"), None), P(("dat", "gen")))
    out_specs = (P(("gen", "dat")), P(("dat", "gen")))
    return jax.shard_map(per_device, mesh=mesh, in_specs=in_specs, out_specs=out_specs, check_vma=False)
```

time: 196 us -> 97.2 us (0.50)
  blocking collectives: 125 us -> 52.5 us
  matrix products: 25 us -> 0 us
  other arithmetic: 23.9 us -> 2.3 us
  waiting for transfers between devices: 0.7 us -> 15.8 us
  Pallas kernels: 0 us -> 7.82 us
    all_gather x5 -> x0, blocking collectives: 102 us -> none  [the longest x4 71.2 us: combined_all(): everything = jax.tree.map(lambda part: lax.all_gather(part, axis), shard)]
    dot_general x16 -> x0, matrix products: 25 us -> none  [block_cost(): lax.dot_general(tile_rows, data_rows, (((1,), (1,)), ((), ())), preferred...]
    reduce_sum x33 -> x2, other arithmetic: 23 us -> 0.94 us  [the longest x1 0.91 us: per_device(): sq_own = jnp.sum(wide * wide, axis=1)]
    unnamed x1, blocking collectives: 23.1 us -> 42.1 us
    all_gather x1, waiting for transfers between devices: 0.02 us -> 15.1 us  [per_device(): everything = lax.all_gather(data_samples, ALL, axis=0, tiled=True)]
    all_to_all x0 -> x1, blocking collectives: none -> 10.4 us  [per_device(): parts = lax.all_to_all(col, ALL, 0, 0, tiled=True)]
    pallas_call x0 -> x1, Pallas kernels: none -> 7.82 us  [per_device(): pl.pallas_call(kernel, out_shape=(jax.ShapeDtypeStruct((rows // LANES, LA...]
  transfers between devices with their start and end apart: 1 -> 1, of which waited for: 0 -> 1; matrix products, arithmetic and copies ran while one was open for 1% -> 3% of each run, Pallas kernels for 0% -> 0%
where the time goes in v1:
time: 97.2 us; the launch traced here: 96.9 us
  blocking collectives  52.5 us (54%)
  waiting for transfers between devices  15.8 us (16%)
  between operations  14.7 us (15%)
  Pallas kernels  7.82 us (8%)
  local copies, waits for them, and re-layouts  3.69 us (4%)
  other arithmetic  2.3 us (2%)
    unnamed x1, blocking collectives  42.1 us
    all_gather x1, waiting for transfers between devices, per_device(): everything = lax.all_gather(data_samples, ALL, axis=0, tiled=True)  15.1 us
    all_to_all x1, blocking collectives, per_device(): parts = lax.all_to_all(col, ALL, 0, 0, tiled=True)  10.4 us
    pallas_call x1, Pallas kernels, per_device(): pl.pallas_call(kernel, out_shape=(jax.ShapeDtypeStruct((rows // LANES, LA...  7.82 us
    unnamed x6, local copies, waits for them, and re-layouts  3.69 us
  transfers between devices with their start and end apart: 1, of which 1 were waited for; matrix products, arithmetic and copies ran while one was open for 3% of the time, Pallas kernels for 0%

profile of v1, /device:TPU:0, one launch (start us, length us, event | category | flops | bytes accessed | tf_op | source)
XLA Modules:
  0.0 96.9 jit_solution(10109158538813835850)
XLA Ops:
  7.2 0.0 all-gather.2.cloned.1.call-start
  7.2 0.7 all-gather.2.cloned.1.call-update
  7.9 1.2 %dynamic-slice = u32[1]{0:T(128)} dynamic-slice(u32[32]{0:T(128)} %constant.19, u32[]{:T(128)S(6)} %add.12), dynamic_slice_sizes={1} | dynamic-slice | bytes 12
  9.8 0.9 multiply_reduce_fusion
  10.7 0.8 multiply_dynamic-update-slice_fusion
  11.5 42.1 %all-reduce = f32[3072]{0:T(1024)S(1)} all-reduce(f32[3072]{0:T(1024)S(1)} %multiply_dynamic-update-slice_fusion), channel_id=1, replica_groups=mesh['gen'=8,'dat'=4] {'dat','gen'}, use_global_device_ids=true, to_apply=%add | all-reduce | flops 3072 | bytes 24576
  53.7 15.1 %all-gather.2.cloned.1.call-done.y_ref = bf16[3072,256]{1,0:T(8,128)(2,1)} async-done(((bf16[96,256]{1,0:T(8,128)(2,1)}), bf16[3072,256]{1,0:T(8,128)(2,1)}) %all-gather.2.cloned.1.call-update) | async-done | bytes 1572880 | tf_op jit(solution)/shard_map/all_gather | solution.py:86
  68.8 0.0 copy-start
  68.8 1.4 %copy-done = bf16[3072,256]{1,0:T(8,128)(2,1)S(1)} copy-done((bf16[3072,256]{1,0:T(8,128)(2,1)S(1)}, bf16[3072,256]{1,0:T(8,128)(2,1)}, u32[]{:S(2)}) %copy-start) | copy-done | bytes 1572888
  70.2 0.0 copy-start.1
  70.2 1.0 %copy-done.1 = bf16[1024,256]{1,0:T(8,128)(2,1)S(1)} copy-done((bf16[1024,256]{1,0:T(8,128)(2,1)S(1)}, bf16[1024,256]{1,0:T(8,128)(2,1)}, u32[]{:S(2)}) %copy-start.1) | copy-done | bytes 524312
  71.2 7.8 %shard_map.50 = (f32[8,128]{1,0:T(8,128)}, f32[32,96]{1,0:T(8,128)S(1)}) custom-call(bf16[1024,256]{1,0:T(8,128)(2,1)S(1)} %copy-done.1, bf16[3072,256]{1,0:T(8,128)(2,1)S(1)} %copy-done, f32[1,3072]{1,0:T(1,128)S(1)} %bitcast.8), custom_call_target="tpu_custom_call" | custom-call | flops 1610612736 | bytes 2097152 | tf_op jit(solution)/shard_map/pallas_call | solution.py:90
  79.0 10.4 %all_to_all.12 = f32[32,1,96]{2,1,0:T(1,128)S(1)} all-to-all(f32[32,1,96]{2,1,0:T(1,128)S(1)} %bitcast.7), channel_id=1, replica_groups=mesh['gen'=8,'dat'=4] {'dat','gen'}, dimensions={0} | all-to-all | bytes 24576 | tf_op jit(solution)/shard_map/all_to_all | solution.py:106
  89.4 0.1 reduce_max.9
  89.5 0.5 subtract_add_fusion
  (2 shorter events, 0.0 us)
Async XLA Ops:
  7.2 61.6 %all-gather.2.cloned.1.call-start = ((), (), s32[]{:S(2)}) async-start(), calls=%async_computation.1 | async-start | bytes 1622016 | tf_op jit(solution)/shard_map/all_gather | solution.py:86
  68.8 1.4 %copy-start = (bf16[3072,256]{1,0:T(8,128)(2,1)S(1)}, bf16[3072,256]{1,0:T(8,128)(2,1)}, u32[]{:S(2)}) copy-start(bf16[3072,256]{1,0:T(8,128)(2,1)} %all-gather.2.cloned.1.call-done.y_ref) | copy-start | bytes 4718596
  70.2 1.0 %copy-start.1 = (bf16[1024,256]{1,0:T(8,128)(2,1)S(1)}, bf16[1024,256]{1,0:T(8,128)(2,1)}, u32[]{:S(2)}) copy-start(bf16[1024,256]{1,0:T(8,128)(2,1)} %x_ref.1) | copy-start | bytes 1572868
Sparse Core Ops, SparseCore 0:
  10.9 57.8 all-gather.1

commit v2 on v1

--- a/solution.py
+++ b/solution.py
@@ -20,9 +20,27 @@
     return [(start, min(step, width - start)) for start in range(0, width, step)]
 
 
-def sinkhorn_kernel(x_ref, y_ref, b_ref, f_ref, col_ref, t_ref, max_ref, sum_ref, *, block, chunk, shares):
+def exchanges(mesh_shape):
+    steps = []
+    for axis in ("gen", "dat"):
+        bit = mesh_shape[axis] // 2
+        while bit:
+            steps.append((axis, bit))
+            bit //= 2
+    return steps
+
+
+def swap(value, axis, bit):
+    size = lax.axis_size(axis)
+    return lax.ppermute(value, axis, [(k, k ^ bit) for k in range(size)])
+
+
+def sinkhorn_kernel(x_ref, y_ref, b_rows_ref, f_ref, col_ref, t_ref, max_ref, sum_ref, b_ref, *, block, chunk, steps):
     rows, width = x_ref.shape
     cols = y_ref.shape[0]
+    shares, share = b_rows_ref.shape
+    for k in range(shares):
+        b_ref[:, k * share : (k + 1) * share] = b_rows_ref[k : k + 1, :]
     alpha = 2.0 * SCALE / width
     max_ref[...] = jnp.full(max_ref.shape, -jnp.inf, jnp.float32)
     sum_ref[...] = jnp.zeros(sum_ref.shape, jnp.float32)
@@ -70,9 +88,16 @@
 
     lax.fori_loop(0, rows // block, step, 0)
     max_ref[...] = max_ref[...] + jnp.log2(sum_ref[...]) - b_ref[...]
-    share = cols // shares
+    gen = lax.axis_index("gen")
+    dat = lax.axis_index("dat")
+    n_gen = lax.axis_size("gen")
     for k in range(shares):
-        col_ref[k : k + 1, :] = max_ref[:, k * share : (k + 1) * share]
+        flips = {"gen": 0, "dat": 0}
+        for place, (axis, bit) in enumerate(steps):
+            if (k >> place) & 1:
+                flips[axis] ^= bit
+        owner = (dat ^ flips["dat"]) * n_gen + (gen ^ flips["gen"])
+        col_ref[pl.ds(owner, 1), :] = max_ref[:, k * share : (k + 1) * share]
 
 
 def per_device(gen_samples, data_samples, data_potential):
@@ -83,10 +108,14 @@
     wide = data_samples.astype(jnp.float32)
     sq_own = jnp.sum(wide * wide, axis=1)
     bias = SCALE * (data_potential - sq_own / width)
-    everything = lax.all_gather(data_samples, ALL, axis=0, tiled=True)
-    biases = lax.all_gather(bias, ALL, axis=0, tiled=True).reshape(1, cols)
+    everything = data_samples
+    biases = bias.reshape(1, share)
+    steps = exchanges({"gen": lax.axis_size("gen"), "dat": lax.axis_size("dat")})
+    for axis, bit in steps:
+        everything = jnp.concatenate([everything, swap(everything, axis, bit)], axis=0)
+        biases = jnp.concatenate([biases, swap(biases, axis, bit)], axis=0)
     block = min(256, rows)
-    kernel = functools.partial(sinkhorn_kernel, block=block, chunk=256, shares=shares)
+    kernel = functools.partial(sinkhorn_kernel, block=block, chunk=256, steps=steps)
     f, col = pl.pallas_call(
         kernel,
         out_shape=(
@@ -95,6 +124,7 @@
         ),
         scratch_shapes=[
             pltpu.VMEM((block, cols), jnp.float32),
+            pltpu.VMEM((1, cols), jnp.float32),
             pltpu.VMEM((1, cols), jnp.float32),
             pltpu.VMEM((1, cols), jnp.float32),
         ],

time: 97.2 us -> 68.1 us (0.70)
  blocking collectives: 52.5 us -> 13 us
  starting transfers between devices: 0.04 us -> 16.7 us
  between operations: 14.7 us -> 0.72 us
  waiting for transfers between devices: 15.8 us -> 21.7 us
    unnamed x1 -> x0, blocking collectives: 42.1 us -> none
    ppermute x0 -> x10, waiting for transfers between devices: none -> 21.7 us  [swap(): return lax.ppermute(value, axis, [(k, k ^ bit) for k in range(size)])]
    ppermute x0 -> x10, starting transfers between devices: none -> 16.7 us  [swap(): return lax.ppermute(value, axis, [(k, k ^ bit) for k in range(size)])]
    all_gather x1 -> x0, waiting for transfers between devices: 15.1 us -> none  [per_device(): everything = lax.all_gather(data_samples, ALL, axis=0, tiled=True)]
    all_to_all x1, blocking collectives: 10.4 us -> 13 us  [per_device(): parts = lax.all_to_all(col, ALL, 0, 0, tiled=True)]
    concatenate x0 -> x6, other arithmetic: none -> 2.47 us  [the longest x3 2.44 us: per_device(): jnp.concatenate([everything, swap(everything, axis, bit)], axis=0)]
    unnamed x6 -> x10, local copies, waits for them, and re-layouts: 3.69 us -> 3.42 us
  transfers between devices with their start and end apart: 1 -> 10, of which waited for: 1 -> 9; matrix products, arithmetic and copies ran while one was open for 3% -> 5% of each run, Pallas kernels for 0% -> 0%
where the time goes in v2:
time: 68.1 us; the launch traced here: 67.7 us
  waiting for transfers between devices  21.7 us (32%)
  starting transfers between devices  16.7 us (25%)
  blocking collectives  13 us (19%)
  Pallas kernels  8.18 us (12%)
  local copies, waits for them, and re-layouts  4.3 us (6%)
  other arithmetic  3.19 us (5%)
  between operations  0.72 us (1%)
    ppermute x10, waiting for transfers between devices, swap(): return lax.ppermute(value, axis, [(k, k ^ bit) for k in range(size)])  21.7 us
    ppermute x10, starting transfers between devices, swap(): return lax.ppermute(value, axis, [(k, k ^ bit) for k in range(size)])  16.7 us
    all_to_all x1, blocking collectives, per_device(): parts = lax.all_to_all(col, ALL, 0, 0, tiled=True)  13 us
    pallas_call x1, Pallas kernels, per_device(): pl.pallas_call(kernel, out_shape=(jax.ShapeDtypeStruct((rows // LANES, LA...  8.18 us
    unnamed x10, local copies, waits for them, and re-layouts  3.42 us
    concatenate x3, other arithmetic, per_device(): jnp.concatenate([everything, swap(everything, axis, bit)], axis=0)  2.44 us
  transfers between devices with their start and end apart: 10, of which 9 were waited for; matrix products, arithmetic and copies ran while one was open for 5% of the time, Pallas kernels for 0%

profile of v2, /device:TPU:0, one launch (start us, length us, event | category | flops | bytes accessed | tf_op | source)
XLA Modules:
  0.0 67.7 jit_solution(16800985000050998567)
XLA Ops:
  0.6 4.1 %collective-permute-start = (bf16[96,256]{1,0:T(8,128)(2,1)}, bf16[96,256]{1,0:T(8,128)(2,1)S(1)}, u32[]{:S(2)}, u32[]{:S(2)}) collective-permute-start(bf16[96,256]{1,0:T(8,128)(2,1)} %param.4), channel_id=1, source_target_pairs={{0,16},{4,20},{8,24},{12,28},{16,0},{20,4},{24,8},{28,12},{1,17},{... | collective-permute-start | bytes 147464 | tf_op jit(solution)/shard_map/ppermute | solution.py:35
  4.7 2.8 %collective-permute-done = bf16[96,256]{1,0:T(8,128)(2,1)S(1)} collective-permute-done((bf16[96,256]{1,0:T(8,128)(2,1)}, bf16[96,256]{1,0:T(8,128)(2,1)S(1)}, u32[]{:S(2)}, u32[]{:S(2)}) %collective-permute-start) | collective-permute-done | bytes 49184 | tf_op jit(solution)/shard_map/ppermute | solution.py:35
  7.5 0.8 %pad_maximum_fusion.2 = bf16[192,256]{1,0:T(8,128)(2,1)S(1)} fusion(bf16[96,256]{1,0:T(8,128)(2,1)S(1)} %collective-permute-done, bf16[96,256]{1,0:T(8,128)(2,1)} %param.4), kind=kLoop, calls=%fused_computation.2 | loop fusion | flops 196608 | bytes 196608 | tf_op jit(solution)/shard_map/concatenate | solution.py:115
  8.3 1.4 %collective-permute-start.1 = (bf16[192,256]{1,0:T(8,128)(2,1)S(1)}, bf16[192,256]{1,0:T(8,128)(2,1)S(1)}, u32[]{:S(2)}, u32[]{:S(2)}) collective-permute-start(bf16[192,256]{1,0:T(8,128)(2,1)S(1)} %pad_maximum_fusion.2), channel_id=1, source_target_pairs={{0,8},{4,12},{8,0},{12,4},{16,24},{20,28},{24,16},{28,20},{1,9},{5... | collective-permute-start | bytes 294920 | tf_op jit(solution)/shard_map/ppermute | solution.py:35
  9.7 3.2 %collective-permute-done.1 = bf16[192,256]{1,0:T(8,128)(2,1)S(1)} collective-permute-done((bf16[192,256]{1,0:T(8,128)(2,1)S(1)}, bf16[192,256]{1,0:T(8,128)(2,1)S(1)}, u32[]{:S(2)}, u32[]{:S(2)}) %collective-permute-start.1) | collective-permute-done | bytes 98336 | tf_op jit(solution)/shard_map/ppermute | solution.py:35
  13.0 0.8 %pad_maximum_fusion.1 = bf16[384,256]{1,0:T(8,128)(2,1)S(1)} fusion(bf16[192,256]{1,0:T(8,128)(2,1)S(1)} %collective-permute-done.1, bf16[96,256]{1,0:T(8,128)(2,1)S(1)} %collective-permute-done, bf16[96,256]{1,0:T(8,128)(2,1)} %param.4), kind=kLoop, calls=%fused_computation.1 | loop fusion | flops 589824 | bytes 393216 | tf_op jit(solution)/shard_map/concatenate | solution.py:115
  13.8 0.0 copy-start.1
  13.8 0.0 copy-start.2
  13.8 1.8 %collective-permute-start.2 = (bf16[384,256]{1,0:T(8,128)(2,1)S(1)}, bf16[384,256]{1,0:T(8,128)(2,1)S(1)}, u32[]{:S(2)}, u32[]{:S(2)}) collective-permute-start(bf16[384,256]{1,0:T(8,128)(2,1)S(1)} %pad_maximum_fusion.1), channel_id=1, source_target_pairs={{0,4},{4,0},{8,12},{12,8},{16,20},{20,16},{24,28},{28,24},{1,5},{5... | collective-permute-start | bytes 589832 | tf_op jit(solution)/shard_map/ppermute | solution.py:35
  15.6 3.9 %collective-permute-done.2 = bf16[384,256]{1,0:T(8,128)(2,1)S(1)} collective-permute-done((bf16[384,256]{1,0:T(8,128)(2,1)S(1)}, bf16[384,256]{1,0:T(8,128)(2,1)S(1)}, u32[]{:S(2)}, u32[]{:S(2)}) %collective-permute-start.2) | collective-permute-done | bytes 196640 | tf_op jit(solution)/shard_map/ppermute | solution.py:35
  19.5 0.8 %pad_maximum_fusion = bf16[768,256]{1,0:T(8,128)(2,1)S(1)} fusion(bf16[384,256]{1,0:T(8,128)(2,1)S(1)} %collective-permute-done.2, bf16[192,256]{1,0:T(8,128)(2,1)S(1)} %collective-permute-done.1, bf16[96,256]{1,0:T(8,128)(2,1)S(1)} %collective-permute-done, bf16[96,256]{1,0:T(8,128)(2,1)} %param.4), kind=kLoop, calls=%fused_computation | loop fusion | flops 1572864 | bytes 786432 | tf_op jit(solution)/shard_map/concatenate | solution.py:115
  20.4 1.8 %collective-permute-start.3 = (bf16[768,256]{1,0:T(8,128)(2,1)S(1)}, bf16[768,256]{1,0:T(8,128)(2,1)S(1)}, u32[]{:S(2)}, u32[]{:S(2)}) collective-permute-start(bf16[768,256]{1,0:T(8,128)(2,1)S(1)} %pad_maximum_fusion), channel_id=1, source_target_pairs={{0,2},{1,3},{2,0},{3,1},{4,6},{5,7},{6,4},{7,5},{8,10},{9,11},{10,... | collective-permute-start | bytes 1179656 | tf_op jit(solution)/shard_map/ppermute | solution.py:35
  22.1 1.4 %constant_dynamic-update-slice_fusion.4 = (bf16[1536,256]{1,0:T(8,128)(2,1)}, bf16[3072,256]{1,0:T(8,128)(2,1)S(1)}) fusion(bf16[96,256]{1,0:T(8,128)(2,1)} %param.4), kind=kLoop, calls=%fused_computation.8 | loop fusion | bytes 147456
  23.5 0.6 constant_dynamic-update-slice_fusion.3
  24.2 0.7 constant_dynamic-update-slice_fusion.2
  24.8 0.7 %constant_dynamic-update-slice_fusion.1 = (bf16[1536,256]{1,0:T(8,128)(2,1)}, bf16[3072,256]{1,0:T(8,128)(2,1)S(1)}) fusion(bf16[1536,256]{1,0:T(8,128)(2,1)} %get-tuple-element.10, bf16[384,256]{1,0:T(8,128)(2,1)S(1)} %collective-permute-done.2, bf16[3072,256]{1,0:T(8,128)(2,1)S(1)} %get-tuple-element.11), kind=kLoop, calls=%fused_computation.5 | loop fusion | bytes 589824
  25.5 0.0 copy-start
  25.5 2.7 %collective-permute-done.3 = bf16[768,256]{1,0:T(8,128)(2,1)S(1)} collective-permute-done((bf16[768,256]{1,0:T(8,128)(2,1)S(1)}, bf16[768,256]{1,0:T(8,128)(2,1)S(1)}, u32[]{:S(2)}, u32[]{:S(2)}) %collective-permute-start.3) | collective-permute-done | bytes 393248 | tf_op jit(solution)/shard_map/ppermute | solution.py:35
  28.2 0.8 %constant_dynamic-update-slice_fusion = (bf16[1536,256]{1,0:T(8,128)(2,1)}, bf16[3072,256]{1,0:T(8,128)(2,1)S(1)}) fusion(bf16[1536,256]{1,0:T(8,128)(2,1)} %get-tuple-element.8, bf16[768,256]{1,0:T(8,128)(2,1)S(1)} %collective-permute-done.3, bf16[3072,256]{1,0:T(8,128)(2,1)S(1)} %get-tuple-element.9), kind=kLoop, calls=%fused_computation.4 | loop fusion | bytes 1179648 | tf_op jit(solution)/shard_map/concatenate | solution.py:115
  29.0 0.0 collective-permute-start.4
  29.0 0.0 copy-done.1
  29.0 0.1 multiply_reduce_fusion
  29.1 0.0 copy-done.2
  29.1 2.5 %collective-permute-start.5 = (f32[1,96]{1,0:T(1,128)S(1)}, f32[1,96]{1,0:T(1,128)S(1)}, u32[]{:S(2)}, u32[]{:S(2)}) collective-permute-start(f32[1,96]{1,0:T(1,128)S(1)} %multiply_bitcast_fusion), channel_id=1, source_target_pairs={{0,16},{4,20},{8,24},{12,28},{16,0},{20,4},{24,8},{28,12},{1,17},{... | collective-permute-start | bytes 1160 | tf_op jit(solution)/shard_map/ppermute | solution.py:35
  31.6 2.0 %collective-permute-done.5 = f32[1,96]{1,0:T(1,128)S(1)} collective-permute-done((f32[1,96]{1,0:T(1,128)S(1)}, f32[1,96]{1,0:T(1,128)S(1)}, u32[]{:S(2)}, u32[]{:S(2)}) %collective-permute-start.5) | collective-permute-done | bytes 416 | tf_op jit(solution)/shard_map/ppermute | solution.py:35
  33.7 1.5 %collective-permute-start.6 = (f32[2,96]{1,0:T(2,128)S(1)}, f32[2,96]{1,0:T(2,128)S(1)}, u32[]{:S(2)}, u32[]{:S(2)}) collective-permute-start(f32[2,96]{1,0:T(2,128)S(1)} %pad_maximum_fusion.5), channel_id=1, source_target_pairs={{0,8},{4,12},{8,0},{12,4},{16,24},{20,28},{24,16},{28,20},{1,9},{5... | collective-permute-start | bytes 2312 | tf_op jit(solution)/shard_map/ppermute | solution.py:35
  35.2 2.1 %collective-permute-done.6 = f32[2,96]{1,0:T(2,128)S(1)} collective-permute-done((f32[2,96]{1,0:T(2,128)S(1)}, f32[2,96]{1,0:T(2,128)S(1)}, u32[]{:S(2)}, u32[]{:S(2)}) %collective-permute-start.6) | collective-permute-done | bytes 800 | tf_op jit(solution)/shard_map/ppermute | solution.py:35
  37.3 1.8 %collective-permute-start.7 = (f32[4,96]{1,0:T(4,128)S(1)}, f32[4,96]{1,0:T(4,128)S(1)}, u32[]{:S(2)}, u32[]{:S(2)}) collective-permute-start(f32[4,96]{1,0:T(4,128)S(1)} %pad_maximum_fusion.4), channel_id=1, source_target_pairs={{0,4},{4,0},{8,12},{12,8},{16,20},{20,16},{24,28},{28,24},{1,5},{5... | collective-permute-start | bytes 4616 | tf_op jit(solution)/shard_map/ppermute | solution.py:35
  39.1 1.9 %collective-permute-done.7 = f32[4,96]{1,0:T(4,128)S(1)} collective-permute-done((f32[4,96]{1,0:T(4,128)S(1)}, f32[4,96]{1,0:T(4,128)S(1)}, u32[]{:S(2)}, u32[]{:S(2)}) %collective-permute-start.7) | collective-permute-done | bytes 1568 | tf_op jit(solution)/shard_map/ppermute | solution.py:35
  41.0 1.8 %collective-permute-start.8 = (f32[8,96]{1,0:T(8,128)S(1)}, f32[8,96]{1,0:T(8,128)S(1)}, u32[]{:S(2)}, u32[]{:S(2)}) collective-permute-start(f32[8,96]{1,0:T(8,128)S(1)} %pad_maximum_fusion.3), channel_id=1, source_target_pairs={{0,2},{1,3},{2,0},{3,1},{4,6},{5,7},{6,4},{7,5},{8,10},{9,11},{10,... | collective-permute-start | bytes 9224 | tf_op jit(solution)/shard_map/ppermute | solution.py:35
  42.7 1.9 %collective-permute-done.8 = f32[8,96]{1,0:T(8,128)S(1)} collective-permute-done((f32[8,96]{1,0:T(8,128)S(1)}, f32[8,96]{1,0:T(8,128)S(1)}, u32[]{:S(2)}, u32[]{:S(2)}) %collective-permute-start.8) | collective-permute-done | bytes 3104 | tf_op jit(solution)/shard_map/ppermute | solution.py:35
  44.6 0.1 collective-permute-start.9
  44.7 1.2 %collective-permute-done.9 = f32[16,96]{1,0:T(8,128)S(1)} collective-permute-done((f32[16,96]{1,0:T(8,128)S(1)}, f32[16,96]{1,0:T(8,128)S(1)}, u32[]{:S(2)}, u32[]{:S(2)}) %collective-permute-start.9) | collective-permute-done | bytes 6176 | tf_op jit(solution)/shard_map/ppermute | solution.py:35
  45.9 0.0 collective-permute-done.4
  45.9 0.1 constant_dynamic-update-slice_fusion.5.y_ref
  46.0 0.0 copy-done
  46.0 8.2 %shard_map.50 = (f32[8,128]{1,0:T(8,128)}, f32[32,96]{1,0:T(8,128)S(1)}) custom-call(bf16[1024,256]{1,0:T(8,128)(2,1)S(1)} %copy-done, bf16[3072,256]{1,0:T(8,128)(2,1)S(1)} %constant_dynamic-update-slice_fusion.5.y_ref, f32[32,96]{1,0:T(8,128)S(1)} %concatenate.47.b_rows_ref), custom_call_target="tpu_custom_call" | custom-call | flops 1610612736 | bytes 2097152 | tf_op jit(solution)/shard_map/pallas_call | solution.py:119
  54.2 13.0 %all_to_all.12 = f32[32,1,96]{2,1,0:T(1,128)S(1)} all-to-all(f32[32,1,96]{2,1,0:T(1,128)S(1)} %bitcast.7), channel_id=1, replica_groups=mesh['gen'=8,'dat'=4] {'dat','gen'}, dimensions={0} | all-to-all | bytes 24576 | tf_op jit(solution)/shard_map/all_to_all | solution.py:136
  67.1 0.1 reduce_max.9
  67.2 0.5 subtract_add_fusion
  (7 shorter events, 0.1 us)
Async XLA Ops:
  0.6 6.9 %collective-permute-start = (bf16[96,256]{1,0:T(8,128)(2,1)}, bf16[96,256]{1,0:T(8,128)(2,1)S(1)}, u32[]{:S(2)}, u32[]{:S(2)}) collective-permute-start(bf16[96,256]{1,0:T(8,128)(2,1)} %param.4), channel_id=1, source_target_pairs={{0,16},{4,20},{8,24},{12,28},{16,0},{20,4},{24,8},{28,12},{1,17},{... | collective-permute-start | bytes 147464 | tf_op jit(solution)/shard_map/ppermute | solution.py:35
  8.3 4.6 %collective-permute-start.1 = (bf16[192,256]{1,0:T(8,128)(2,1)S(1)}, bf16[192,256]{1,0:T(8,128)(2,1)S(1)}, u32[]{:S(2)}, u32[]{:S(2)}) collective-permute-start(bf16[192,256]{1,0:T(8,128)(2,1)S(1)} %pad_maximum_fusion.2), channel_id=1, source_target_pairs={{0,8},{4,12},{8,0},{12,4},{16,24},{20,28},{24,16},{28,20},{1,9},{5... | collective-permute-start | bytes 294920 | tf_op jit(solution)/shard_map/ppermute | solution.py:35
  13.8 15.2 %copy-start.1 = (bf16[96,256]{1,0:T(8,128)(2,1)S(1)}, bf16[96,256]{1,0:T(8,128)(2,1)}, u32[]{:S(2)}) copy-start(bf16[96,256]{1,0:T(8,128)(2,1)} %param.4) | copy-start | bytes 147460
  13.8 15.3 %copy-start.2 = (f32[96]{0:T(128)S(1)}, f32[96]{0:T(128)}, u32[]{:S(2)}) copy-start(f32[96]{0:T(128)} %param.5) | copy-start | bytes 1156
  13.8 5.7 %collective-permute-start.2 = (bf16[384,256]{1,0:T(8,128)(2,1)S(1)}, bf16[384,256]{1,0:T(8,128)(2,1)S(1)}, u32[]{:S(2)}, u32[]{:S(2)}) collective-permute-start(bf16[384,256]{1,0:T(8,128)(2,1)S(1)} %pad_maximum_fusion.1), channel_id=1, source_target_pairs={{0,4},{4,0},{8,12},{12,8},{16,20},{20,16},{24,28},{28,24},{1,5},{5... | collective-permute-start | bytes 589832 | tf_op jit(solution)/shard_map/ppermute | solution.py:35
  20.4 7.8 %collective-permute-start.3 = (bf16[768,256]{1,0:T(8,128)(2,1)S(1)}, bf16[768,256]{1,0:T(8,128)(2,1)S(1)}, u32[]{:S(2)}, u32[]{:S(2)}) collective-permute-start(bf16[768,256]{1,0:T(8,128)(2,1)S(1)} %pad_maximum_fusion), channel_id=1, source_target_pairs={{0,2},{1,3},{2,0},{3,1},{4,6},{5,7},{6,4},{7,5},{8,10},{9,11},{10,... | collective-permute-start | bytes 1179656 | tf_op jit(solution)/shard_map/ppermute | solution.py:35
  25.5 20.4 %copy-start = (bf16[1024,256]{1,0:T(8,128)(2,1)S(1)}, bf16[1024,256]{1,0:T(8,128)(2,1)}, u32[]{:S(2)}) copy-start(bf16[1024,256]{1,0:T(8,128)(2,1)} %x_ref.1) | copy-start | bytes 1572868
  29.0 16.9 %collective-permute-start.4 = (bf16[1536,256]{1,0:T(8,128)(2,1)}, bf16[1536,256]{1,0:T(8,128)(2,1)S(1)}, u32[]{:S(2)}, u32[]{:S(2)}) collective-permute-start(bf16[1536,256]{1,0:T(8,128)(2,1)} %get-tuple-element.6), channel_id=1, source_target_pairs={{0,1},{1,0},{2,3},{3,2},{4,5},{5,4},{6,7},{7,6},{8,9},{9,8},{10,11... | collective-permute-start | bytes 2359304 | tf_op jit(solution)/shard_map/ppermute | solution.py:35
  29.1 4.5 %collective-permute-start.5 = (f32[1,96]{1,0:T(1,128)S(1)}, f32[1,96]{1,0:T(1,128)S(1)}, u32[]{:S(2)}, u32[]{:S(2)}) collective-permute-start(f32[1,96]{1,0:T(1,128)S(1)} %multiply_bitcast_fusion), channel_id=1, source_target_pairs={{0,16},{4,20},{8,24},{12,28},{16,0},{20,4},{24,8},{28,12},{1,17},{... | collective-permute-start | bytes 1160 | tf_op jit(solution)/shard_map/ppermute | solution.py:35
  33.7 3.6 %collective-permute-start.6 = (f32[2,96]{1,0:T(2,128)S(1)}, f32[2,96]{1,0:T(2,128)S(1)}, u32[]{:S(2)}, u32[]{:S(2)}) collective-permute-start(f32[2,96]{1,0:T(2,128)S(1)} %pad_maximum_fusion.5), channel_id=1, source_target_pairs={{0,8},{4,12},{8,0},{12,4},{16,24},{20,28},{24,16},{28,20},{1,9},{5... | collective-permute-start | bytes 2312 | tf_op jit(solution)/shard_map/ppermute | solution.py:35
  37.3 3.7 %collective-permute-start.7 = (f32[4,96]{1,0:T(4,128)S(1)}, f32[4,96]{1,0:T(4,128)S(1)}, u32[]{:S(2)}, u32[]{:S(2)}) collective-permute-start(f32[4,96]{1,0:T(4,128)S(1)} %pad_maximum_fusion.4), channel_id=1, source_target_pairs={{0,4},{4,0},{8,12},{12,8},{16,20},{20,16},{24,28},{28,24},{1,5},{5... | collective-permute-start | bytes 4616 | tf_op jit(solution)/shard_map/ppermute | solution.py:35
  41.0 3.7 %collective-permute-start.8 = (f32[8,96]{1,0:T(8,128)S(1)}, f32[8,96]{1,0:T(8,128)S(1)}, u32[]{:S(2)}, u32[]{:S(2)}) collective-permute-start(f32[8,96]{1,0:T(8,128)S(1)} %pad_maximum_fusion.3), channel_id=1, source_target_pairs={{0,2},{1,3},{2,0},{3,1},{4,6},{5,7},{6,4},{7,5},{8,10},{9,11},{10,... | collective-permute-start | bytes 9224 | tf_op jit(solution)/shard_map/ppermute | solution.py:35
  44.6 1.2 %collective-permute-start.9 = (f32[16,96]{1,0:T(8,128)S(1)}, f32[16,96]{1,0:T(8,128)S(1)}, u32[]{:S(2)}, u32[]{:S(2)}) collective-permute-start(f32[16,96]{1,0:T(8,128)S(1)} %concatenate.46), channel_id=1, source_target_pairs={{0,1},{1,0},{2,3},{3,2},{4,5},{5,4},{6,7},{7,6},{8,9},{9,8},{10,11... | collective-permute-start | bytes 18440 | tf_op jit(solution)/shard_map/ppermute | solution.py:35

commit v3 on v1

--- a/solution.py
+++ b/solution.py
@@ -14,15 +14,81 @@
 SCALE = LOG2E / EPS
 ALL = ("dat", "gen")
 LANES = 128
+TILE = 16
 
 
 def lane_chunks(width, step):
     return [(start, min(step, width - start)) for start in range(0, width, step)]
 
 
-def sinkhorn_kernel(x_ref, y_ref, b_ref, f_ref, col_ref, t_ref, max_ref, sum_ref, *, block, chunk, shares):
+def phases(n_gen, n_dat):
+    far = [(mask, 0) for mask in range(2, n_gen, 2)]
+    plane = [(g, d) for d in range(0, n_dat, 2) for g in range(2)][1:]
+    return far, plane, [(0, 1)]
+
+
+def swap(value, mask):
+    n_gen, n_dat = lax.axis_size("gen"), lax.axis_size("dat")
+    pairs = [
+        (g * n_dat + d, (g ^ mask[0]) * n_dat + (d ^ mask[1])) for g in range(n_gen) for d in range(n_dat)
+    ]
+    return lax.ppermute(value, ("gen", "dat"), pairs)
+
+
+def round_up(value, step):
+    return -(-value // step) * step
+
+
+def pack_kernel(y_ref, g_ref, packed_ref, sq_ref):
+    share, width = y_ref.shape
+    tall = packed_ref.shape[0] - TILE
+    y = y_ref[...]
+    wide = y.astype(jnp.float32)
+    sq = jnp.sum(wide * wide, axis=1, keepdims=True)
+    sq = jnp.broadcast_to(sq, (share, LANES)).T[0:1, :]
+    sq_ref[...] = sq
+    bias = SCALE * (g_ref[...] - sq / width)
+    first = bias.astype(jnp.bfloat16).astype(jnp.float32)
+    rest = bias - first
+    second = rest.astype(jnp.bfloat16).astype(jnp.float32)
+    third = rest - second
+    row = lax.broadcasted_iota(jnp.int32, (TILE, share), 0)
+    pieces = jnp.where(row == 0, first, jnp.where(row == 1, second, jnp.where(row == 2, third, 0.0)))
+    if share < tall:
+        packed_ref[...] = jnp.zeros(packed_ref.shape, jnp.bfloat16)
+    else:
+        packed_ref[tall:, :] = jnp.zeros((TILE, width), jnp.bfloat16)
+    packed_ref[:share, :] = y
+    packed_ref[tall:, :share] = pieces.astype(jnp.bfloat16)
+
+
+def unpack(parts, share, y_ref, b_ref):
+    tall = round_up(share, TILE)
+    span = tall + TILE
+    batch = TILE // math.gcd(share, TILE)
+    held = []
+    k = 0
+    for part in parts:
+        for start in range(0, part.shape[0], span):
+            pieces = part[start + tall : start + span, :share].astype(jnp.float32)
+            b_ref[:, k * share : (k + 1) * share] = pieces[0:1, :] + pieces[1:2, :] + pieces[2:3, :]
+            if batch == 1:
+                y_ref[k * share : (k + 1) * share, :] = part[start : start + share, :]
+            else:
+                held.append(part[start : start + tall, :].astype(jnp.float32)[:share, :])
+                if len(held) == batch:
+                    end = (k + 1) * share
+                    y_ref[end - batch * share : end, :] = jnp.concatenate(held, axis=0).astype(jnp.bfloat16)
+                    held = []
+            k += 1
+
+
+def sinkhorn_kernel(x_ref, *refs, block, chunk, masks):
+    *parts, f_ref, col_ref, y_ref, t_ref, max_ref, sum_ref, b_ref = refs
     rows, width = x_ref.shape
     cols = y_ref.shape[0]
+    share = col_ref.shape[1]
+    unpack(parts, share, y_ref, b_ref)
     alpha = 2.0 * SCALE / width
     max_ref[...] = jnp.full(max_ref.shape, -jnp.inf, jnp.float32)
     sum_ref[...] = jnp.zeros(sum_ref.shape, jnp.float32)
@@ -70,23 +136,38 @@
 
     lax.fori_loop(0, rows // block, step, 0)
     max_ref[...] = max_ref[...] + jnp.log2(sum_ref[...]) - b_ref[...]
-    share = cols // shares
-    for k in range(shares):
-        col_ref[k : k + 1, :] = max_ref[:, k * share : (k + 1) * share]
+    gen = lax.axis_index("gen")
+    dat = lax.axis_index("dat")
+    n_gen = lax.axis_size("gen")
+    for k, mask in enumerate(masks):
+        owner = (dat ^ mask[1]) * n_gen + (gen ^ mask[0])
+        col_ref[pl.ds(owner, 1), :] = max_ref[:, k * share : (k + 1) * share]
 
 
 def per_device(gen_samples, data_samples, data_potential):
     rows, width = gen_samples.shape
-    shares = lax.axis_size("dat") * lax.axis_size("gen")
+    n_gen, n_dat = lax.axis_size("gen"), lax.axis_size("dat")
+    shares = n_gen * n_dat
     share = data_samples.shape[0]
     cols = share * shares
-    wide = data_samples.astype(jnp.float32)
-    sq_own = jnp.sum(wide * wide, axis=1)
-    bias = SCALE * (data_potential - sq_own / width)
-    everything = lax.all_gather(data_samples, ALL, axis=0, tiled=True)
-    biases = lax.all_gather(bias, ALL, axis=0, tiled=True).reshape(1, cols)
+    far, plane, pair = phases(n_gen, n_dat)
+    packed, sq_own = pl.pallas_call(
+        pack_kernel,
+        out_shape=(
+            jax.ShapeDtypeStruct((round_up(share, TILE) + TILE, width), jnp.bfloat16),
+            jax.ShapeDtypeStruct((1, share), jnp.float32),
+        ),
+    )(data_samples, data_potential.reshape(1, share))
+    column = jnp.concatenate([packed] + [swap(packed, m) for m in far], axis=0)
+    half = [column] + [swap(column, m) for m in plane]
+    parts = half + [swap(part, m) for m in pair for part in half]
+    none = [(0, 0)]
+    masks = [
+        (a[0] ^ b[0] ^ c[0], a[1] ^ b[1] ^ c[1]) for c in none + pair for b in none + plane for a in none + far
+    ]
+
     block = min(256, rows)
-    kernel = functools.partial(sinkhorn_kernel, block=block, chunk=256, shares=shares)
+    kernel = functools.partial(sinkhorn_kernel, block=block, chunk=256, masks=masks)
     f, col = pl.pallas_call(
         kernel,
         out_shape=(
@@ -94,7 +175,9 @@
             jax.ShapeDtypeStruct((shares, share), jnp.float32),
         ),
         scratch_shapes=[
+            pltpu.VMEM((cols, width), jnp.bfloat16),
             pltpu.VMEM((block, cols), jnp.float32),
+            pltpu.VMEM((1, cols), jnp.float32),
             pltpu.VMEM((1, cols), jnp.float32),
             pltpu.VMEM((1, cols), jnp.float32),
         ],
@@ -102,11 +185,11 @@
         cost_estimate=pl.CostEstimate(
             flops=2 * rows * cols * width, bytes_accessed=2 * (rows + cols) * width, transcendentals=2 * rows * cols
         ),
-    )(gen_samples, everything, biases)
-    parts = lax.all_to_all(col, ALL, 0, 0, tiled=True)
-    top = jnp.max(parts, axis=0)
-    total = top + jnp.log2(jnp.sum(jnp.exp2(parts - top[None, :]), axis=0))
-    new_data = sq_own / width - (EPS * LN2) * total + EPS * math.log(rows * shares / cols)
+    )(gen_samples, *parts)
+    totals = lax.all_to_all(col, ALL, 0, 0, tiled=True)
+    top = jnp.max(totals, axis=0)
+    total = top + jnp.log2(jnp.sum(jnp.exp2(totals - top[None, :]), axis=0))
+    new_data = sq_own[0] / width - (EPS * LN2) * total + EPS * math.log(rows * shares / cols)
     return f.reshape(rows), new_data
 
 

time: 97.2 us -> 48.4 us (0.50)
  blocking collectives: 52.5 us -> 10.5 us
  between operations: 14.7 us -> 0.66 us
  starting transfers between devices: 0.04 us -> 9.69 us
  Pallas kernels: 7.82 us -> 9.8 us
  other arithmetic: 2.3 us -> 0.6 us
  waiting for transfers between devices: 15.8 us -> 14.3 us
  local copies, waits for them, and re-layouts: 3.69 us -> 2.57 us
    unnamed x1 -> x0, blocking collectives: 42.1 us -> none
    all_gather x1 -> x0, waiting for transfers between devices: 15.1 us -> none  [per_device(): everything = lax.all_gather(data_samples, ALL, axis=0, tiled=True)]
    ppermute x0 -> x10, waiting for transfers between devices: none -> 14.3 us  [swap(): return lax.ppermute(value, ('gen', 'dat'), pairs)]
    ppermute x0 -> x10, starting transfers between devices: none -> 9.69 us  [swap(): return lax.ppermute(value, ('gen', 'dat'), pairs)]
    pallas_call x0 -> x1, Pallas kernels: none -> 1.58 us  [per_device(): pl.pallas_call(pack_kernel, out_shape=(jax.ShapeDtypeStruct((round_up(sha...]
    unnamed x6 -> x7, local copies, waits for them, and re-layouts: 3.69 us -> 2.56 us
  transfers between devices with their start and end apart: 1 -> 10, of which waited for: 1 -> 6; matrix products, arithmetic and copies ran while one was open for 3% -> 2% of each run, Pallas kernels for 0% -> 0%
where the time goes in v3:
time: 48.4 us; the launch traced here: 48.1 us
  waiting for transfers between devices  14.3 us (30%)
  blocking collectives  10.5 us (22%)
  Pallas kernels  9.8 us (20%)
  starting transfers between devices  9.69 us (20%)
  local copies, waits for them, and re-layouts  2.57 us (5%)
  between operations  0.66 us (1%)
  other arithmetic  0.6 us (1%)
    ppermute x10, waiting for transfers between devices, swap(): return lax.ppermute(value, ('gen', 'dat'), pairs)  14.3 us
    all_to_all x1, blocking collectives, per_device(): totals = lax.all_to_all(col, ALL, 0, 0, tiled=True)  10.5 us
    ppermute x10, starting transfers between devices, swap(): return lax.ppermute(value, ('gen', 'dat'), pairs)  9.69 us
    pallas_call x1, Pallas kernels, per_device(): pl.pallas_call(kernel, out_shape=(jax.ShapeDtypeStruct((rows // LANES, LA...  8.22 us
    unnamed x7, local copies, waits for them, and re-layouts  2.56 us
    pallas_call x1, Pallas kernels, per_device(): pl.pallas_call(pack_kernel, out_shape=(jax.ShapeDtypeStruct((round_up(sha...  1.58 us
  transfers between devices with their start and end apart: 10, of which 6 were waited for; matrix products, arithmetic and copies ran while one was open for 2% of the time, Pallas kernels for 0%

profile of v3, /device:TPU:0, one launch (start us, length us, event | category | flops | bytes accessed | tf_op | source)
XLA Modules:
  0.0 48.1 jit_solution(10044777143969709339)
XLA Ops:
  0.6 1.6 %shard_map.50 = (bf16[112,256]{1,0:T(8,128)(2,1)}, f32[1,96]{1,0:T(1,128)}) custom-call(bf16[96,256]{1,0:T(8,128)(2,1)} %y_ref.1, f32[1,96]{1,0:T(1,128)} %bitcast.12), custom_call_target="tpu_custom_call" | custom-call | tf_op jit(solution)/shard_map/pallas_call | solution.py:154
  2.2 5.0 %collective-permute-start.2 = (bf16[112,256]{1,0:T(8,128)(2,1)}, bf16[112,256]{1,0:T(8,128)(2,1)S(1)}, u32[]{:S(2)}, u32[]{:S(2)}) collective-permute-start(bf16[112,256]{1,0:T(8,128)(2,1)} %get-tuple-element.6), channel_id=1, source_target_pairs={{0,24},{1,25},{2,26},{3,27},{4,28},{5,29},{6,30},{7,31},{8,16},{9,... | collective-permute-start | bytes 172040 | tf_op jit(solution)/shard_map/ppermute | solution.py:35
  7.3 0.0 collective-permute-start.1
  7.3 0.6 %collective-permute-start = (bf16[112,256]{1,0:T(8,128)(2,1)}, bf16[112,256]{1,0:T(8,128)(2,1)S(1)}, u32[]{:S(2)}, u32[]{:S(2)}) collective-permute-start(bf16[112,256]{1,0:T(8,128)(2,1)} %get-tuple-element.6), channel_id=1, source_target_pairs={{0,8},{1,9},{2,10},{3,11},{4,12},{5,13},{6,14},{7,15},{8,0},{9,1},... | collective-permute-start | bytes 172040 | tf_op jit(solution)/shard_map/ppermute | solution.py:35
  7.8 0.9 %constant_dynamic-update-slice_fusion.3 = bf16[448,256]{1,0:T(8,128)(2,1)S(1)} fusion(bf16[112,256]{1,0:T(8,128)(2,1)} %get-tuple-element.6), kind=kLoop, calls=%fused_computation.4 | loop fusion | bytes 114688
  8.7 3.0 %collective-permute-done = bf16[112,256]{1,0:T(8,128)(2,1)S(1)} collective-permute-done((bf16[112,256]{1,0:T(8,128)(2,1)}, bf16[112,256]{1,0:T(8,128)(2,1)S(1)}, u32[]{:S(2)}, u32[]{:S(2)}) %collective-permute-start) | collective-permute-done | bytes 57376 | tf_op jit(solution)/shard_map/ppermute | solution.py:35
  11.7 0.9 %collective-permute-done.1 = bf16[112,256]{1,0:T(8,128)(2,1)S(1)} collective-permute-done((bf16[112,256]{1,0:T(8,128)(2,1)}, bf16[112,256]{1,0:T(8,128)(2,1)S(1)}, u32[]{:S(2)}, u32[]{:S(2)}) %collective-permute-start.1) | collective-permute-done | bytes 57376 | tf_op jit(solution)/shard_map/ppermute | solution.py:35
  12.5 0.0 collective-permute-done.2
  12.6 2.5 %collective-permute-start.5 = (bf16[448,256]{1,0:T(8,128)(2,1)S(1)}, bf16[448,256]{1,0:T(8,128)(2,1)S(1)}, u32[]{:S(2)}, u32[]{:S(2)}) collective-permute-start(bf16[448,256]{1,0:T(8,128)(2,1)S(1)} %constant_dynamic-update-slice_fusion.refs_0_), channel_id=1, source_target_pairs={{0,6},{1,7},{2,4},{3,5},{4,2},{5,3},{6,0},{7,1},{8,14},{9,15},{10,... | collective-permute-start | bytes 688136 | tf_op jit(solution)/shard_map/ppermute | solution.py:35
  15.1 0.5 %collective-permute-start.4 = (bf16[448,256]{1,0:T(8,128)(2,1)S(1)}, bf16[448,256]{1,0:T(8,128)(2,1)S(1)}, u32[]{:S(2)}, u32[]{:S(2)}) collective-permute-start(bf16[448,256]{1,0:T(8,128)(2,1)S(1)} %constant_dynamic-update-slice_fusion.refs_0_), channel_id=1, source_target_pairs={{0,2},{1,3},{2,0},{3,1},{4,6},{5,7},{6,4},{7,5},{8,10},{9,11},{10,... | collective-permute-start | bytes 688136 | tf_op jit(solution)/shard_map/ppermute | solution.py:35
  15.6 0.5 collective-permute-start.3
  16.1 0.0 collective-permute-start.6
  16.1 5.9 %collective-permute-done.5.refs_3_ = bf16[448,256]{1,0:T(8,128)(2,1)S(1)} collective-permute-done((bf16[448,256]{1,0:T(8,128)(2,1)S(1)}, bf16[448,256]{1,0:T(8,128)(2,1)S(1)}, u32[]{:S(2)}, u32[]{:S(2)}) %collective-permute-start.5) | collective-permute-done | bytes 229408 | tf_op jit(solution)/shard_map/ppermute | solution.py:35
  22.1 0.0 collective-permute-start.9
  22.1 3.2 %collective-permute-done.4.refs_2_ = bf16[448,256]{1,0:T(8,128)(2,1)S(1)} collective-permute-done((bf16[448,256]{1,0:T(8,128)(2,1)S(1)}, bf16[448,256]{1,0:T(8,128)(2,1)S(1)}, u32[]{:S(2)}, u32[]{:S(2)}) %collective-permute-start.4) | collective-permute-done | bytes 229408 | tf_op jit(solution)/shard_map/ppermute | solution.py:35
  25.3 0.0 collective-permute-start.8
  25.3 0.0 collective-permute-done.3.refs_1_
  25.3 0.5 %collective-permute-start.7 = (bf16[448,256]{1,0:T(8,128)(2,1)S(1)}, bf16[448,256]{1,0:T(8,128)(2,1)S(1)}, u32[]{:S(2)}, u32[]{:S(2)}) collective-permute-start(bf16[448,256]{1,0:T(8,128)(2,1)S(1)} %collective-permute-done.3.refs_1_), channel_id=1, source_target_pairs={{0,1},{1,0},{2,3},{3,2},{4,5},{5,4},{6,7},{7,6},{8,9},{9,8},{10,11... | collective-permute-start | bytes 688136 | tf_op jit(solution)/shard_map/ppermute | solution.py:35
  25.8 0.0 collective-permute-done.6.refs_4_
  25.8 0.0 collective-permute-done.9.refs_7_
  25.8 1.0 %collective-permute-done.8.refs_6_ = bf16[448,256]{1,0:T(8,128)(2,1)S(1)} collective-permute-done((bf16[448,256]{1,0:T(8,128)(2,1)S(1)}, bf16[448,256]{1,0:T(8,128)(2,1)S(1)}, u32[]{:S(2)}, u32[]{:S(2)}) %collective-permute-start.8) | collective-permute-done | bytes 229408 | tf_op jit(solution)/shard_map/ppermute | solution.py:35
  26.8 0.3 collective-permute-done.7.refs_5_
  27.1 0.0 copy-start
  27.1 1.0 %copy-done = bf16[1024,256]{1,0:T(8,128)(2,1)S(1)} copy-done((bf16[1024,256]{1,0:T(8,128)(2,1)S(1)}, bf16[1024,256]{1,0:T(8,128)(2,1)}, u32[]{:S(2)}) %copy-start) | copy-done | bytes 524312
  28.1 8.2 %shard_map.51 = (f32[8,128]{1,0:T(8,128)}, f32[32,96]{1,0:T(8,128)S(1)}) custom-call(bf16[1024,256]{1,0:T(8,128)(2,1)S(1)} %copy-done, bf16[448,256]{1,0:T(8,128)(2,1)S(1)} %constant_dynamic-update-slice_fusion.refs_0_, bf16[448,256]{1,0:T(8,128)(2,1)S(1)} %collective-permute-done.3.refs_1_, bf16[448,256]{1,0:T(8,128)(2,1)S(1)} %collective-permute-done.4.refs_2_, ...), custom_call_target="tpu_custom_call" | custom-call | flops 1610612736 | bytes 2097152 | tf_op jit(solution)/shard_map/pallas_call | solution.py:171
  36.4 10.5 %all_to_all.12 = f32[32,1,96]{2,1,0:T(1,128)S(1)} all-to-all(f32[32,1,96]{2,1,0:T(1,128)S(1)} %bitcast.10), channel_id=1, replica_groups=mesh['gen'=8,'dat'=4] {'dat','gen'}, dimensions={0} | all-to-all | bytes 24576 | tf_op jit(solution)/shard_map/all_to_all | solution.py:189
  46.9 0.1 reduce_max.9
  47.0 0.0 copy-start.1
  47.0 0.7 %copy-done.1 = f32[1,96]{1,0:T(1,128)S(1)} copy-done((f32[1,96]{1,0:T(1,128)S(1)}, f32[1,96]{1,0:T(1,128)}, u32[]{:S(2)}) %copy-start.1) | copy-done | bytes 408
  47.6 0.5 %fusion = f32[96]{0:T(128)} fusion(f32[96]{0:T(128)S(1)} %reduce_max.9, f32[96]{0:T(128)S(1)} %exponential_reduce_fusion, f32[1,96]{1,0:T(1,128)S(1)} %copy-done.1), kind=kLoop, calls=%fused_computation.6 | loop fusion | flops 576 | bytes 1536 | tf_op jit(solution)/shard_map/add | solution.py:192
  (4 shorter events, 0.0 us)
Async XLA Ops:
  2.2 10.3 %collective-permute-start.2 = (bf16[112,256]{1,0:T(8,128)(2,1)}, bf16[112,256]{1,0:T(8,128)(2,1)S(1)}, u32[]{:S(2)}, u32[]{:S(2)}) collective-permute-start(bf16[112,256]{1,0:T(8,128)(2,1)} %get-tuple-element.6), channel_id=1, source_target_pairs={{0,24},{1,25},{2,26},{3,27},{4,28},{5,29},{6,30},{7,31},{8,16},{9,... | collective-permute-start | bytes 172040 | tf_op jit(solution)/shard_map/ppermute | solution.py:35
  7.3 5.3 %collective-permute-start.1 = (bf16[112,256]{1,0:T(8,128)(2,1)}, bf16[112,256]{1,0:T(8,128)(2,1)S(1)}, u32[]{:S(2)}, u32[]{:S(2)}) collective-permute-start(bf16[112,256]{1,0:T(8,128)(2,1)} %get-tuple-element.6), channel_id=1, source_target_pairs={{0,16},{1,17},{2,18},{3,19},{4,20},{5,21},{6,22},{7,23},{8,24},{9,... | collective-permute-start | bytes 172040 | tf_op jit(solution)/shard_map/ppermute | solution.py:35
  7.3 4.4 %collective-permute-start = (bf16[112,256]{1,0:T(8,128)(2,1)}, bf16[112,256]{1,0:T(8,128)(2,1)S(1)}, u32[]{:S(2)}, u32[]{:S(2)}) collective-permute-start(bf16[112,256]{1,0:T(8,128)(2,1)} %get-tuple-element.6), channel_id=1, source_target_pairs={{0,8},{1,9},{2,10},{3,11},{4,12},{5,13},{6,14},{7,15},{8,0},{9,1},... | collective-permute-start | bytes 172040 | tf_op jit(solution)/shard_map/ppermute | solution.py:35
  12.6 9.5 %collective-permute-start.5 = (bf16[448,256]{1,0:T(8,128)(2,1)S(1)}, bf16[448,256]{1,0:T(8,128)(2,1)S(1)}, u32[]{:S(2)}, u32[]{:S(2)}) collective-permute-start(bf16[448,256]{1,0:T(8,128)(2,1)S(1)} %constant_dynamic-update-slice_fusion.refs_0_), channel_id=1, source_target_pairs={{0,6},{1,7},{2,4},{3,5},{4,2},{5,3},{6,0},{7,1},{8,14},{9,15},{10,... | collective-permute-start | bytes 688136 | tf_op jit(solution)/shard_map/ppermute | solution.py:35
  15.1 10.2 %collective-permute-start.4 = (bf16[448,256]{1,0:T(8,128)(2,1)S(1)}, bf16[448,256]{1,0:T(8,128)(2,1)S(1)}, u32[]{:S(2)}, u32[]{:S(2)}) collective-permute-start(bf16[448,256]{1,0:T(8,128)(2,1)S(1)} %constant_dynamic-update-slice_fusion.refs_0_), channel_id=1, source_target_pairs={{0,2},{1,3},{2,0},{3,1},{4,6},{5,7},{6,4},{7,5},{8,10},{9,11},{10,... | collective-permute-start | bytes 688136 | tf_op jit(solution)/shard_map/ppermute | solution.py:35
  15.6 9.6 %collective-permute-start.3 = (bf16[448,256]{1,0:T(8,128)(2,1)S(1)}, bf16[448,256]{1,0:T(8,128)(2,1)S(1)}, u32[]{:S(2)}, u32[]{:S(2)}) collective-permute-start(bf16[448,256]{1,0:T(8,128)(2,1)S(1)} %constant_dynamic-update-slice_fusion.refs_0_), channel_id=1, source_target_pairs={{0,4},{1,5},{2,6},{3,7},{4,0},{5,1},{6,2},{7,3},{8,12},{9,13},{10,... | collective-permute-start | bytes 688136 | tf_op jit(solution)/shard_map/ppermute | solution.py:35
  16.1 9.7 %collective-permute-start.6 = (bf16[448,256]{1,0:T(8,128)(2,1)S(1)}, bf16[448,256]{1,0:T(8,128)(2,1)S(1)}, u32[]{:S(2)}, u32[]{:S(2)}) collective-permute-start(bf16[448,256]{1,0:T(8,128)(2,1)S(1)} %constant_dynamic-update-slice_fusion.refs_0_), channel_id=1, source_target_pairs={{0,1},{1,0},{2,3},{3,2},{4,5},{5,4},{6,7},{7,6},{8,9},{9,8},{10,11... | collective-permute-start | bytes 688136 | tf_op jit(solution)/shard_map/ppermute | solution.py:35
  22.1 3.7 %collective-permute-start.9 = (bf16[448,256]{1,0:T(8,128)(2,1)S(1)}, bf16[448,256]{1,0:T(8,128)(2,1)S(1)}, u32[]{:S(2)}, u32[]{:S(2)}) collective-permute-start(bf16[448,256]{1,0:T(8,128)(2,1)S(1)} %collective-permute-done.5.refs_3_), channel_id=1, source_target_pairs={{0,1},{1,0},{2,3},{3,2},{4,5},{5,4},{6,7},{7,6},{8,9},{9,8},{10,11... | collective-permute-start | bytes 688136 | tf_op jit(solution)/shard_map/ppermute | solution.py:35
  25.3 1.5 %collective-permute-start.8 = (bf16[448,256]{1,0:T(8,128)(2,1)S(1)}, bf16[448,256]{1,0:T(8,128)(2,1)S(1)}, u32[]{:S(2)}, u32[]{:S(2)}) collective-permute-start(bf16[448,256]{1,0:T(8,128)(2,1)S(1)} %collective-permute-done.4.refs_2_), channel_id=1, source_target_pairs={{0,1},{1,0},{2,3},{3,2},{4,5},{5,4},{6,7},{7,6},{8,9},{9,8},{10,11... | collective-permute-start | bytes 688136 | tf_op jit(solution)/shard_map/ppermute | solution.py:35
  25.3 1.8 %collective-permute-start.7 = (bf16[448,256]{1,0:T(8,128)(2,1)S(1)}, bf16[448,256]{1,0:T(8,128)(2,1)S(1)}, u32[]{:S(2)}, u32[]{:S(2)}) collective-permute-start(bf16[448,256]{1,0:T(8,128)(2,1)S(1)} %collective-permute-done.3.refs_1_), channel_id=1, source_target_pairs={{0,1},{1,0},{2,3},{3,2},{4,5},{5,4},{6,7},{7,6},{8,9},{9,8},{10,11... | collective-permute-start | bytes 688136 | tf_op jit(solution)/shard_map/ppermute | solution.py:35
  27.1 1.0 %copy-start = (bf16[1024,256]{1,0:T(8,128)(2,1)S(1)}, bf16[1024,256]{1,0:T(8,128)(2,1)}, u32[]{:S(2)}) copy-start(bf16[1024,256]{1,0:T(8,128)(2,1)} %x_ref.1) | copy-start | bytes 1572868
  47.0 0.7 %copy-start.1 = (f32[1,96]{1,0:T(1,128)S(1)}, f32[1,96]{1,0:T(1,128)}, u32[]{:S(2)}) copy-start(f32[1,96]{1,0:T(1,128)} %get-tuple-element.8) | copy-start | bytes 1156

commit v4 on v3

--- a/solution.py
+++ b/solution.py
@@ -21,10 +21,10 @@
     return [(start, min(step, width - start)) for start in range(0, width, step)]
 
 
-def phases(n_gen, n_dat):
-    far = [(mask, 0) for mask in range(2, n_gen, 2)]
-    plane = [(g, d) for d in range(0, n_dat, 2) for g in range(2)][1:]
-    return far, plane, [(0, 1)]
+def partners(n_gen, n_dat):
+    far = [(g, 0) for g in range(2, n_gen, 2)]
+    plane = [(g, d) for g in range(2) for d in range(0, n_dat, 2)][1:]
+    return far, plane, (0, 1)
 
 
 def swap(value, mask):
@@ -35,18 +35,48 @@
     return lax.ppermute(value, ("gen", "dat"), pairs)
 
 
+def join(blocks):
+    if len(blocks) == 1:
+        return blocks[0]
+    return jnp.concatenate([array for array, _ in blocks], axis=0), [m for _, masks in blocks for m in masks]
+
+
+def sent(block, mask):
+    array, masks = block
+    return swap(array, mask), [(g ^ mask[0], d ^ mask[1]) for g, d in masks]
+
+
+def gather(own, n_gen, n_dat):
+    far, plane, pair = partners(n_gen, n_dat)
+    own = (own, [(0, 0)])
+    along = [sent(own, m) for m in far]
+    across = [sent(own, m) for m in plane]
+    straight = [m for m in plane if 0 in m]
+    bent = [block for block, m in zip(across, plane) if 0 not in m]
+    blocks = [own] + along + across
+    twins = [sent(own, pair)]
+    second = []
+    column = join(along)
+    second += [sent(column, m) for m in straight]
+    if bent:
+        corner = join(bent)
+        second += [sent(corner, m) for m in far]
+    twins += [sent(join(along + across), pair)]
+    twins += [sent(block, pair) for block in second]
+    return blocks + second + twins
+
+
 def round_up(value, step):
     return -(-value // step) * step
 
 
-def pack_kernel(y_ref, g_ref, packed_ref, sq_ref):
+def pack_kernel(y_ref, g_ref, packed_ref):
     share, width = y_ref.shape
     tall = packed_ref.shape[0] - TILE
     y = y_ref[...]
     wide = y.astype(jnp.float32)
     sq = jnp.sum(wide * wide, axis=1, keepdims=True)
     sq = jnp.broadcast_to(sq, (share, LANES)).T[0:1, :]
-    sq_ref[...] = sq
     bias = SCALE * (g_ref[...] - sq / width)
     first = bias.astype(jnp.bfloat16).astype(jnp.float32)
     rest = bias - first
@@ -135,7 +165,7 @@
         return carry
 
     lax.fori_loop(0, rows // block, step, 0)
-    max_ref[...] = max_ref[...] + jnp.log2(sum_ref[...]) - b_ref[...]
+    max_ref[...] = max_ref[...] + jnp.log2(sum_ref[...])
     gen = lax.axis_index("gen")
     dat = lax.axis_index("dat")
     n_gen = lax.axis_size("gen")
@@ -150,21 +180,12 @@
     shares = n_gen * n_dat
     share = data_samples.shape[0]
     cols = share * shares
-    far, plane, pair = phases(n_gen, n_dat)
-    packed, sq_own = pl.pallas_call(
+    packed = pl.pallas_call(
         pack_kernel,
-        out_shape=(
-            jax.ShapeDtypeStruct((round_up(share, TILE) + TILE, width), jnp.bfloat16),
-            jax.ShapeDtypeStruct((1, share), jnp.float32),
-        ),
+        out_shape=jax.ShapeDtypeStruct((round_up(share, TILE) + TILE, width), jnp.bfloat16),
     )(data_samples, data_potential.reshape(1, share))
-    column = jnp.concatenate([packed] + [swap(packed, m) for m in far], axis=0)
-    half = [column] + [swap(column, m) for m in plane]
-    parts = half + [swap(part, m) for m in pair for part in half]
-    none = [(0, 0)]
-    masks = [
-        (a[0] ^ b[0] ^ c[0], a[1] ^ b[1] ^ c[1]) for c in none + pair for b in none + plane for a in none + far
-    ]
+    blocks = gather(packed, n_gen, n_dat)
+    masks = [m for _, owners in blocks for m in owners]
 
     block = min(256, rows)
     kernel = functools.partial(sinkhorn_kernel, block=block, chunk=256, masks=masks)
@@ -185,11 +206,11 @@
         cost_estimate=pl.CostEstimate(
             flops=2 * rows * cols * width, bytes_accessed=2 * (rows + cols) * width, transcendentals=2 * rows * cols
         ),
-    )(gen_samples, *parts)
+    )(gen_samples, *[array for array, _ in blocks])
     totals = lax.all_to_all(col, ALL, 0, 0, tiled=True)
     top = jnp.max(totals, axis=0)
     total = top + jnp.log2(jnp.sum(jnp.exp2(totals - top[None, :]), axis=0))
-    new_data = sq_own[0] / width - (EPS * LN2) * total + EPS * math.log(rows * shares / cols)
+    new_data = data_potential - (EPS * LN2) * total + EPS * math.log(rows * shares / cols)
     return f.reshape(rows), new_data
 
 

time: 48.4 us -> 51.8 us (1.070)
  starting transfers between devices: 9.69 us -> 18.9 us
  waiting for transfers between devices: 14.3 us -> 9.96 us
  local copies, waits for them, and re-layouts: 2.57 us -> 0.68 us
    ppermute x10 -> x18, starting transfers between devices: 9.69 us -> 18.9 us  [swap(): return lax.ppermute(value, ('gen', 'dat'), pairs)]
    ppermute x10 -> x18, waiting for transfers between devices: 14.3 us -> 9.96 us  [swap(): return lax.ppermute(value, ('gen', 'dat'), pairs)]
    unnamed x7 -> x11, local copies, waits for them, and re-layouts: 2.56 us -> 0.67 us
  transfers between devices with their start and end apart: 10 -> 18, of which waited for: 6 -> 8; matrix products, arithmetic and copies ran while one was open for 2% -> 0% of each run, Pallas kernels for 0% -> 0%
where the time goes in v4:
time: 51.8 us; the launch traced here: 51.7 us
  starting transfers between devices  18.9 us (36%)
  blocking collectives  10.9 us (21%)
  waiting for transfers between devices  9.96 us (19%)
  Pallas kernels  9.9 us (19%)
  between operations  0.71 us (1%)
  local copies, waits for them, and re-layouts  0.68 us (1%)
  other arithmetic  0.6 us (1%)
    ppermute x18, starting transfers between devices, swap(): return lax.ppermute(value, ('gen', 'dat'), pairs)  18.9 us
    all_to_all x1, blocking collectives, per_device(): totals = lax.all_to_all(col, ALL, 0, 0, tiled=True)  10.9 us
    ppermute x18, waiting for transfers between devices, swap(): return lax.ppermute(value, ('gen', 'dat'), pairs)  9.96 us
    pallas_call x1, Pallas kernels, per_device(): pl.pallas_call(kernel, out_shape=(jax.ShapeDtypeStruct((rows // LANES, LA...  8.25 us
    pallas_call x1, Pallas kernels, per_device(): pl.pallas_call(pack_kernel, out_shape=jax.ShapeDtypeStruct((round_up(shar...  1.65 us
  transfers between devices with their start and end apart: 18, of which 8 were waited for; matrix products, arithmetic and copies ran while one was open for 0% of the time, Pallas kernels for 0%

profile of v4, /device:TPU:0, one launch (start us, length us, event | category | flops | bytes accessed | tf_op | source)
XLA Modules:
  0.0 51.7 jit_solution(7756047699665892257)
XLA Ops:
  0.6 0.0 copy-start.1
  0.6 1.6 %shard_map.50.refs_0_ = bf16[112,256]{1,0:T(8,128)(2,1)} custom-call(bf16[96,256]{1,0:T(8,128)(2,1)} %y_ref.1, f32[1,96]{1,0:T(1,128)} %bitcast.8), custom_call_target="tpu_custom_call" | custom-call | tf_op jit(solution)/shard_map/pallas_call | solution.py:183
  2.3 3.0 %collective-permute-start = (bf16[112,256]{1,0:T(8,128)(2,1)}, bf16[112,256]{1,0:T(8,128)(2,1)S(1)}, u32[]{:S(2)}, u32[]{:S(2)}) collective-permute-start(bf16[112,256]{1,0:T(8,128)(2,1)} %shard_map.50.refs_0_), channel_id=1, source_target_pairs={{0,8},{1,9},{2,10},{3,11},{4,12},{5,13},{6,14},{7,15},{8,0},{9,1},... | collective-permute-start | bytes 172040 | tf_op jit(solution)/shard_map/ppermute | solution.py:35
  5.3 2.6 %collective-permute-start.1 = (bf16[112,256]{1,0:T(8,128)(2,1)}, bf16[112,256]{1,0:T(8,128)(2,1)S(1)}, u32[]{:S(2)}, u32[]{:S(2)}) collective-permute-start(bf16[112,256]{1,0:T(8,128)(2,1)} %shard_map.50.refs_0_), channel_id=1, source_target_pairs={{0,16},{1,17},{2,18},{3,19},{4,20},{5,21},{6,22},{7,23},{8,24},{9,... | collective-permute-start | bytes 172040 | tf_op jit(solution)/shard_map/ppermute | solution.py:35
  7.9 0.0 collective-permute-start.2
  7.9 1.7 %collective-permute-start.3 = (bf16[112,256]{1,0:T(8,128)(2,1)}, bf16[112,256]{1,0:T(8,128)(2,1)S(1)}, u32[]{:S(2)}, u32[]{:S(2)}) collective-permute-start(bf16[112,256]{1,0:T(8,128)(2,1)} %shard_map.50.refs_0_), channel_id=1, source_target_pairs={{0,2},{1,3},{2,0},{3,1},{4,6},{5,7},{6,4},{7,5},{8,10},{9,11},{10,... | collective-permute-start | bytes 172040 | tf_op jit(solution)/shard_map/ppermute | solution.py:35
  9.6 1.5 %collective-permute-start.4 = (bf16[112,256]{1,0:T(8,128)(2,1)}, bf16[112,256]{1,0:T(8,128)(2,1)S(1)}, u32[]{:S(2)}, u32[]{:S(2)}) collective-permute-start(bf16[112,256]{1,0:T(8,128)(2,1)} %shard_map.50.refs_0_), channel_id=1, source_target_pairs={{0,4},{1,5},{2,6},{3,7},{4,0},{5,1},{6,2},{7,3},{8,12},{9,13},{10,... | collective-permute-start | bytes 172040 | tf_op jit(solution)/shard_map/ppermute | solution.py:35
  11.1 0.0 collective-permute-done.refs_1_
  11.1 0.3 collective-permute-start.5
  11.4 0.3 collective-permute-done.1.refs_2_
  11.7 2.4 %collective-permute-done.2.refs_3_ = bf16[112,256]{1,0:T(8,128)(2,1)S(1)} collective-permute-done((bf16[112,256]{1,0:T(8,128)(2,1)}, bf16[112,256]{1,0:T(8,128)(2,1)S(1)}, u32[]{:S(2)}, u32[]{:S(2)}) %collective-permute-start.2) | collective-permute-done | bytes 57376 | tf_op jit(solution)/shard_map/ppermute | solution.py:35
  14.1 1.6 %collective-permute-start.6 = (bf16[336,256]{1,0:T(8,128)(2,1)S(1)}, bf16[336,256]{1,0:T(8,128)(2,1)S(1)}, u32[]{:S(2)}, u32[]{:S(2)}) collective-permute-start(bf16[336,256]{1,0:T(8,128)(2,1)S(1)} %get-tuple-element.7), channel_id=1, source_target_pairs={{0,2},{1,3},{2,0},{3,1},{4,6},{5,7},{6,4},{7,5},{8,10},{9,11},{10,... | collective-permute-start | bytes 516104 | tf_op jit(solution)/shard_map/ppermute | solution.py:35
  15.7 0.0 collective-permute-done.3.refs_4_
  15.7 0.0 collective-permute-done.4.refs_5_
  15.7 0.0 copy-start
  15.7 1.2 %collective-permute-done.5.refs_6_ = bf16[112,256]{1,0:T(8,128)(2,1)S(1)} collective-permute-done((bf16[112,256]{1,0:T(8,128)(2,1)}, bf16[112,256]{1,0:T(8,128)(2,1)S(1)}, u32[]{:S(2)}, u32[]{:S(2)}) %collective-permute-start.5) | collective-permute-done | bytes 57376 | tf_op jit(solution)/shard_map/ppermute | solution.py:35
  16.9 0.0 collective-permute-start.12
  16.9 0.6 %collective-permute-start.7 = (bf16[336,256]{1,0:T(8,128)(2,1)S(1)}, bf16[336,256]{1,0:T(8,128)(2,1)S(1)}, u32[]{:S(2)}, u32[]{:S(2)}) collective-permute-start(bf16[336,256]{1,0:T(8,128)(2,1)S(1)} %get-tuple-element.7), channel_id=1, source_target_pairs={{0,4},{1,5},{2,6},{3,7},{4,0},{5,1},{6,2},{7,3},{8,12},{9,13},{10,... | collective-permute-start | bytes 516104 | tf_op jit(solution)/shard_map/ppermute | solution.py:35
  17.5 0.0 copy-done
  17.5 0.2 collective-permute-start.11
  17.6 0.8 %collective-permute-start.8 = (bf16[112,256]{1,0:T(8,128)(2,1)S(1)}, bf16[112,256]{1,0:T(8,128)(2,1)S(1)}, u32[]{:S(2)}, u32[]{:S(2)}) collective-permute-start(bf16[112,256]{1,0:T(8,128)(2,1)S(1)} %collective-permute-done.5.refs_6_), channel_id=1, source_target_pairs={{0,8},{1,9},{2,10},{3,11},{4,12},{5,13},{6,14},{7,15},{8,0},{9,1},... | collective-permute-start | bytes 172040 | tf_op jit(solution)/shard_map/ppermute | solution.py:35
  18.4 0.3 collective-permute-done.11.refs_12_
  18.7 2.7 %collective-permute-start.9 = (bf16[112,256]{1,0:T(8,128)(2,1)S(1)}, bf16[112,256]{1,0:T(8,128)(2,1)S(1)}, u32[]{:S(2)}, u32[]{:S(2)}) collective-permute-start(bf16[112,256]{1,0:T(8,128)(2,1)S(1)} %collective-permute-done.5.refs_6_), channel_id=1, source_target_pairs={{0,16},{1,17},{2,18},{3,19},{4,20},{5,21},{6,22},{7,23},{8,24},{9,... | collective-permute-start | bytes 172040 | tf_op jit(solution)/shard_map/ppermute | solution.py:35
  21.5 0.0 collective-permute-done.6.refs_7_
  21.5 0.0 collective-permute-start.13
  21.5 2.2 %collective-permute-done.7.refs_8_ = bf16[336,256]{1,0:T(8,128)(2,1)S(1)} collective-permute-done((bf16[336,256]{1,0:T(8,128)(2,1)S(1)}, bf16[336,256]{1,0:T(8,128)(2,1)S(1)}, u32[]{:S(2)}, u32[]{:S(2)}) %collective-permute-start.7) | collective-permute-done | bytes 172064 | tf_op jit(solution)/shard_map/ppermute | solution.py:35
  23.7 0.0 collective-permute-start.14
  23.7 0.0 collective-permute-done.8.refs_9_
  23.7 3.2 %collective-permute-start.10 = (bf16[112,256]{1,0:T(8,128)(2,1)S(1)}, bf16[112,256]{1,0:T(8,128)(2,1)S(1)}, u32[]{:S(2)}, u32[]{:S(2)}) collective-permute-start(bf16[112,256]{1,0:T(8,128)(2,1)S(1)} %collective-permute-done.5.refs_6_), channel_id=1, source_target_pairs={{0,24},{1,25},{2,26},{3,27},{4,28},{5,29},{6,30},{7,31},{8,16},{9,... | collective-permute-start | bytes 172040 | tf_op jit(solution)/shard_map/ppermute | solution.py:35
  26.9 0.0 collective-permute-done.9.refs_10_
  26.9 0.2 collective-permute-start.15
  27.2 2.7 %collective-permute-done.10.refs_11_ = bf16[112,256]{1,0:T(8,128)(2,1)S(1)} collective-permute-done((bf16[112,256]{1,0:T(8,128)(2,1)S(1)}, bf16[112,256]{1,0:T(8,128)(2,1)S(1)}, u32[]{:S(2)}, u32[]{:S(2)}) %collective-permute-start.10) | collective-permute-done | bytes 57376 | tf_op jit(solution)/shard_map/ppermute | solution.py:35
  29.8 0.0 collective-permute-start.16
  29.8 0.0 collective-permute-done.15.refs_16_
  29.8 0.5 collective-permute-start.17
  30.3 0.7 %collective-permute-done.16.refs_17_ = bf16[112,256]{1,0:T(8,128)(2,1)S(1)} collective-permute-done((bf16[112,256]{1,0:T(8,128)(2,1)S(1)}, bf16[112,256]{1,0:T(8,128)(2,1)S(1)}, u32[]{:S(2)}, u32[]{:S(2)}) %collective-permute-start.16) | collective-permute-done | bytes 57376 | tf_op jit(solution)/shard_map/ppermute | solution.py:35
  31.1 0.2 collective-permute-done.17.refs_18_
  31.2 0.0 collective-permute-done.12.refs_13_
  31.2 0.0 collective-permute-done.13.refs_14_
  31.2 0.0 collective-permute-done.14.refs_15_
  31.3 0.0 copy-done.1
  31.3 8.3 %shard_map.51 = (f32[8,128]{1,0:T(8,128)}, f32[32,96]{1,0:T(8,128)S(1)}) custom-call(bf16[1024,256]{1,0:T(8,128)(2,1)S(1)} %copy-done.1, bf16[112,256]{1,0:T(8,128)(2,1)S(1)} %copy-done, bf16[112,256]{1,0:T(8,128)(2,1)S(1)} %collective-permute-done.refs_1_, bf16[112,256]{1,0:T(8,128)(2,1)S(1)} %collective-permute-done.1.refs_2_, ...), custom_call_target="tpu_custom_call" | custom-call | flops 1610612736 | bytes 2097152 | tf_op jit(solution)/shard_map/pallas_call | solution.py:192
  39.5 10.9 %all_to_all.12 = f32[32,1,96]{2,1,0:T(1,128)S(1)} all-to-all(f32[32,1,96]{2,1,0:T(1,128)S(1)} %bitcast.6), channel_id=1, replica_groups=mesh['gen'=8,'dat'=4] {'dat','gen'}, dimensions={0} | all-to-all | bytes 24576 | tf_op jit(solution)/shard_map/all_to_all | solution.py:210
  50.4 0.1 reduce_max.9
  50.5 0.0 copy-start.2
  50.5 0.6 %copy-done.2 = f32[96]{0:T(128)S(1)} copy-done((f32[96]{0:T(128)S(1)}, f32[96]{0:T(128)}, u32[]{:S(2)}) %copy-start.2) | copy-done | bytes 408
  51.1 0.5 %subtract_add_fusion = f32[96]{0:T(128)} fusion(f32[96]{0:T(128)S(1)} %copy-done.2, f32[96]{0:T(128)S(1)} %reduce_max.9, f32[96]{0:T(128)S(1)} %exponential_reduce_fusion), kind=kLoop, calls=%fused_computation.10 | loop fusion | flops 480 | bytes 1536 | tf_op jit(solution)/shard_map/add | solution.py:213
  (7 shorter events, 0.1 us)
Async XLA Ops:
  0.6 30.6 %copy-start.1 = (bf16[1024,256]{1,0:T(8,128)(2,1)S(1)}, bf16[1024,256]{1,0:T(8,128)(2,1)}, u32[]{:S(2)}) copy-start(bf16[1024,256]{1,0:T(8,128)(2,1)} %x_ref.1) | copy-start | bytes 1572868
  2.3 8.8 %collective-permute-start = (bf16[112,256]{1,0:T(8,128)(2,1)}, bf16[112,256]{1,0:T(8,128)(2,1)S(1)}, u32[]{:S(2)}, u32[]{:S(2)}) collective-permute-start(bf16[112,256]{1,0:T(8,128)(2,1)} %shard_map.50.refs_0_), channel_id=1, source_target_pairs={{0,8},{1,9},{2,10},{3,11},{4,12},{5,13},{6,14},{7,15},{8,0},{9,1},... | collective-permute-start | bytes 172040 | tf_op jit(solution)/shard_map/ppermute | solution.py:35
  5.3 6.4 %collective-permute-start.1 = (bf16[112,256]{1,0:T(8,128)(2,1)}, bf16[112,256]{1,0:T(8,128)(2,1)S(1)}, u32[]{:S(2)}, u32[]{:S(2)}) collective-permute-start(bf16[112,256]{1,0:T(8,128)(2,1)} %shard_map.50.refs_0_), channel_id=1, source_target_pairs={{0,16},{1,17},{2,18},{3,19},{4,20},{5,21},{6,22},{7,23},{8,24},{9,... | collective-permute-start | bytes 172040 | tf_op jit(solution)/shard_map/ppermute | solution.py:35
  7.9 6.2 %collective-permute-start.2 = (bf16[112,256]{1,0:T(8,128)(2,1)}, bf16[112,256]{1,0:T(8,128)(2,1)S(1)}, u32[]{:S(2)}, u32[]{:S(2)}) collective-permute-start(bf16[112,256]{1,0:T(8,128)(2,1)} %shard_map.50.refs_0_), channel_id=1, source_target_pairs={{0,24},{1,25},{2,26},{3,27},{4,28},{5,29},{6,30},{7,31},{8,16},{9,... | collective-permute-start | bytes 172040 | tf_op jit(solution)/shard_map/ppermute | solution.py:35
  7.9 7.8 %collective-permute-start.3 = (bf16[112,256]{1,0:T(8,128)(2,1)}, bf16[112,256]{1,0:T(8,128)(2,1)S(1)}, u32[]{:S(2)}, u32[]{:S(2)}) collective-permute-start(bf16[112,256]{1,0:T(8,128)(2,1)} %shard_map.50.refs_0_), channel_id=1, source_target_pairs={{0,2},{1,3},{2,0},{3,1},{4,6},{5,7},{6,4},{7,5},{8,10},{9,11},{10,... | collective-permute-start | bytes 172040 | tf_op jit(solution)/shard_map/ppermute | solution.py:35
  9.6 6.1 %collective-permute-start.4 = (bf16[112,256]{1,0:T(8,128)(2,1)}, bf16[112,256]{1,0:T(8,128)(2,1)S(1)}, u32[]{:S(2)}, u32[]{:S(2)}) collective-permute-start(bf16[112,256]{1,0:T(8,128)(2,1)} %shard_map.50.refs_0_), channel_id=1, source_target_pairs={{0,4},{1,5},{2,6},{3,7},{4,0},{5,1},{6,2},{7,3},{8,12},{9,13},{10,... | collective-permute-start | bytes 172040 | tf_op jit(solution)/shard_map/ppermute | solution.py:35
  11.1 5.8 %collective-permute-start.5 = (bf16[112,256]{1,0:T(8,128)(2,1)}, bf16[112,256]{1,0:T(8,128)(2,1)S(1)}, u32[]{:S(2)}, u32[]{:S(2)}) collective-permute-start(bf16[112,256]{1,0:T(8,128)(2,1)} %shard_map.50.refs_0_), channel_id=1, source_target_pairs={{0,6},{1,7},{2,4},{3,5},{4,2},{5,3},{6,0},{7,1},{8,14},{9,15},{10,... | collective-permute-start | bytes 172040 | tf_op jit(solution)/shard_map/ppermute | solution.py:35
  14.1 7.4 %collective-permute-start.6 = (bf16[336,256]{1,0:T(8,128)(2,1)S(1)}, bf16[336,256]{1,0:T(8,128)(2,1)S(1)}, u32[]{:S(2)}, u32[]{:S(2)}) collective-permute-start(bf16[336,256]{1,0:T(8,128)(2,1)S(1)} %get-tuple-element.7), channel_id=1, source_target_pairs={{0,2},{1,3},{2,0},{3,1},{4,6},{5,7},{6,4},{7,5},{8,10},{9,11},{10,... | collective-permute-start | bytes 516104 | tf_op jit(solution)/shard_map/ppermute | solution.py:35
  15.7 1.8 %copy-start = (bf16[112,256]{1,0:T(8,128)(2,1)S(1)}, bf16[112,256]{1,0:T(8,128)(2,1)}, u32[]{:S(2)}) copy-start(bf16[112,256]{1,0:T(8,128)(2,1)} %shard_map.50.refs_0_) | copy-start | bytes 172036
  16.9 14.3 %collective-permute-start.12 = (bf16[672,256]{1,0:T(8,128)(2,1)S(1)}, bf16[672,256]{1,0:T(8,128)(2,1)S(1)}, u32[]{:S(2)}, u32[]{:S(2)}) collective-permute-start(bf16[672,256]{1,0:T(8,128)(2,1)S(1)} %constant_dynamic-update-slice_fusion.3), channel_id=1, source_target_pairs={{0,1},{1,0},{2,3},{3,2},{4,5},{5,4},{6,7},{7,6},{8,9},{9,8},{10,11... | collective-permute-start | bytes 1032200 | tf_op jit(solution)/shard_map/ppermute | solution.py:35
  16.9 6.8 %collective-permute-start.7 = (bf16[336,256]{1,0:T(8,128)(2,1)S(1)}, bf16[336,256]{1,0:T(8,128)(2,1)S(1)}, u32[]{:S(2)}, u32[]{:S(2)}) collective-permute-start(bf16[336,256]{1,0:T(8,128)(2,1)S(1)} %get-tuple-element.7), channel_id=1, source_target_pairs={{0,4},{1,5},{2,6},{3,7},{4,0},{5,1},{6,2},{7,3},{8,12},{9,13},{10,... | collective-permute-start | bytes 516104 | tf_op jit(solution)/shard_map/ppermute | solution.py:35
  17.5 1.2 %collective-permute-start.11 = (bf16[112,256]{1,0:T(8,128)(2,1)S(1)}, bf16[112,256]{1,0:T(8,128)(2,1)S(1)}, u32[]{:S(2)}, u32[]{:S(2)}) collective-permute-start(bf16[112,256]{1,0:T(8,128)(2,1)S(1)} %copy-done), channel_id=1, source_target_pairs={{0,1},{1,0},{2,3},{3,2},{4,5},{5,4},{6,7},{7,6},{8,9},{9,8},{10,11... | collective-permute-start | bytes 172040 | tf_op jit(solution)/shard_map/ppermute | solution.py:35
  17.6 6.1 %collective-permute-start.8 = (bf16[112,256]{1,0:T(8,128)(2,1)S(1)}, bf16[112,256]{1,0:T(8,128)(2,1)S(1)}, u32[]{:S(2)}, u32[]{:S(2)}) collective-permute-start(bf16[112,256]{1,0:T(8,128)(2,1)S(1)} %collective-permute-done.5.refs_6_), channel_id=1, source_target_pairs={{0,8},{1,9},{2,10},{3,11},{4,12},{5,13},{6,14},{7,15},{8,0},{9,1},... | collective-permute-start | bytes 172040 | tf_op jit(solution)/shard_map/ppermute | solution.py:35
  18.7 8.2 %collective-permute-start.9 = (bf16[112,256]{1,0:T(8,128)(2,1)S(1)}, bf16[112,256]{1,0:T(8,128)(2,1)S(1)}, u32[]{:S(2)}, u32[]{:S(2)}) collective-permute-start(bf16[112,256]{1,0:T(8,128)(2,1)S(1)} %collective-permute-done.5.refs_6_), channel_id=1, source_target_pairs={{0,16},{1,17},{2,18},{3,19},{4,20},{5,21},{6,22},{7,23},{8,24},{9,... | collective-permute-start | bytes 172040 | tf_op jit(solution)/shard_map/ppermute | solution.py:35
  21.5 9.8 %collective-permute-start.13 = (bf16[336,256]{1,0:T(8,128)(2,1)S(1)}, bf16[336,256]{1,0:T(8,128)(2,1)S(1)}, u32[]{:S(2)}, u32[]{:S(2)}) collective-permute-start(bf16[336,256]{1,0:T(8,128)(2,1)S(1)} %collective-permute-done.6.refs_7_), channel_id=1, source_target_pairs={{0,1},{1,0},{2,3},{3,2},{4,5},{5,4},{6,7},{7,6},{8,9},{9,8},{10,11... | collective-permute-start | bytes 516104 | tf_op jit(solution)/shard_map/ppermute | solution.py:35
  23.7 7.6 %collective-permute-start.14 = (bf16[336,256]{1,0:T(8,128)(2,1)S(1)}, bf16[336,256]{1,0:T(8,128)(2,1)S(1)}, u32[]{:S(2)}, u32[]{:S(2)}) collective-permute-start(bf16[336,256]{1,0:T(8,128)(2,1)S(1)} %collective-permute-done.7.refs_8_), channel_id=1, source_target_pairs={{0,1},{1,0},{2,3},{3,2},{4,5},{5,4},{6,7},{7,6},{8,9},{9,8},{10,11... | collective-permute-start | bytes 516104 | tf_op jit(solution)/shard_map/ppermute | solution.py:35
  23.7 6.1 %collective-permute-start.10 = (bf16[112,256]{1,0:T(8,128)(2,1)S(1)}, bf16[112,256]{1,0:T(8,128)(2,1)S(1)}, u32[]{:S(2)}, u32[]{:S(2)}) collective-permute-start(bf16[112,256]{1,0:T(8,128)(2,1)S(1)} %collective-permute-done.5.refs_6_), channel_id=1, source_target_pairs={{0,24},{1,25},{2,26},{3,27},{4,28},{5,29},{6,30},{7,31},{8,16},{9,... | collective-permute-start | bytes 172040 | tf_op jit(solution)/shard_map/ppermute | solution.py:35
  26.9 2.9 %collective-permute-start.15 = (bf16[112,256]{1,0:T(8,128)(2,1)S(1)}, bf16[112,256]{1,0:T(8,128)(2,1)S(1)}, u32[]{:S(2)}, u32[]{:S(2)}) collective-permute-start(bf16[112,256]{1,0:T(8,128)(2,1)S(1)} %collective-permute-done.8.refs_9_), channel_id=1, source_target_pairs={{0,1},{1,0},{2,3},{3,2},{4,5},{5,4},{6,7},{7,6},{8,9},{9,8},{10,11... | collective-permute-start | bytes 172040 | tf_op jit(solution)/shard_map/ppermute | solution.py:35
  29.8 1.2 %collective-permute-start.16 = (bf16[112,256]{1,0:T(8,128)(2,1)S(1)}, bf16[112,256]{1,0:T(8,128)(2,1)S(1)}, u32[]{:S(2)}, u32[]{:S(2)}) collective-permute-start(bf16[112,256]{1,0:T(8,128)(2,1)S(1)} %collective-permute-done.9.refs_10_), channel_id=1, source_target_pairs={{0,1},{1,0},{2,3},{3,2},{4,5},{5,4},{6,7},{7,6},{8,9},{9,8},{10,11... | collective-permute-start | bytes 172040 | tf_op jit(solution)/shard_map/ppermute | solution.py:35
  29.8 1.4 %collective-permute-start.17 = (bf16[112,256]{1,0:T(8,128)(2,1)S(1)}, bf16[112,256]{1,0:T(8,128)(2,1)S(1)}, u32[]{:S(2)}, u32[]{:S(2)}) collective-permute-start(bf16[112,256]{1,0:T(8,128)(2,1)S(1)} %collective-permute-done.10.refs_11_), channel_id=1, source_target_pairs={{0,1},{1,0},{2,3},{3,2},{4,5},{5,4},{6,7},{7,6},{8,9},{9,8},{10,11... | collective-permute-start | bytes 172040 | tf_op jit(solution)/shard_map/ppermute | solution.py:35
  50.5 0.7 %copy-start.2 = (f32[96]{0:T(128)S(1)}, f32[96]{0:T(128)}, u32[]{:S(2)}) copy-start(f32[96]{0:T(128)} %param.5) | copy-start | bytes 1156

commit v5 on v3

v5 whole, which is shorter than its diff:
```python
import functools
import math

import jax
import jax.numpy as jnp
from jax import lax
from jax.experimental import pallas as pl
from jax.experimental.pallas import tpu as pltpu
from jax.sharding import PartitionSpec as P

EPS = 0.05
LOG2E = 1.4426950408889634
LN2 = 0.6931471805599453
SCALE = LOG2E / EPS
LANES = 128
TILE = 16
LIFT = 100.0
FLOOR = 2.0**-90
VMEM_LIMIT = 40 * 1024 * 1024


def round_up(value, step):
    return -(-value // step) * step


def swap(value, axis, mask):
    return lax.ppermute(value, axis, [(k, k ^ mask) for k in range(lax.axis_size(axis))])


def sent(block, axis, mask):
    array, masks = block
    return swap(array, axis, mask), [m ^ mask for m in masks]


def join(blocks):
    arrays = [array for array, _ in blocks]
    whole = arrays[0] if len(arrays) == 1 else jnp.concatenate(arrays, axis=0)
    return whole, [m for _, masks in blocks for m in masks]


def gather(gen_own, data_own):
    n_dat, n_gen = lax.axis_size("dat"), lax.axis_size("gen")
    gens = [(gen_own, [0])]
    bit = n_dat // 2
    while bit > 1:
        gens += [sent(block, "dat", bit) for block in gens]
        bit //= 2
    own = (data_own, [0])
    column = join([own] + [sent(own, "gen", m) for m in range(2, n_gen, 2)])
    parts = [column, sent(column, "gen", 1)]
    gens.insert(1, sent(gens[0], "dat", 1))
    held, _ = lax.optimization_barrier(([array for array, _ in gens[2:]], parts[1][0]))
    later = [sent((array, masks), "dat", 1) for array, (_, masks) in zip(held, gens[2:])]
    return gens, later, parts


def pack_kernel(y_ref, g_ref, packed_ref):
    share, width = y_ref.shape
    tall = packed_ref.shape[0] - TILE
    y = y_ref[...]
    wide = y.astype(jnp.float32)
    sq = jnp.sum(wide * wide, axis=1, keepdims=True)
    sq = jnp.broadcast_to(sq, (share, LANES)).T[0:1, :]
    bias = SCALE * (g_ref[...] - sq / width)
    first = bias.astype(jnp.bfloat16).astype(jnp.float32)
    rest = bias - first
    second = rest.astype(jnp.bfloat16).astype(jnp.float32)
    third = rest - second
    row = lax.broadcasted_iota(jnp.int32, (TILE, share), 0)
    pieces = jnp.where(row == 0, first, jnp.where(row == 1, second, jnp.where(row == 2, third, 0.0)))
    if share < tall:
        packed_ref[...] = jnp.zeros(packed_ref.shape, jnp.bfloat16)
    else:
        packed_ref[tall:, :] = jnp.zeros((TILE, width), jnp.bfloat16)
    packed_ref[:share, :] = y
    packed_ref[tall:, :share] = pieces.astype(jnp.bfloat16)


def unpack(parts, share, y_ref, b_ref):
    tall = round_up(share, TILE)
    span = tall + TILE
    batch = TILE // math.gcd(share, TILE)
    held = []
    k = 0
    for part in parts:
        for start in range(0, part.shape[0], span):
            pieces = part[start + tall : start + span, :share].astype(jnp.float32)
            bias = pieces[0:1, :] + pieces[1:2, :] + pieces[2:3, :]
            b_ref[k * share : (k + 1) * share, :] = jnp.broadcast_to(bias, (LANES, share)).T
            if batch == 1:
                y_ref[k * share : (k + 1) * share, :] = part[start : start + share, :]
            else:
                held.append(part[start : start + tall, :].astype(jnp.float32)[:share, :])
                if len(held) == batch:
                    end = (k + 1) * share
                    y_ref[end - batch * share : end, :] = jnp.concatenate(held, axis=0).astype(jnp.bfloat16)
                    held = []
            k += 1


def norm_kernel(x_ref, sq_ref):
    for k in range(sq_ref.shape[0]):
        x = x_ref[k * LANES : (k + 1) * LANES, :].astype(jnp.float32)
        sq = jnp.sum(x * x, axis=1, keepdims=True)
        sq_ref[k : k + 1, :] = jnp.broadcast_to(sq, (LANES, LANES)).T[0:1, :]


def spans(total, step):
    return [(start, min(step, total - start)) for start in range(0, total, step)]


def scores(y, x, bias, alpha):
    dots = lax.dot_general(y, x, (((1,), (1,)), ((), ())), preferred_element_type=jnp.float32)
    return alpha * dots + jnp.concatenate([bias] * (dots.shape[1] // LANES), axis=1)


def eight(values, op):
    groups = values.reshape(values.shape[0] // 8, 8, values.shape[1])
    return op(groups, axis=0)


def fold(values, op):
    out = values[:, :LANES]
    for start in range(LANES, values.shape[1], LANES):
        out = op(out, values[:, start : start + LANES])
    return out


def first_row_kernel(*refs, count, share, block, tall):
    xs, refs = refs[:count], refs[count:]
    *parts, l_ref, y_ref, b_ref, t_ref = refs
    unpack(parts, share, y_ref, b_ref)
    row_kernel(*xs, y_ref, b_ref, l_ref, t_ref, block=block, tall=tall)


def row_kernel(*refs, block, tall):
    *xs, y_ref, b_ref, l_ref, t_ref = refs
    cols, width = y_ref.shape
    rows = xs[0].shape[0]
    alpha = 2.0 * SCALE / width
    for place, x_ref in enumerate(xs):

        def step(index, carry, place=place, x_ref=x_ref):
            x = x_ref[pl.ds(pl.multiple_of(index * block, block), block), :]
            top = None
            for start, size in spans(cols, tall):
                here = slice(start, start + size)
                t = scores(y_ref[here, :], x, b_ref[here, :], alpha)
                t_ref[here, :] = t
                part = eight(t, jnp.max)
                top = part if top is None else jnp.maximum(top, part)
            top = jnp.max(top, axis=0, keepdims=True)
            total = None
            for start, size in spans(cols, tall):
                part = eight(jnp.exp2(t_ref[start : start + size, :] - top), jnp.sum)
                total = part if total is None else total + part
            log_sum = top + jnp.log2(jnp.sum(total, axis=0, keepdims=True))
            for k in range(block // LANES):
                row = (place * rows + index * block) // LANES + k
                l_ref[pl.ds(row, 1), :] = log_sum[:, k * LANES : (k + 1) * LANES]
            return carry

        lax.fori_loop(0, rows // block, step, 0)


def column_kernel(*refs, count, share, block, tall, orders, masks, log_cols):
    xs, refs = refs[:count], refs[count:]
    logs, refs = refs[: len(orders)], refs[len(orders) :]
    sq_ref, y_ref, b_ref, f_ref, col_ref, l_ref, sum_ref, top_ref = refs
    cols, width = y_ref.shape
    rows = xs[0].shape[0]
    alpha = 2.0 * SCALE / width
    tiles = rows // LANES
    for k in range(count):
        pieces = [log[order[k] * tiles : (order[k] + 1) * tiles, :] for log, order in zip(logs, orders)]
        top = functools.reduce(jnp.maximum, pieces)
        l_ref[k * tiles : (k + 1) * tiles, :] = top + jnp.log2(sum(jnp.exp2(piece - top) for piece in pieces))
    f_ref[...] = sq_ref[...] / width - (EPS * LN2) * l_ref[:tiles, :] + EPS * log_cols

    def each(visit):
        for place, x_ref in enumerate(xs):

            def step(index, carry, place=place, x_ref=x_ref):
                x = x_ref[pl.ds(pl.multiple_of(index * block, block), block), :]
                first = (place * rows + index * block) // LANES
                logs_here = [l_ref[pl.ds(first + k, 1), :] for k in range(block // LANES)]
                log_here = jnp.concatenate(logs_here, axis=1)
                for start, size in spans(cols, tall):
                    here = slice(start, start + size)
                    visit(here, scores(y_ref[here, :], x, b_ref[here, :], alpha) - log_here)
                return carry

            lax.fori_loop(0, rows // block, step, 0)

    def add(here, values):
        sum_ref[here, :] += fold(jnp.exp2(values + LIFT), jnp.add)

    def raise_top(here, values):
        top_ref[here, :] = jnp.maximum(top_ref[here, :], fold(values, jnp.maximum))

    def add_from_top(here, values):
        top = jnp.concatenate([top_ref[here, :]] * (block // LANES), axis=1)
        sum_ref[here, :] += fold(jnp.exp2(values - top), jnp.add)

    sum_ref[...] = jnp.zeros(sum_ref.shape, jnp.float32)
    each(add)
    least = jnp.min(jnp.sum(sum_ref[...], axis=1, keepdims=True))
    top_ref[...] = jnp.full(top_ref.shape, -LIFT, jnp.float32)

    @pl.when(jnp.logical_not(least >= FLOOR))
    def _():
        top_ref[...] = jnp.full(top_ref.shape, -jnp.inf, jnp.float32)
        each(raise_top)
        top = jnp.max(top_ref[...], axis=1, keepdims=True)
        top_ref[...] = jnp.broadcast_to(top, top_ref.shape)
        sum_ref[...] = jnp.zeros(sum_ref.shape, jnp.float32)
        each(add_from_top)

    gen = lax.axis_index("gen")
    for k, mask in enumerate(masks):
        here = slice(k * share, (k + 1) * share)
        total = jnp.sum(sum_ref[here, :].T, axis=0, keepdims=True)
        col_ref[pl.ds(gen ^ mask, 1), :] = top_ref[here, :].T[0:1, :] + jnp.log2(total)


def per_device(gen_samples, data_samples, data_potential):
    rows, width = gen_samples.shape
    n_gen, n_dat = lax.axis_size("gen"), lax.axis_size("dat")
    share = data_samples.shape[0]
    cols = share * n_gen
    tiles = rows // LANES
    params = pltpu.CompilerParams(vmem_limit_bytes=VMEM_LIMIT)
    packed = pl.pallas_call(
        pack_kernel,
        out_shape=jax.ShapeDtypeStruct((round_up(share, TILE) + TILE, width), jnp.bfloat16),
    )(data_samples, data_potential.reshape(1, share))
    early, late, parts = gather(gen_samples, packed)
    sq = pl.pallas_call(norm_kernel, out_shape=jax.ShapeDtypeStruct((tiles, LANES), jnp.float32))(gen_samples)
    order = [owners[0] for _, owners in early + late]
    masks = [m for _, owners in parts for m in owners]
    early, late, parts = [[array for array, _ in blocks] for blocks in (early, late, parts)]
    block = min(256, rows)
    tall = 128

    def cost(count):
        return pl.CostEstimate(
            flops=2 * rows * count * cols * width,
            bytes_accessed=2 * (rows * count + cols) * width,
            transcendentals=rows * count * cols,
        )

    scratch = [pltpu.VMEM((cols, block), jnp.float32)]
    log_early, y, bias = pl.pallas_call(
        functools.partial(first_row_kernel, count=len(early), share=share, block=block, tall=tall),
        out_shape=(
            jax.ShapeDtypeStruct((len(early) * tiles, LANES), jnp.float32),
            jax.ShapeDtypeStruct((cols, width), jnp.bfloat16),
            jax.ShapeDtypeStruct((cols, LANES), jnp.float32),
        ),
        scratch_shapes=scratch,
        compiler_params=params,
        cost_estimate=cost(len(early)),
    )(*early, *parts)
    log_late = pl.pallas_call(
        functools.partial(row_kernel, block=block, tall=tall),
        out_shape=jax.ShapeDtypeStruct((len(late) * tiles, LANES), jnp.float32),
        scratch_shapes=scratch,
        compiler_params=params,
        cost_estimate=cost(len(late)),
    )(*late, y, bias)
    log_own = jnp.concatenate([log_early, log_late], axis=0)
    logs = [log_own] + [swap(log_own, "dat", m) for m in order[1:]]
    orders = [[order.index(m ^ partner) for m in order] for partner in order]
    f, col = pl.pallas_call(
        functools.partial(
            column_kernel,
            count=n_dat,
            share=share,
            block=block,
            tall=tall,
            orders=orders,
            masks=masks,
            log_cols=math.log(cols * n_dat),
        ),
        out_shape=(
            jax.ShapeDtypeStruct((tiles, LANES), jnp.float32),
            jax.ShapeDtypeStruct((n_gen, share), jnp.float32),
        ),
        scratch_shapes=[
            pltpu.VMEM((n_dat * tiles, LANES), jnp.float32),
            pltpu.VMEM((cols, LANES), jnp.float32),
            pltpu.VMEM((cols, LANES), jnp.float32),
        ],
        compiler_params=params,
        cost_estimate=cost(n_dat),
    )(*early, *late, *logs, sq, y, bias)
    totals = lax.all_to_all(col, "gen", 0, 0, tiled=True)
    top = jnp.max(totals, axis=0)
    total = top + jnp.log2(jnp.sum(jnp.exp2(totals - top[None, :]), axis=0))
    new_data = data_potential - (EPS * LN2) * total + EPS * math.log(rows * n_gen / cols)
    return f.reshape(rows), new_data


def solution(mesh):
    in_specs = (P(("gen", "dat"), None), P(("dat", "gen"), None), P(("dat", "gen")))
    out_specs = (P(("gen", "dat")), P(("dat", "gen")))
    return jax.shard_map(per_device, mesh=mesh, in_specs=in_specs, out_specs=out_specs, check_vma=False)
```

time: 48.4 us -> 68 us (1.40)
  Pallas kernels: 9.8 us -> 32.9 us
  waiting for transfers between devices: 14.3 us -> 10.9 us
  starting transfers between devices: 9.69 us -> 11 us
  local copies, waits for them, and re-layouts: 2.57 us -> 1.33 us
  blocking collectives: 10.5 us -> 9.47 us
  other arithmetic: 0.6 us -> 1.41 us
    pallas_call x2 -> x5, Pallas kernels: 9.8 us -> 32.9 us  [the longest x1 20.7 us: per_device(): pl.pallas_call(functools.partial(column_kernel, count=n_dat, share=share,...]
    ppermute x10, waiting for transfers between devices: 14.3 us -> 10.9 us  [swap(): lax.ppermute(value, axis, [(k, k ^ mask) for k in range(lax.axis_size(axi...]
    ppermute x10, starting transfers between devices: 9.69 us -> 11 us  [swap(): lax.ppermute(value, axis, [(k, k ^ mask) for k in range(lax.axis_size(axi...]
    unnamed x7 -> x8, local copies, waits for them, and re-layouts: 2.56 us -> 1.33 us
    all_to_all x1, blocking collectives: 10.5 us -> 9.47 us  [per_device(): totals = lax.all_to_all(col, 'gen', 0, 0, tiled=True)]
    concatenate x0 -> x2, other arithmetic: none -> 0.84 us  [the longest x1 0.83 us: join(): whole = arrays[0] if len(arrays) == 1 else jnp.concatenate(arrays, axis=0)]
  transfers between devices with their start and end apart: 10 -> 10, of which waited for: 6 -> 4; matrix products, arithmetic and copies ran while one was open for 2% -> 1% of each run, Pallas kernels for 0% -> 15%
where the time goes in v5:
time: 68 us; the launch traced here: 67.7 us
  Pallas kernels  32.9 us (48%)
  starting transfers between devices  11 us (16%)
  waiting for transfers between devices  10.9 us (16%)
  blocking collectives  9.47 us (14%)
  other arithmetic  1.41 us (2%)
  local copies, waits for them, and re-layouts  1.33 us (2%)
  between operations  0.7 us (1%)
    pallas_call x1, Pallas kernels, per_device(): pl.pallas_call(functools.partial(column_kernel, count=n_dat, share=share,...  20.7 us
    ppermute x10, starting transfers between devices, swap(): lax.ppermute(value, axis, [(k, k ^ mask) for k in range(lax.axis_size(axi...  11 us
    ppermute x10, waiting for transfers between devices, swap(): lax.ppermute(value, axis, [(k, k ^ mask) for k in range(lax.axis_size(axi...  10.9 us
    all_to_all x1, blocking collectives, per_device(): totals = lax.all_to_all(col, 'gen', 0, 0, tiled=True)  9.47 us
    pallas_call x1, Pallas kernels, per_device(): pl.pallas_call(functools.partial(first_row_kernel, count=len(early), shar...  6.49 us
    pallas_call x1, Pallas kernels, per_device(): pl.pallas_call(functools.partial(row_kernel, block=block, tall=tall), out...  2.1 us
    pallas_call x1, Pallas kernels, per_device(): pl.pallas_call(norm_kernel, out_shape=jax.ShapeDtypeStruct((tiles, LANES)...  1.99 us
    pallas_call x1, Pallas kernels, per_device(): pl.pallas_call(pack_kernel, out_shape=jax.ShapeDtypeStruct((round_up(shar...  1.58 us
  transfers between devices with their start and end apart: 10, of which 4 were waited for; matrix products, arithmetic and copies ran while one was open for 1% of the time, Pallas kernels for 15%

profile of v5, /device:TPU:0, one launch (start us, length us, event | category | flops | bytes accessed | tf_op | source)
XLA Modules:
  0.0 67.7 jit_solution(30213484500494305)
XLA Ops:
  0.6 0.0 copy-start
  0.6 3.0 %collective-permute-start.1 = (bf16[1024,256]{1,0:T(8,128)(2,1)}, bf16[1024,256]{1,0:T(8,128)(2,1)S(1)}, u32[]{:S(2)}, u32[]{:S(2)}) collective-permute-start(bf16[1024,256]{1,0:T(8,128)(2,1)} %refs_0_.3), channel_id=1, source_target_pairs={{0,2},{1,3},{2,0},{3,1},{4,6},{5,7},{6,4},{7,5},{8,10},{9,11},{10,... | collective-permute-start | bytes 1572872 | tf_op jit(solution)/shard_map/ppermute | solution.py:27
  3.6 1.6 %shard_map.50 = bf16[112,256]{1,0:T(8,128)(2,1)} custom-call(bf16[96,256]{1,0:T(8,128)(2,1)} %y_ref.1, f32[1,96]{1,0:T(1,128)} %bitcast.8), custom_call_target="tpu_custom_call" | custom-call | tf_op jit(solution)/shard_map/pallas_call | solution.py:233
  5.2 1.6 %collective-permute-start.2 = (bf16[112,256]{1,0:T(8,128)(2,1)}, bf16[112,256]{1,0:T(8,128)(2,1)S(1)}, u32[]{:S(2)}, u32[]{:S(2)}) collective-permute-start(bf16[112,256]{1,0:T(8,128)(2,1)} %shard_map.50), channel_id=1, source_target_pairs={{0,8},{4,12},{8,0},{12,4},{16,24},{20,28},{24,16},{28,20},{1,9},{5... | collective-permute-start | bytes 172040 | tf_op jit(solution)/shard_map/ppermute | solution.py:27
  6.8 2.6 %collective-permute-start.3 = (bf16[112,256]{1,0:T(8,128)(2,1)}, bf16[112,256]{1,0:T(8,128)(2,1)S(1)}, u32[]{:S(2)}, u32[]{:S(2)}) collective-permute-start(bf16[112,256]{1,0:T(8,128)(2,1)} %shard_map.50), channel_id=1, source_target_pairs={{0,16},{4,20},{8,24},{12,28},{16,0},{20,4},{24,8},{28,12},{1,17},{... | collective-permute-start | bytes 172040 | tf_op jit(solution)/shard_map/ppermute | solution.py:27
  9.4 0.2 collective-permute-start.4
  9.6 0.0 collective-permute-done.2
  9.6 3.3 %collective-permute-done.3 = bf16[112,256]{1,0:T(8,128)(2,1)S(1)} collective-permute-done((bf16[112,256]{1,0:T(8,128)(2,1)}, bf16[112,256]{1,0:T(8,128)(2,1)S(1)}, u32[]{:S(2)}, u32[]{:S(2)}) %collective-permute-start.3) | collective-permute-done | bytes 57376 | tf_op jit(solution)/shard_map/ppermute | solution.py:27
  12.9 2.7 %collective-permute-done.4 = bf16[112,256]{1,0:T(8,128)(2,1)S(1)} collective-permute-done((bf16[112,256]{1,0:T(8,128)(2,1)}, bf16[112,256]{1,0:T(8,128)(2,1)S(1)}, u32[]{:S(2)}, u32[]{:S(2)}) %collective-permute-start.4) | collective-permute-done | bytes 57376 | tf_op jit(solution)/shard_map/ppermute | solution.py:27
  15.6 0.8 %pad_maximum_fusion.refs_3_ = bf16[448,256]{1,0:T(8,128)(2,1)S(1)} fusion(bf16[112,256]{1,0:T(8,128)(2,1)S(1)} %collective-permute-done.4, bf16[112,256]{1,0:T(8,128)(2,1)S(1)} %collective-permute-done.3, bf16[112,256]{1,0:T(8,128)(2,1)S(1)} %collective-permute-done.2, bf16[112,256]{1,0:T(8,128)(2,1)} %shard_map.50), kind=kLoop, calls=%fused_computation | loop fusion | flops 917504 | bytes 458752 | tf_op jit(solution)/shard_map/concatenate | solution.py:37
  16.4 1.6 %collective-permute-start.5 = (bf16[448,256]{1,0:T(8,128)(2,1)S(1)}, bf16[448,256]{1,0:T(8,128)(2,1)S(1)}, u32[]{:S(2)}, u32[]{:S(2)}) collective-permute-start(bf16[448,256]{1,0:T(8,128)(2,1)S(1)} %pad_maximum_fusion.refs_3_), channel_id=1, source_target_pairs={{0,4},{4,0},{8,12},{12,8},{16,20},{20,16},{24,28},{28,24},{1,5},{5... | collective-permute-start | bytes 688136 | tf_op jit(solution)/shard_map/ppermute | solution.py:27
  18.0 0.0 copy-done
  18.0 0.0 collective-permute-start
  18.0 4.5 %collective-permute-done.5.refs_4_ = bf16[448,256]{1,0:T(8,128)(2,1)S(1)} collective-permute-done((bf16[448,256]{1,0:T(8,128)(2,1)S(1)}, bf16[448,256]{1,0:T(8,128)(2,1)S(1)}, u32[]{:S(2)}, u32[]{:S(2)}) %collective-permute-start.5) | collective-permute-done | bytes 229408 | tf_op jit(solution)/shard_map/ppermute | solution.py:27
  22.5 0.0 collective-permute-done.1.refs_2_
  22.5 0.0 collective-permute-start.6
  22.5 0.0 collective-permute-done.refs_1_
  22.5 6.5 %shard_map.51 = (f32[24,128]{1,0:T(8,128)S(1)}, bf16[768,256]{1,0:T(8,128)(2,1)S(1)}, f32[768,128]{1,0:T(8,128)S(1)}) custom-call(bf16[1024,256]{1,0:T(8,128)(2,1)S(1)} %copy-done, bf16[1024,256]{1,0:T(8,128)(2,1)S(1)} %collective-permute-done.refs_1_, bf16[1024,256]{1,0:T(8,128)(2,1)S(1)} %collective-permute-done.1.refs_2_, ...), custom_call_target="tpu_custom_call" | custom-call | flops 1207959552 | bytes 1966080 | tf_op jit(solution)/shard_map/pallas_call | solution.py:253
  29.0 0.0 collective-permute-done.6.refs_0_.refs_3_
  29.0 2.1 %shard_map.52 = f32[8,128]{1,0:T(8,128)S(1)} custom-call(bf16[1024,256]{1,0:T(8,128)(2,1)S(1)} %collective-permute-done.6.refs_0_.refs_3_, bf16[768,256]{1,0:T(8,128)(2,1)S(1)} %get-tuple-element.10.refs_1_.refs_9_, f32[768,128]{1,0:T(8,128)S(1)} %get-tuple-element.11.refs_2_.refs_10_), custom_call_target="tpu_custom_call" | custom-call | flops 402653184 | bytes 917504 | tf_op jit(solution)/shard_map/pallas_call | solution.py:264
  31.1 0.0 copy-start.1
  31.2 0.6 collective-permute-start.7
  31.7 0.5 collective-permute-start.8
  32.3 0.9 %collective-permute-start.9 = (f32[32,128]{1,0:T(8,128)S(1)}, f32[32,128]{1,0:T(8,128)S(1)}, u32[]{:S(2)}, u32[]{:S(2)}) collective-permute-start(f32[32,128]{1,0:T(8,128)S(1)} %pad_maximum_fusion.1.refs_4_), channel_id=1, source_target_pairs={{0,3},{1,2},{2,1},{3,0},{4,7},{5,6},{6,5},{7,4},{8,11},{9,10},{10,... | collective-permute-start | bytes 49160 | tf_op jit(solution)/shard_map/ppermute | solution.py:27
  33.2 2.0 %shard_map.53.refs_8_ = f32[8,128]{1,0:T(8,128)} custom-call(bf16[1024,256]{1,0:T(8,128)(2,1)} %refs_0_.3), custom_call_target="tpu_custom_call" | custom-call | tf_op jit(solution)/shard_map/pallas_call | solution.py:238
  35.1 0.0 collective-permute-done.7.refs_5_
  35.1 0.5 collective-permute-done.8.refs_6_
  35.6 0.0 collective-permute-done.9.refs_7_
  35.6 0.0 copy-done.1
  35.6 0.0 copy-start.2
  35.6 0.7 %copy-done.2 = f32[8,128]{1,0:T(8,128)S(1)} copy-done((f32[8,128]{1,0:T(8,128)S(1)}, f32[8,128]{1,0:T(8,128)}, u32[]{:S(2)}) %copy-start.2) | copy-done | bytes 4120
  36.3 20.7 %shard_map.54 = (f32[8,128]{1,0:T(8,128)}, f32[8,96]{1,0:T(8,128)S(1)}) custom-call(bf16[1024,256]{1,0:T(8,128)(2,1)S(1)} %copy-done.1, bf16[1024,256]{1,0:T(8,128)(2,1)S(1)} %collective-permute-done.refs_1_, bf16[1024,256]{1,0:T(8,128)(2,1)S(1)} %collective-permute-done.1.refs_2_, bf16[1024,256]{1,0:T(8,128)(2,1)S(1)} %collective-permute-done.6.refs_0_.refs_3_, ...), custom_call_target="tpu_custom_call" | custom-call | flops 1610612736 | bytes 2490368 | tf_op jit(solution)/shard_map/pallas_call | solution.py:274
  57.0 9.5 %all_to_all.12 = f32[8,1,96]{2,1,0:T(1,128)S(1)} all-to-all(f32[8,1,96]{2,1,0:T(1,128)S(1)} %bitcast.6), channel_id=1, replica_groups=mesh['gen'=8,'dat'=4] {'gen'}, dimensions={0} | all-to-all | bytes 6144 | tf_op jit(solution)/shard_map/all_to_all | solution.py:297
  66.5 0.0 copy-start.3
  66.5 0.6 copy-done.3
  67.1 0.5 subtract_add_fusion
  (3 shorter events, 0.1 us)
Async XLA Ops:
  0.6 17.4 %copy-start = (bf16[1024,256]{1,0:T(8,128)(2,1)S(1)}, bf16[1024,256]{1,0:T(8,128)(2,1)}, u32[]{:S(2)}) copy-start(bf16[1024,256]{1,0:T(8,128)(2,1)} %refs_0_.3) | copy-start | bytes 1572868
  0.6 21.9 %collective-permute-start.1 = (bf16[1024,256]{1,0:T(8,128)(2,1)}, bf16[1024,256]{1,0:T(8,128)(2,1)S(1)}, u32[]{:S(2)}, u32[]{:S(2)}) collective-permute-start(bf16[1024,256]{1,0:T(8,128)(2,1)} %refs_0_.3), channel_id=1, source_target_pairs={{0,2},{1,3},{2,0},{3,1},{4,6},{5,7},{6,4},{7,5},{8,10},{9,11},{10,... | collective-permute-start | bytes 1572872 | tf_op jit(solution)/shard_map/ppermute | solution.py:27
  5.2 4.4 %collective-permute-start.2 = (bf16[112,256]{1,0:T(8,128)(2,1)}, bf16[112,256]{1,0:T(8,128)(2,1)S(1)}, u32[]{:S(2)}, u32[]{:S(2)}) collective-permute-start(bf16[112,256]{1,0:T(8,128)(2,1)} %shard_map.50), channel_id=1, source_target_pairs={{0,8},{4,12},{8,0},{12,4},{16,24},{20,28},{24,16},{28,20},{1,9},{5... | collective-permute-start | bytes 172040 | tf_op jit(solution)/shard_map/ppermute | solution.py:27
  6.8 6.1 %collective-permute-start.3 = (bf16[112,256]{1,0:T(8,128)(2,1)}, bf16[112,256]{1,0:T(8,128)(2,1)S(1)}, u32[]{:S(2)}, u32[]{:S(2)}) collective-permute-start(bf16[112,256]{1,0:T(8,128)(2,1)} %shard_map.50), channel_id=1, source_target_pairs={{0,16},{4,20},{8,24},{12,28},{16,0},{20,4},{24,8},{28,12},{1,17},{... | collective-permute-start | bytes 172040 | tf_op jit(solution)/shard_map/ppermute | solution.py:27
  9.4 6.2 %collective-permute-start.4 = (bf16[112,256]{1,0:T(8,128)(2,1)}, bf16[112,256]{1,0:T(8,128)(2,1)S(1)}, u32[]{:S(2)}, u32[]{:S(2)}) collective-permute-start(bf16[112,256]{1,0:T(8,128)(2,1)} %shard_map.50), channel_id=1, source_target_pairs={{0,24},{4,28},{8,16},{12,20},{16,8},{20,12},{24,0},{28,4},{1,25},{... | collective-permute-start | bytes 172040 | tf_op jit(solution)/shard_map/ppermute | solution.py:27
  16.4 6.1 %collective-permute-start.5 = (bf16[448,256]{1,0:T(8,128)(2,1)S(1)}, bf16[448,256]{1,0:T(8,128)(2,1)S(1)}, u32[]{:S(2)}, u32[]{:S(2)}) collective-permute-start(bf16[448,256]{1,0:T(8,128)(2,1)S(1)} %pad_maximum_fusion.refs_3_), channel_id=1, source_target_pairs={{0,4},{4,0},{8,12},{12,8},{16,20},{20,16},{24,28},{28,24},{1,5},{5... | collective-permute-start | bytes 688136 | tf_op jit(solution)/shard_map/ppermute | solution.py:27
  18.0 4.5 %collective-permute-start = (bf16[1024,256]{1,0:T(8,128)(2,1)S(1)}, bf16[1024,256]{1,0:T(8,128)(2,1)S(1)}, u32[]{:S(2)}, u32[]{:S(2)}) collective-permute-start(bf16[1024,256]{1,0:T(8,128)(2,1)S(1)} %copy-done), channel_id=1, source_target_pairs={{0,1},{1,0},{2,3},{3,2},{4,5},{5,4},{6,7},{7,6},{8,9},{9,8},{10,11... | collective-permute-start | bytes 1572872 | tf_op jit(solution)/shard_map/ppermute | solution.py:27
  22.5 6.5 %collective-permute-start.6 = (bf16[1024,256]{1,0:T(8,128)(2,1)S(1)}, bf16[1024,256]{1,0:T(8,128)(2,1)S(1)}, u32[]{:S(2)}, u32[]{:S(2)}) collective-permute-start(bf16[1024,256]{1,0:T(8,128)(2,1)S(1)} %collective-permute-done.1.refs_2_), channel_id=1, source_target_pairs={{0,1},{1,0},{2,3},{3,2},{4,5},{5,4},{6,7},{7,6},{8,9},{9,8},{10,11... | collective-permute-start | bytes 1572872 | tf_op jit(solution)/shard_map/ppermute | solution.py:27
  31.1 4.5 %copy-start.1 = (bf16[1024,256]{1,0:T(8,128)(2,1)S(1)}, bf16[1024,256]{1,0:T(8,128)(2,1)}, u32[]{:S(2)}) copy-start(bf16[1024,256]{1,0:T(8,128)(2,1)} %refs_0_.3) | copy-start | bytes 1572868
  31.2 4.0 %collective-permute-start.7 = (f32[32,128]{1,0:T(8,128)S(1)}, f32[32,128]{1,0:T(8,128)S(1)}, u32[]{:S(2)}, u32[]{:S(2)}) collective-permute-start(f32[32,128]{1,0:T(8,128)S(1)} %pad_maximum_fusion.1.refs_4_), channel_id=1, source_target_pairs={{0,1},{1,0},{2,3},{3,2},{4,5},{5,4},{6,7},{7,6},{8,9},{9,8},{10,11... | collective-permute-start | bytes 49160 | tf_op jit(solution)/shard_map/ppermute | solution.py:27
  31.7 3.9 %collective-permute-start.8 = (f32[32,128]{1,0:T(8,128)S(1)}, f32[32,128]{1,0:T(8,128)S(1)}, u32[]{:S(2)}, u32[]{:S(2)}) collective-permute-start(f32[32,128]{1,0:T(8,128)S(1)} %pad_maximum_fusion.1.refs_4_), channel_id=1, source_target_pairs={{0,2},{1,3},{2,0},{3,1},{4,6},{5,7},{6,4},{7,5},{8,10},{9,11},{10,... | collective-permute-start | bytes 49160 | tf_op jit(solution)/shard_map/ppermute | solution.py:27
  32.3 3.3 %collective-permute-start.9 = (f32[32,128]{1,0:T(8,128)S(1)}, f32[32,128]{1,0:T(8,128)S(1)}, u32[]{:S(2)}, u32[]{:S(2)}) collective-permute-start(f32[32,128]{1,0:T(8,128)S(1)} %pad_maximum_fusion.1.refs_4_), channel_id=1, source_target_pairs={{0,3},{1,2},{2,1},{3,0},{4,7},{5,6},{6,5},{7,4},{8,11},{9,10},{10,... | collective-permute-start | bytes 49160 | tf_op jit(solution)/shard_map/ppermute | solution.py:27
  35.6 0.7 %copy-start.2 = (f32[8,128]{1,0:T(8,128)S(1)}, f32[8,128]{1,0:T(8,128)}, u32[]{:S(2)}) copy-start(f32[8,128]{1,0:T(8,128)} %shard_map.53.refs_8_) | copy-start | bytes 12292
  66.5 0.7 copy-start.3

commit v6 on v5

v6 whole, which is shorter than its diff:
```python
import functools
import math

import jax
import jax.numpy as jnp
from jax import lax
from jax.experimental import pallas as pl
from jax.experimental.pallas import tpu as pltpu
from jax.sharding import PartitionSpec as P

EPS = 0.05
LOG2E = 1.4426950408889634
LN2 = 0.6931471805599453
SCALE = LOG2E / EPS
LANES = 128
TILE = 16
LIFT = 100.0
FLOOR = 2.0**-90
VMEM_LIMIT = 40 * 1024 * 1024


def round_up(value, step):
    return -(-value // step) * step


def swap(value, axis, mask):
    return lax.ppermute(value, axis, [(k, k ^ mask) for k in range(lax.axis_size(axis))])


def gather(gen_own, message, column):
    n_dat, n_gen = lax.axis_size("dat"), lax.axis_size("gen")
    gens = [(gen_own, [0])]
    bit = n_dat // 2
    while bit > 1:
        gens += [(swap(array, "dat", bit), [m ^ bit for m in masks]) for array, masks in gens]
        bit //= 2
    span = message.shape[0]
    far = range(2, n_gen, 2)
    for k, mask in enumerate(far):
        column = lax.dynamic_update_slice(column, swap(message, "gen", mask), ((k + 1) * span, 0))
    masks = [(m, 0) for m in [0, *far]]
    near = swap(column, "gen", 1), [(g ^ 1, d) for g, d in masks]
    parts = [(column, masks), near]
    return gens, parts + [(swap(array, "dat", 1), [(g, 1) for g, _ in masks]) for array, masks in parts]


def pack_kernel(y_ref, g_ref, packed_ref, column_ref):
    share, width = y_ref.shape
    tall = packed_ref.shape[0] - TILE
    y = y_ref[...]
    wide = y.astype(jnp.float32)
    sq = jnp.sum(wide * wide, axis=1, keepdims=True)
    sq = jnp.broadcast_to(sq, (share, LANES)).T[0:1, :]
    bias = SCALE * (g_ref[...] - sq / width)
    first = bias.astype(jnp.bfloat16).astype(jnp.float32)
    rest = bias - first
    second = rest.astype(jnp.bfloat16).astype(jnp.float32)
    third = rest - second
    row = lax.broadcasted_iota(jnp.int32, (TILE, share), 0)
    pieces = jnp.where(row == 0, first, jnp.where(row == 1, second, jnp.where(row == 2, third, 0.0)))
    if share < tall:
        packed_ref[...] = jnp.zeros(packed_ref.shape, jnp.bfloat16)
    else:
        packed_ref[tall:, :] = jnp.zeros((TILE, width), jnp.bfloat16)
    packed_ref[:share, :] = y
    packed_ref[tall:, :share] = pieces.astype(jnp.bfloat16)
    column_ref[: packed_ref.shape[0], :] = packed_ref[...]


def unpack(parts, share, y_ref, b_ref):
    tall = round_up(share, TILE)
    span = tall + TILE
    batch = TILE // math.gcd(share, TILE)
    held = []
    k = 0
    for part in parts:
        for start in range(0, part.shape[0], span):
            pieces = part[start + tall : start + span, :share].astype(jnp.float32)
            bias = pieces[0:1, :] + pieces[1:2, :] + pieces[2:3, :]
            b_ref[k * share : (k + 1) * share, :] = jnp.broadcast_to(bias, (LANES, share)).T
            if batch == 1:
                y_ref[k * share : (k + 1) * share, :] = part[start : start + share, :]
            else:
                held.append(part[start : start + tall, :].astype(jnp.float32)[:share, :])
                if len(held) == batch:
                    end = (k + 1) * share
                    y_ref[end - batch * share : end, :] = jnp.concatenate(held, axis=0).astype(jnp.bfloat16)
                    held = []
            k += 1


def norm_kernel(x_ref, sq_ref):
    x = x_ref[...].astype(jnp.float32)
    square = x * x
    high = square.astype(jnp.bfloat16)
    low = (square - high.astype(jnp.float32)).astype(jnp.bfloat16)
    ones = jnp.ones((TILE, x.shape[1]), jnp.bfloat16)
    sq = jnp.zeros((TILE, x.shape[0]), jnp.float32)
    for half in (high, low):
        sq += lax.dot_general(ones, half, (((1,), (1,)), ((), ())), preferred_element_type=jnp.float32)
    for k in range(sq_ref.shape[0]):
        sq_ref[k : k + 1, :] = sq[0:1, k * LANES : (k + 1) * LANES]


def spans(total, step):
    return [(start, min(step, total - start)) for start in range(0, total, step)]


def dots(y, x):
    return lax.dot_general(y, x, (((1,), (1,)), ((), ())), preferred_element_type=jnp.float32)


def across(values, count):
    return jnp.concatenate([values] * count, axis=1)


def each_pair(xs, block, dots_ref, fill, visit):
    rows = xs[0].shape[0]
    pair = 2 if rows // block % 2 == 0 else 1
    for place, x_ref in enumerate(xs):

        def step(index, carry, place=place, x_ref=x_ref):
            firsts = [(index * pair + k) * block for k in range(pair)]
            for k, first in enumerate(firsts):
                fill(dots_ref.at[k], x_ref[pl.ds(pl.multiple_of(first, block), block), :])
            for k, first in enumerate(firsts):
                visit(dots_ref.at[k], (place * rows + first) // LANES)
            return carry

        lax.fori_loop(0, rows // block // pair, step, 0)


def eight(values, op):
    groups = values.reshape(values.shape[0] // 8, 8, values.shape[1])
    return op(groups, axis=0)


def fold(values, op):
    out = values[:, :LANES]
    for start in range(LANES, values.shape[1], LANES):
        out = op(out, values[:, start : start + LANES])
    return out


def row_kernel(*refs, count, share, block, tall, merge):
    xs, refs = refs[:count], refs[count:]
    *parts, l_ref, y_ref, b_ref, t_ref = refs
    before = parts.pop() if merge else None
    unpack(parts, share, y_ref, b_ref)
    cols, width = y_ref.shape
    alpha = 2.0 * SCALE / width
    repeat = block // LANES

    def fill(slot, x):
        slot[...] = dots(y_ref[...], x)

    def visit(slot, place):
        top = None
        for start, size in spans(cols, tall):
            here = slice(start, start + size)
            t = alpha * slot[here, :] + across(b_ref[here, :], repeat)
            slot[here, :] = t
            part = eight(t, jnp.max)
            top = part if top is None else jnp.maximum(top, part)
        top = jnp.max(top, axis=0, keepdims=True)
        total = None
        for start, size in spans(cols, tall):
            part = eight(jnp.exp2(slot[start : start + size, :] - top), jnp.sum)
            total = part if total is None else total + part
        log_sum = top + jnp.log2(jnp.sum(total, axis=0, keepdims=True))
        for k in range(repeat):
            l_ref[pl.ds(place + k, 1), :] = log_sum[:, k * LANES : (k + 1) * LANES]

    each_pair(xs, block, t_ref, fill, visit)
    if merge:
        l_ref[...] = merged([before[...], l_ref[...]])


def merged(pieces):
    top = functools.reduce(jnp.maximum, pieces)
    return top + jnp.log2(sum(jnp.exp2(piece - top) for piece in pieces))


def column_kernel(*refs, count, share, block, tall, orders, masks, log_cols):
    xs, refs = refs[:count], refs[count:]
    logs, refs = refs[: len(orders)], refs[len(orders) :]
    sq_ref, g_ref, *data, f_ref, own_g_ref, col_ref, l_ref, sum_ref, top_ref, t_ref = refs
    ys, biases = data[::2], data[1::2]
    rows, width = xs[0].shape
    alpha = 2.0 * SCALE / width
    repeat = block // LANES
    tiles = rows // LANES
    for k in range(count):
        pieces = [log[order[k] * tiles : (order[k] + 1) * tiles, :] for log, order in zip(logs, orders)]
        l_ref[k * tiles : (k + 1) * tiles, :] = merged(pieces)
    own_g_ref[...] = g_ref[...]
    f_ref[...] = sq_ref[...] / width - (EPS * LN2) * l_ref[:tiles, :] + EPS * log_cols

    def fill(slot, x):
        offset = 0
        for y_ref in ys:
            cols = y_ref.shape[0]
            slot[offset : offset + cols, :] = dots(y_ref[...], x)
            offset += cols

    def each(lift, visit):
        def visit_all(slot, place):
            log_here = jnp.concatenate([l_ref[pl.ds(place + k, 1), :] for k in range(repeat)], axis=1) - lift
            offset = 0
            for b_ref in biases:
                for start, size in spans(b_ref.shape[0], tall):
                    here = slice(offset + start, offset + start + size)
                    bias = across(b_ref[start : start + size, :], repeat)
                    visit(here, alpha * slot[here, :] + bias - log_here)
                offset += b_ref.shape[0]

        each_pair(xs, block, t_ref, fill, visit_all)

    def add(here, values):
        sum_ref[here, :] += fold(jnp.exp2(values), jnp.add)

    def raise_top(here, values):
        top_ref[here, :] = jnp.maximum(top_ref[here, :], fold(values, jnp.maximum))

    def add_from_top(here, values):
        sum_ref[here, :] += fold(jnp.exp2(values - across(top_ref[here, :], repeat)), jnp.add)

    sum_ref[...] = jnp.zeros(sum_ref.shape, jnp.float32)
    each(LIFT, add)
    least = jnp.min(jnp.sum(sum_ref[...], axis=1, keepdims=True))
    top_ref[...] = jnp.full(top_ref.shape, -LIFT, jnp.float32)

    @pl.when(jnp.logical_not(least >= FLOOR))
    def _():
        top_ref[...] = jnp.full(top_ref.shape, -jnp.inf, jnp.float32)
        each(0.0, raise_top)
        top = jnp.max(top_ref[...], axis=1, keepdims=True)
        top_ref[...] = jnp.broadcast_to(top, top_ref.shape)
        sum_ref[...] = jnp.zeros(sum_ref.shape, jnp.float32)
        each(0.0, add_from_top)

    gen, core = lax.axis_index("gen"), lax.rem(lax.axis_index("dat"), 2)
    n_gen = lax.axis_size("gen")
    for k, mask in enumerate(masks):
        here = slice(k * share, (k + 1) * share)
        total = jnp.sum(sum_ref[here, :].T, axis=0, keepdims=True)
        place = ((core ^ mask[1]) * n_gen) + (gen ^ mask[0])
        col_ref[pl.ds(place, 1), :] = top_ref[here, :].T[0:1, :] + jnp.log2(total)


def per_device(gen_samples, data_samples, data_potential):
    rows, width = gen_samples.shape
    n_gen, n_dat = lax.axis_size("gen"), lax.axis_size("dat")
    share = data_samples.shape[0]
    half = share * n_gen
    cols = 2 * half
    tiles = rows // LANES
    span = round_up(share, TILE) + TILE
    own_g = data_potential.reshape(1, share)
    params = pltpu.CompilerParams(vmem_limit_bytes=VMEM_LIMIT)
    message, column = pl.pallas_call(
        pack_kernel,
        out_shape=(
            jax.ShapeDtypeStruct((span, width), jnp.bfloat16),
            jax.ShapeDtypeStruct((span * (n_gen // 2), width), jnp.bfloat16),
        ),
    )(data_samples, own_g)
    gens, parts = gather(gen_samples, message, column)
    sq = pl.pallas_call(norm_kernel, out_shape=jax.ShapeDtypeStruct((tiles, LANES), jnp.float32))(gen_samples)
    order = [owners[0] for _, owners in gens]
    masks = [m for _, owners in parts for m in owners]
    xs = [array for array, _ in gens]
    parts = [array for array, _ in parts]
    block = min(256, rows)
    tall = 64
    pair = 2 if rows // block % 2 == 0 else 1

    def cost(count):
        return pl.CostEstimate(
            flops=2 * rows * len(xs) * count * width,
            bytes_accessed=2 * (rows * len(xs) + count) * width,
            transcendentals=rows * len(xs) * count,
        )

    logs = []
    data = []
    for some in (parts[:3], parts[3:]):
        count = len(some) * half // 2
        log, y, bias = pl.pallas_call(
            functools.partial(
                row_kernel, count=len(xs), share=share, block=block, tall=tall, merge=bool(logs)
            ),
            out_shape=(
                jax.ShapeDtypeStruct((len(xs) * tiles, LANES), jnp.float32),
                jax.ShapeDtypeStruct((count, width), jnp.bfloat16),
                jax.ShapeDtypeStruct((count, LANES), jnp.float32),
            ),
            scratch_shapes=[pltpu.VMEM((pair, count, block), jnp.float32)],
            compiler_params=params,
            cost_estimate=cost(count),
        )(*xs, *some, *logs)
        logs = [log]
        data += [y, bias]
    logs += [swap(logs[0], "dat", m) for m in order[1:]]
    orders = [[order.index(m ^ partner) for m in order] for partner in order]
    f, own_g, col = pl.pallas_call(
        functools.partial(
            column_kernel,
            count=len(xs),
            share=share,
            block=block,
            tall=tall,
            orders=orders,
            masks=masks,
            log_cols=math.log(half * n_dat),
        ),
        out_shape=(
            jax.ShapeDtypeStruct((tiles, LANES), jnp.float32),
            jax.ShapeDtypeStruct((1, share), jnp.float32),
            jax.ShapeDtypeStruct((2 * n_gen, share), jnp.float32),
        ),
        scratch_shapes=[
            pltpu.VMEM((len(xs) * tiles, LANES), jnp.float32),
            pltpu.VMEM((cols, LANES), jnp.float32),
            pltpu.VMEM((cols, LANES), jnp.float32),
            pltpu.VMEM((pair, cols, block), jnp.float32),
        ],
        compiler_params=params,
        cost_estimate=cost(cols),
    )(*xs, *logs, sq, own_g, *data)
    groups = [list(range(start, start + 2 * n_gen)) for start in range(0, n_gen * n_dat, 2 * n_gen)]
    totals = lax.all_to_all(col, ("dat", "gen"), 0, 0, axis_index_groups=groups, tiled=True)
    top = jnp.max(totals, axis=0)
    total = top + jnp.log2(jnp.sum(jnp.exp2(totals - top[None, :]), axis=0))
    new_data = own_g[0] - (EPS * LN2) * total + EPS * math.log(rows * n_gen / half)
    return f.reshape(rows), new_data


def solution(mesh):
    in_specs = (P(("gen", "dat"), None), P(("dat", "gen"), None), P(("dat", "gen")))
    out_specs = (P(("gen", "dat")), P(("dat", "gen")))
    return jax.shard_map(per_device, mesh=mesh, in_specs=in_specs, out_specs=out_specs, check_vma=False)
```

time: 68 us -> 57.6 us (0.85)
  Pallas kernels: 32.9 us -> 20.7 us
  local copies, waits for them, and re-layouts: 1.33 us -> 4.52 us
  blocking collectives: 9.47 us -> 12.1 us
  waiting for transfers between devices: 10.9 us -> 8.3 us
  other arithmetic: 1.41 us -> 0.59 us
    pallas_call x4, Pallas kernels: 30.9 us -> 18.6 us  [the longest x1 11.4 us: per_device(): pl.pallas_call(functools.partial(column_kernel, count=len(xs), share=shar...]
    ppermute x10 -> x8, waiting for transfers between devices: 10.9 us -> 8.3 us  [swap(): lax.ppermute(value, axis, [(k, k ^ mask) for k in range(lax.axis_size(axi...]
    all_to_all x1, blocking collectives: 9.47 us -> 12.1 us  [per_device(): lax.all_to_all(col, ('dat', 'gen'), 0, 0, axis_index_groups=groups, tiled...]
    dynamic_update_slice x0 -> x3, local copies, waits for them, and re-layouts: none -> 1.87 us  [gather(): lax.dynamic_update_slice(column, swap(message, 'gen', mask), ((k + 1) * s...]
    unnamed x8 -> x12, local copies, waits for them, and re-layouts: 1.33 us -> 2.64 us
    concatenate x2 -> x0, other arithmetic: 0.84 us -> none  [the longest x1 0.83 us: join(): whole = arrays[0] if len(arrays) == 1 else jnp.concatenate(arrays, axis=0)]
    ppermute x10 -> x8, starting transfers between devices: 11 us -> 10.4 us  [swap(): lax.ppermute(value, axis, [(k, k ^ mask) for k in range(lax.axis_size(axi...]
  transfers between devices with their start and end apart: 10 -> 8, of which waited for: 4 -> 5; matrix products, arithmetic and copies ran while one was open for 1% -> 3% of each run, Pallas kernels for 15% -> 10%
where the time goes in v6:
time: 57.6 us; the launch traced here: 57.2 us
  Pallas kernels  20.7 us (36%)
  blocking collectives  12.1 us (21%)
  starting transfers between devices  10.4 us (18%)
  waiting for transfers between devices  8.3 us (14%)
  local copies, waits for them, and re-layouts  4.52 us (8%)
  between operations  0.68 us (1%)
  other arithmetic  0.59 us (1%)
    all_to_all x1, blocking collectives, per_device(): lax.all_to_all(col, ('dat', 'gen'), 0, 0, axis_index_groups=groups, tiled...  12.1 us
    pallas_call x1, Pallas kernels, per_device(): pl.pallas_call(functools.partial(column_kernel, count=len(xs), share=shar...  11.4 us
    ppermute x8, starting transfers between devices, swap(): lax.ppermute(value, axis, [(k, k ^ mask) for k in range(lax.axis_size(axi...  10.4 us
    ppermute x8, waiting for transfers between devices, swap(): lax.ppermute(value, axis, [(k, k ^ mask) for k in range(lax.axis_size(axi...  8.3 us
    pallas_call x2, Pallas kernels, per_device(): pl.pallas_call(functools.partial(row_kernel, count=len(xs), share=share,...  5.53 us
    unnamed x12, local copies, waits for them, and re-layouts  2.64 us
    pallas_call x1, Pallas kernels, per_device(): pl.pallas_call(norm_kernel, out_shape=jax.ShapeDtypeStruct((tiles, LANES)...  2.06 us
    dynamic_update_slice x3, local copies, waits for them, and re-layouts, gather(): lax.dynamic_update_slice(column, swap(message, 'gen', mask), ((k + 1) * s...  1.87 us
  transfers between devices with their start and end apart: 8, of which 5 were waited for; matrix products, arithmetic and copies ran while one was open for 3% of the time, Pallas kernels for 10%

profile of v6, /device:TPU:0, one launch (start us, length us, event | category | flops | bytes accessed | tf_op | source)
XLA Modules:
  0.0 57.2 jit_solution(9625957988470530241)
XLA Ops:
  0.6 1.7 %shard_map.50 = (bf16[112,256]{1,0:T(8,128)(2,1)}, bf16[448,256]{1,0:T(8,128)(2,1)}) custom-call(bf16[96,256]{1,0:T(8,128)(2,1)} %y_ref.1, f32[1,96]{1,0:T(1,128)} %bitcast.11), custom_call_target="tpu_custom_call" | custom-call | tf_op jit(solution)/shard_map/pallas_call | solution.py:261
  2.3 3.0 %collective-permute-start.1 = (bf16[112,256]{1,0:T(8,128)(2,1)}, bf16[112,256]{1,0:T(8,128)(2,1)S(1)}, u32[]{:S(2)}, u32[]{:S(2)}) collective-permute-start(bf16[112,256]{1,0:T(8,128)(2,1)} %get-tuple-element.14), channel_id=1, source_target_pairs={{0,8},{4,12},{8,0},{12,4},{16,24},{20,28},{24,16},{28,20},{1,9},{5... | collective-permute-start | bytes 172040 | tf_op jit(solution)/shard_map/ppermute | solution.py:27
  5.4 2.6 %collective-permute-start.2 = (bf16[112,256]{1,0:T(8,128)(2,1)}, bf16[112,256]{1,0:T(8,128)(2,1)S(1)}, u32[]{:S(2)}, u32[]{:S(2)}) collective-permute-start(bf16[112,256]{1,0:T(8,128)(2,1)} %get-tuple-element.14), channel_id=1, source_target_pairs={{0,16},{4,20},{8,24},{12,28},{16,0},{20,4},{24,8},{28,12},{1,17},{... | collective-permute-start | bytes 172040 | tf_op jit(solution)/shard_map/ppermute | solution.py:27
  7.9 0.0 collective-permute-start.3
  8.0 1.7 %collective-permute-start = (bf16[1024,256]{1,0:T(8,128)(2,1)}, bf16[1024,256]{1,0:T(8,128)(2,1)S(1)}, u32[]{:S(2)}, u32[]{:S(2)}) collective-permute-start(bf16[1024,256]{1,0:T(8,128)(2,1)} %refs_0_.5), channel_id=1, source_target_pairs={{0,2},{1,3},{2,0},{3,1},{4,6},{5,7},{6,4},{7,5},{8,10},{9,11},{10,... | collective-permute-start | bytes 1572872 | tf_op jit(solution)/shard_map/ppermute | solution.py:27
  9.7 0.0 collective-permute-done.1
  9.7 0.6 %constant_dynamic-update-slice_fusion.2 = bf16[448,256]{1,0:T(8,128)(2,1)} fusion(bf16[448,256]{1,0:T(8,128)(2,1)} %get-tuple-element.13, bf16[112,256]{1,0:T(8,128)(2,1)S(1)} %collective-permute-done.1), kind=kLoop, calls=%fused_computation.3 | loop fusion | bytes 114688 | tf_op jit(solution)/shard_map/dynamic_update_slice | solution.py:40
  10.3 1.5 %collective-permute-done.2 = bf16[112,256]{1,0:T(8,128)(2,1)S(1)} collective-permute-done((bf16[112,256]{1,0:T(8,128)(2,1)}, bf16[112,256]{1,0:T(8,128)(2,1)S(1)}, u32[]{:S(2)}, u32[]{:S(2)}) %collective-permute-start.2) | collective-permute-done | bytes 57376 | tf_op jit(solution)/shard_map/ppermute | solution.py:27
  11.8 0.6 %constant_dynamic-update-slice_fusion.1 = bf16[448,256]{1,0:T(8,128)(2,1)} fusion(bf16[448,256]{1,0:T(8,128)(2,1)} %constant_dynamic-update-slice_fusion.2, bf16[112,256]{1,0:T(8,128)(2,1)S(1)} %collective-permute-done.2), kind=kLoop, calls=%fused_computation.2 | loop fusion | bytes 114688 | tf_op jit(solution)/shard_map/dynamic_update_slice | solution.py:40
  12.4 1.7 %collective-permute-done.3 = bf16[112,256]{1,0:T(8,128)(2,1)S(1)} collective-permute-done((bf16[112,256]{1,0:T(8,128)(2,1)}, bf16[112,256]{1,0:T(8,128)(2,1)S(1)}, u32[]{:S(2)}, u32[]{:S(2)}) %collective-permute-start.3) | collective-permute-done | bytes 57376 | tf_op jit(solution)/shard_map/ppermute | solution.py:27
  14.1 0.6 %constant_dynamic-update-slice_fusion.refs_2_ = bf16[448,256]{1,0:T(8,128)(2,1)} fusion(bf16[448,256]{1,0:T(8,128)(2,1)} %constant_dynamic-update-slice_fusion.1, bf16[112,256]{1,0:T(8,128)(2,1)S(1)} %collective-permute-done.3), kind=kLoop, calls=%fused_computation.1 | loop fusion | bytes 114688 | tf_op jit(solution)/shard_map/dynamic_update_slice | solution.py:40
  14.8 1.5 %collective-permute-start.4 = (bf16[448,256]{1,0:T(8,128)(2,1)}, bf16[448,256]{1,0:T(8,128)(2,1)S(1)}, u32[]{:S(2)}, u32[]{:S(2)}) collective-permute-start(bf16[448,256]{1,0:T(8,128)(2,1)} %constant_dynamic-update-slice_fusion.refs_2_), channel_id=1, source_target_pairs={{0,4},{4,0},{8,12},{12,8},{16,20},{20,16},{24,28},{28,24},{1,5},{5... | collective-permute-start | bytes 688136 | tf_op jit(solution)/shard_map/ppermute | solution.py:27
  16.3 0.0 collective-permute-start.6
  16.3 4.7 %collective-permute-done.4.refs_3_ = bf16[448,256]{1,0:T(8,128)(2,1)S(1)} collective-permute-done((bf16[448,256]{1,0:T(8,128)(2,1)}, bf16[448,256]{1,0:T(8,128)(2,1)S(1)}, u32[]{:S(2)}, u32[]{:S(2)}) %collective-permute-start.4) | collective-permute-done | bytes 229408 | tf_op jit(solution)/shard_map/ppermute | solution.py:27
  21.0 0.0 collective-permute-start.5
  21.0 0.0 collective-permute-done.6.refs_4_
  21.0 0.3 collective-permute-done.refs_1_
  21.3 0.0 copy-start
  21.3 1.0 %copy-done = bf16[1024,256]{1,0:T(8,128)(2,1)S(1)} copy-done((bf16[1024,256]{1,0:T(8,128)(2,1)S(1)}, bf16[1024,256]{1,0:T(8,128)(2,1)}, u32[]{:S(2)}) %copy-start) | copy-done | bytes 524312
  22.3 0.0 copy-start.5
  22.3 0.9 %copy-done.5 = bf16[448,256]{1,0:T(8,128)(2,1)S(1)} copy-done((bf16[448,256]{1,0:T(8,128)(2,1)S(1)}, bf16[448,256]{1,0:T(8,128)(2,1)}, u32[]{:S(2)}) %copy-start.5) | copy-done | bytes 229400
  23.2 0.0 copy-start.1
  23.2 3.7 %shard_map.51 = (f32[16,128]{1,0:T(8,128)S(1)}, bf16[1152,256]{1,0:T(8,128)(2,1)S(1)}, f32[1152,128]{1,0:T(8,128)S(1)}) custom-call(bf16[1024,256]{1,0:T(8,128)(2,1)S(1)} %copy-done, bf16[1024,256]{1,0:T(8,128)(2,1)S(1)} %collective-permute-done.refs_1_, bf16[448,256]{1,0:T(8,128)(2,1)S(1)} %copy-done.5, ...), custom_call_target="tpu_custom_call" | custom-call | flops 1207959552 | bytes 1638400 | tf_op jit(solution)/shard_map/pallas_call | solution.py:289
  26.9 0.0 collective-permute-done.5.refs_2_
  26.9 0.0 copy-done.1
  26.9 1.9 %shard_map.52 = (f32[16,128]{1,0:T(8,128)S(1)}, bf16[384,256]{1,0:T(8,128)(2,1)S(1)}, f32[384,128]{1,0:T(8,128)S(1)}) custom-call(bf16[1024,256]{1,0:T(8,128)(2,1)S(1)} %copy-done.1, bf16[1024,256]{1,0:T(8,128)(2,1)S(1)} %collective-permute-done.refs_1_, bf16[448,256]{1,0:T(8,128)(2,1)S(1)} %collective-permute-done.5.refs_2_, ...), custom_call_target="tpu_custom_call" | custom-call | flops 402653184 | bytes 1245184 | tf_op jit(solution)/shard_map/pallas_call | solution.py:289
  28.8 0.0 copy-start.2
  28.8 1.6 %collective-permute-start.7 = (f32[16,128]{1,0:T(8,128)S(1)}, f32[16,128]{1,0:T(8,128)S(1)}, u32[]{:S(2)}, u32[]{:S(2)}) collective-permute-start(f32[16,128]{1,0:T(8,128)S(1)} %get-tuple-element.16.refs_2_), channel_id=1, source_target_pairs={{0,2},{1,3},{2,0},{3,1},{4,6},{5,7},{6,4},{7,5},{8,10},{9,11},{10,... | collective-permute-start | bytes 24584 | tf_op jit(solution)/shard_map/ppermute | solution.py:27
  30.4 2.1 %shard_map.53.refs_4_ = f32[8,128]{1,0:T(8,128)} custom-call(bf16[1024,256]{1,0:T(8,128)(2,1)} %refs_0_.5), custom_call_target="tpu_custom_call" | custom-call | tf_op jit(solution)/shard_map/pallas_call | solution.py:269
  32.4 0.0 copy-start.3
  32.4 0.1 collective-permute-done.7.refs_3_
  32.5 0.0 copy-start.4
  32.5 0.0 copy-done.2
  32.5 0.6 %copy-done.3 = f32[8,128]{1,0:T(8,128)S(1)} copy-done((f32[8,128]{1,0:T(8,128)S(1)}, f32[8,128]{1,0:T(8,128)}, u32[]{:S(2)}) %copy-start.3) | copy-done | bytes 4120
  33.1 0.1 copy-done.4
  33.2 11.4 %shard_map.54 = (f32[8,128]{1,0:T(8,128)}, f32[1,96]{1,0:T(1,128)S(1)}, f32[16,96]{1,0:T(8,128)S(1)}) custom-call(bf16[1024,256]{1,0:T(8,128)(2,1)S(1)} %copy-done.2, bf16[1024,256]{1,0:T(8,128)(2,1)S(1)} %collective-permute-done.refs_1_, f32[16,128]{1,0:T(8,128)S(1)} %get-tuple-element.16.refs_2_, f32[16,128]{1,0:T(8,128)S(1)} %collective-permute-done.7.refs_3_, ...), custom_call_target="tpu_custom_call" | custom-call | flops 1610612736 | bytes 1835008 | tf_op jit(solution)/shard_map/pallas_call | solution.py:306
  44.6 12.1 %all_to_all.12 = f32[16,1,96]{2,1,0:T(1,128)S(1)} all-to-all(f32[16,1,96]{2,1,0:T(1,128)S(1)} %bitcast.10), channel_id=1, replica_groups={{0,4,8,12,16,20,24,28,1,5,9,13,17,21,25,29},{2,6,10,14,18,22,26,30,3,7,..., dimensions={0} | all-to-all | bytes 12288 | tf_op jit(solution)/shard_map/all_to_all | solution.py:332
  56.7 0.5 fusion
  (2 shorter events, 0.1 us)
Async XLA Ops:
  2.3 7.3 %collective-permute-start.1 = (bf16[112,256]{1,0:T(8,128)(2,1)}, bf16[112,256]{1,0:T(8,128)(2,1)S(1)}, u32[]{:S(2)}, u32[]{:S(2)}) collective-permute-start(bf16[112,256]{1,0:T(8,128)(2,1)} %get-tuple-element.14), channel_id=1, source_target_pairs={{0,8},{4,12},{8,0},{12,4},{16,24},{20,28},{24,16},{28,20},{1,9},{5... | collective-permute-start | bytes 172040 | tf_op jit(solution)/shard_map/ppermute | solution.py:27
  5.4 6.4 %collective-permute-start.2 = (bf16[112,256]{1,0:T(8,128)(2,1)}, bf16[112,256]{1,0:T(8,128)(2,1)S(1)}, u32[]{:S(2)}, u32[]{:S(2)}) collective-permute-start(bf16[112,256]{1,0:T(8,128)(2,1)} %get-tuple-element.14), channel_id=1, source_target_pairs={{0,16},{4,20},{8,24},{12,28},{16,0},{20,4},{24,8},{28,12},{1,17},{... | collective-permute-start | bytes 172040 | tf_op jit(solution)/shard_map/ppermute | solution.py:27
  7.9 6.2 %collective-permute-start.3 = (bf16[112,256]{1,0:T(8,128)(2,1)}, bf16[112,256]{1,0:T(8,128)(2,1)S(1)}, u32[]{:S(2)}, u32[]{:S(2)}) collective-permute-start(bf16[112,256]{1,0:T(8,128)(2,1)} %get-tuple-element.14), channel_id=1, source_target_pairs={{0,24},{4,28},{8,16},{12,20},{16,8},{20,12},{24,0},{28,4},{1,25},{... | collective-permute-start | bytes 172040 | tf_op jit(solution)/shard_map/ppermute | solution.py:27
  8.0 13.3 %collective-permute-start = (bf16[1024,256]{1,0:T(8,128)(2,1)}, bf16[1024,256]{1,0:T(8,128)(2,1)S(1)}, u32[]{:S(2)}, u32[]{:S(2)}) collective-permute-start(bf16[1024,256]{1,0:T(8,128)(2,1)} %refs_0_.5), channel_id=1, source_target_pairs={{0,2},{1,3},{2,0},{3,1},{4,6},{5,7},{6,4},{7,5},{8,10},{9,11},{10,... | collective-permute-start | bytes 1572872 | tf_op jit(solution)/shard_map/ppermute | solution.py:27
  14.8 6.2 %collective-permute-start.4 = (bf16[448,256]{1,0:T(8,128)(2,1)}, bf16[448,256]{1,0:T(8,128)(2,1)S(1)}, u32[]{:S(2)}, u32[]{:S(2)}) collective-permute-start(bf16[448,256]{1,0:T(8,128)(2,1)} %constant_dynamic-update-slice_fusion.refs_2_), channel_id=1, source_target_pairs={{0,4},{4,0},{8,12},{12,8},{16,20},{20,16},{24,28},{28,24},{1,5},{5... | collective-permute-start | bytes 688136 | tf_op jit(solution)/shard_map/ppermute | solution.py:27
  16.3 4.7 %collective-permute-start.6 = (bf16[448,256]{1,0:T(8,128)(2,1)}, bf16[448,256]{1,0:T(8,128)(2,1)S(1)}, u32[]{:S(2)}, u32[]{:S(2)}) collective-permute-start(bf16[448,256]{1,0:T(8,128)(2,1)} %constant_dynamic-update-slice_fusion.refs_2_), channel_id=1, source_target_pairs={{0,1},{1,0},{2,3},{3,2},{4,5},{5,4},{6,7},{7,6},{8,9},{9,8},{10,11... | collective-permute-start | bytes 688136 | tf_op jit(solution)/shard_map/ppermute | solution.py:27
  21.0 5.9 %collective-permute-start.5 = (bf16[448,256]{1,0:T(8,128)(2,1)S(1)}, bf16[448,256]{1,0:T(8,128)(2,1)S(1)}, u32[]{:S(2)}, u32[]{:S(2)}) collective-permute-start(bf16[448,256]{1,0:T(8,128)(2,1)S(1)} %collective-permute-done.4.refs_3_), channel_id=1, source_target_pairs={{0,1},{1,0},{2,3},{3,2},{4,5},{5,4},{6,7},{7,6},{8,9},{9,8},{10,11... | collective-permute-start | bytes 688136 | tf_op jit(solution)/shard_map/ppermute | solution.py:27
  21.3 1.0 %copy-start = (bf16[1024,256]{1,0:T(8,128)(2,1)S(1)}, bf16[1024,256]{1,0:T(8,128)(2,1)}, u32[]{:S(2)}) copy-start(bf16[1024,256]{1,0:T(8,128)(2,1)} %refs_0_.5) | copy-start | bytes 1572868
  22.3 0.9 %copy-start.5 = (bf16[448,256]{1,0:T(8,128)(2,1)S(1)}, bf16[448,256]{1,0:T(8,128)(2,1)}, u32[]{:S(2)}) copy-start(bf16[448,256]{1,0:T(8,128)(2,1)} %constant_dynamic-update-slice_fusion.refs_2_) | copy-start | bytes 688132
  23.2 3.7 %copy-start.1 = (bf16[1024,256]{1,0:T(8,128)(2,1)S(1)}, bf16[1024,256]{1,0:T(8,128)(2,1)}, u32[]{:S(2)}) copy-start(bf16[1024,256]{1,0:T(8,128)(2,1)} %refs_0_.5) | copy-start | bytes 1572868
  28.8 3.7 %copy-start.2 = (bf16[1024,256]{1,0:T(8,128)(2,1)S(1)}, bf16[1024,256]{1,0:T(8,128)(2,1)}, u32[]{:S(2)}) copy-start(bf16[1024,256]{1,0:T(8,128)(2,1)} %refs_0_.5) | copy-start | bytes 1572868
  28.8 3.7 %collective-permute-start.7 = (f32[16,128]{1,0:T(8,128)S(1)}, f32[16,128]{1,0:T(8,128)S(1)}, u32[]{:S(2)}, u32[]{:S(2)}) collective-permute-start(f32[16,128]{1,0:T(8,128)S(1)} %get-tuple-element.16.refs_2_), channel_id=1, source_target_pairs={{0,2},{1,3},{2,0},{3,1},{4,6},{5,7},{6,4},{7,5},{8,10},{9,11},{10,... | collective-permute-start | bytes 24584 | tf_op jit(solution)/shard_map/ppermute | solution.py:27
  32.4 0.7 %copy-start.3 = (f32[8,128]{1,0:T(8,128)S(1)}, f32[8,128]{1,0:T(8,128)}, u32[]{:S(2)}) copy-start(f32[8,128]{1,0:T(8,128)} %shard_map.53.refs_4_) | copy-start | bytes 12292
  32.5 0.7 %copy-start.4 = (f32[96]{0:T(128)S(1)}, f32[96]{0:T(128)}, u32[]{:S(2)}) copy-start(f32[96]{0:T(128)} %param.5) | copy-start | bytes 1156

commit v7 on v6

--- a/solution.py
+++ b/solution.py
@@ -16,7 +16,8 @@
 TILE = 16
 LIFT = 100.0
 FLOOR = 2.0**-90
-VMEM_LIMIT = 40 * 1024 * 1024
+MIB = 1024 * 1024
+NOTHING = -1e30
 
 
 def round_up(value, step):
@@ -27,21 +28,21 @@
     return lax.ppermute(value, axis, [(k, k ^ mask) for k in range(lax.axis_size(axis))])
 
 
-def gather(gen_own, message, column):
-    n_dat, n_gen = lax.axis_size("dat"), lax.axis_size("gen")
-    gens = [(gen_own, [0])]
-    bit = n_dat // 2
+def gather_gen(gen_own):
+    gens = [(gen_own, 0)]
+    bit = lax.axis_size("dat") // 2
     while bit > 1:
-        gens += [(swap(array, "dat", bit), [m ^ bit for m in masks]) for array, masks in gens]
+        gens += [(swap(array, "dat", bit), mask ^ bit) for array, mask in gens]
         bit //= 2
+    return [array for array, _ in gens], [mask for _, mask in gens]
+
+
+def gather_column(message, column):
     span = message.shape[0]
-    far = range(2, n_gen, 2)
+    far = range(2, lax.axis_size("gen"), 2)
     for k, mask in enumerate(far):
         column = lax.dynamic_update_slice(column, swap(message, "gen", mask), ((k + 1) * span, 0))
-    masks = [(m, 0) for m in [0, *far]]
-    near = swap(column, "gen", 1), [(g ^ 1, d) for g, d in masks]
-    parts = [(column, masks), near]
-    return gens, parts + [(swap(array, "dat", 1), [(g, 1) for g, _ in masks]) for array, masks in parts]
+    return column, [0, *far]
 
 
 def pack_kernel(y_ref, g_ref, packed_ref, column_ref):
@@ -89,7 +90,8 @@
             k += 1
 
 
-def norm_kernel(x_ref, sq_ref):
+def norm_kernel(x_ref, sq_ref, copy_ref):
+    copy_ref[...] = x_ref[...]
     x = x_ref[...].astype(jnp.float32)
     square = x * x
     high = square.astype(jnp.bfloat16)
@@ -239,12 +241,13 @@
         sum_ref[...] = jnp.zeros(sum_ref.shape, jnp.float32)
         each(0.0, add_from_top)
 
-    gen, core = lax.axis_index("gen"), lax.rem(lax.axis_index("dat"), 2)
+    gen, dat = lax.axis_index("gen"), lax.axis_index("dat")
     n_gen = lax.axis_size("gen")
+    col_ref[...] = jnp.full(col_ref.shape, NOTHING, jnp.float32)
     for k, mask in enumerate(masks):
         here = slice(k * share, (k + 1) * share)
         total = jnp.sum(sum_ref[here, :].T, axis=0, keepdims=True)
-        place = ((core ^ mask[1]) * n_gen) + (gen ^ mask[0])
+        place = (dat ^ mask[1]) * n_gen + (gen ^ mask[0])
         col_ref[pl.ds(place, 1), :] = top_ref[here, :].T[0:1, :] + jnp.log2(total)
 
 
@@ -257,20 +260,24 @@
     tiles = rows // LANES
     span = round_up(share, TILE) + TILE
     own_g = data_potential.reshape(1, share)
-    params = pltpu.CompilerParams(vmem_limit_bytes=VMEM_LIMIT)
     message, column = pl.pallas_call(
         pack_kernel,
         out_shape=(
             jax.ShapeDtypeStruct((span, width), jnp.bfloat16),
             jax.ShapeDtypeStruct((span * (n_gen // 2), width), jnp.bfloat16),
         ),
+        compiler_params=pltpu.CompilerParams(vmem_limit_bytes=4 * MIB),
     )(data_samples, own_g)
-    gens, parts = gather(gen_samples, message, column)
-    sq = pl.pallas_call(norm_kernel, out_shape=jax.ShapeDtypeStruct((tiles, LANES), jnp.float32))(gen_samples)
-    order = [owners[0] for _, owners in gens]
-    masks = [m for _, owners in parts for m in owners]
-    xs = [array for array, _ in gens]
-    parts = [array for array, _ in parts]
+    xs, order = gather_gen(gen_samples)
+    column, far = gather_column(message, column)
+    sq, xs[0] = pl.pallas_call(
+        norm_kernel,
+        out_shape=(
+            jax.ShapeDtypeStruct((tiles, LANES), jnp.float32),
+            jax.ShapeDtypeStruct(gen_samples.shape, gen_samples.dtype),
+        ),
+        compiler_params=pltpu.CompilerParams(vmem_limit_bytes=8 * MIB),
+    )(gen_samples)
     block = min(256, rows)
     tall = 64
     pair = 2 if rows // block % 2 == 0 else 1
@@ -282,13 +289,11 @@
             transcendentals=rows * len(xs) * count,
         )
 
-    logs = []
-    data = []
-    for some in (parts[:3], parts[3:]):
-        count = len(some) * half // 2
-        log, y, bias = pl.pallas_call(
+    def row_pass(parts, before):
+        count = len(parts) * half // 2
+        return pl.pallas_call(
             functools.partial(
-                row_kernel, count=len(xs), share=share, block=block, tall=tall, merge=bool(logs)
+                row_kernel, count=len(xs), share=share, block=block, tall=tall, merge=bool(before)
             ),
             out_shape=(
                 jax.ShapeDtypeStruct((len(xs) * tiles, LANES), jnp.float32),
@@ -296,11 +301,22 @@
                 jax.ShapeDtypeStruct((count, LANES), jnp.float32),
             ),
             scratch_shapes=[pltpu.VMEM((pair, count, block), jnp.float32)],
-            compiler_params=params,
+            compiler_params=pltpu.CompilerParams(vmem_limit_bytes=12 * MIB),
             cost_estimate=cost(count),
-        )(*xs, *some, *logs)
-        logs = [log]
-        data += [y, bias]
+        )(*xs, *parts, *before)
+
+    near = swap(column, "gen", 1)
+    twin = swap(column, "dat", 1)
+    log, *data = row_pass([column, twin], [])
+    near, log = lax.optimization_barrier((near, log))
+    near_twin = swap(near, "dat", 1)
+    log, *more = row_pass([near], [log])
+    data += more
+    near_twin, log = lax.optimization_barrier((near_twin, log))
+    log, *more = row_pass([near_twin], [log])
+    data += more
+    masks = [(g ^ a, b) for a in (0, 1) for b in (0, 1) for g in far]
+    logs = [log]
     logs += [swap(logs[0], "dat", m) for m in order[1:]]
     orders = [[order.index(m ^ partner) for m in order] for partner in order]
     f, own_g, col = pl.pallas_call(
@@ -317,7 +333,7 @@
         out_shape=(
             jax.ShapeDtypeStruct((tiles, LANES), jnp.float32),
             jax.ShapeDtypeStruct((1, share), jnp.float32),
-            jax.ShapeDtypeStruct((2 * n_gen, share), jnp.float32),
+            jax.ShapeDtypeStruct((n_dat * n_gen, share), jnp.float32),
         ),
         scratch_shapes=[
             pltpu.VMEM((len(xs) * tiles, LANES), jnp.float32),
@@ -325,11 +341,10 @@
             pltpu.VMEM((cols, LANES), jnp.float32),
             pltpu.VMEM((pair, cols, block), jnp.float32),
         ],
-        compiler_params=params,
+        compiler_params=pltpu.CompilerParams(vmem_limit_bytes=16 * MIB),
         cost_estimate=cost(cols),
     )(*xs, *logs, sq, own_g, *data)
-    groups = [list(range(start, start + 2 * n_gen)) for start in range(0, n_gen * n_dat, 2 * n_gen)]
-    totals = lax.all_to_all(col, ("dat", "gen"), 0, 0, axis_index_groups=groups, tiled=True)
+    totals = lax.all_to_all(col, ("dat", "gen"), 0, 0, tiled=True)
     top = jnp.max(totals, axis=0)
     total = top + jnp.log2(jnp.sum(jnp.exp2(totals - top[None, :]), axis=0))
     new_data = own_g[0] - (EPS * LN2) * total + EPS * math.log(rows * n_gen / half)

time: 57.6 us -> 55.5 us (0.964)
  waiting for transfers between devices: 8.3 us -> 10.8 us
  Pallas kernels: 20.7 us -> 18.3 us
  local copies, waits for them, and re-layouts: 4.52 us -> 2.5 us
    ppermute x8, waiting for transfers between devices: 8.3 us -> 10.8 us  [swap(): lax.ppermute(value, axis, [(k, k ^ mask) for k in range(lax.axis_size(axi...]
    dynamic_update_slice x3, local copies, waits for them, and re-layouts: 1.87 us -> 0.02 us  [gather_column(): lax.dynamic_update_slice(column, swap(message, 'gen', mask), ((k + 1) * s...]
    pallas_call x1, Pallas kernels: 1.7 us -> 0.15 us  [per_device(): pl.pallas_call(pack_kernel, out_shape=(jax.ShapeDtypeStruct((span, width)...]
    pallas_call x3 -> x4, Pallas kernels: 7.59 us -> 6.91 us  [the longest x3 6.5 us: row_pass(): pl.pallas_call(functools.partial(row_kernel, count=len(xs), share=share,...]
    unnamed x12 -> x6, local copies, waits for them, and re-layouts: 2.64 us -> 2.49 us
  transfers between devices with their start and end apart: 8 -> 8, of which waited for: 5 -> 3; matrix products, arithmetic and copies ran while one was open for 3% -> 0% of each run, Pallas kernels for 10% -> 9%
where the time goes in v7:
time: 55.5 us; the launch traced here: 55.2 us
  Pallas kernels  18.3 us (33%)
  blocking collectives  11.8 us (21%)
  waiting for transfers between devices  10.8 us (19%)
  starting transfers between devices  10.5 us (19%)
  local copies, waits for them, and re-layouts  2.5 us (5%)
  between operations  0.71 us (1%)
  other arithmetic  0.61 us (1%)
    all_to_all x1, blocking collectives, per_device(): totals = lax.all_to_all(col, ('dat', 'gen'), 0, 0, tiled=True)  11.8 us
    pallas_call x1, Pallas kernels, per_device(): pl.pallas_call(functools.partial(column_kernel, count=len(xs), share=shar...  11.2 us
    ppermute x8, waiting for transfers between devices, swap(): lax.ppermute(value, axis, [(k, k ^ mask) for k in range(lax.axis_size(axi...  10.8 us
    ppermute x8, starting transfers between devices, swap(): lax.ppermute(value, axis, [(k, k ^ mask) for k in range(lax.axis_size(axi...  10.5 us
    pallas_call x3, Pallas kernels, row_pass(): pl.pallas_call(functools.partial(row_kernel, count=len(xs), share=share,...  6.5 us
    unnamed x6, local copies, waits for them, and re-layouts  2.49 us
  transfers between devices with their start and end apart: 8, of which 3 were waited for; matrix products, arithmetic and copies ran while one was open for 0% of the time, Pallas kernels for 9%

profile of v7, /device:TPU:0, one launch (start us, length us, event | category | flops | bytes accessed | tf_op | source)
XLA Modules:
  0.0 55.2 jit_solution(11436513174244038289)
XLA Ops:
  0.6 0.0 copy-start.2
  0.6 0.6 %copy-done.2 = f32[96]{0:T(128)S(1)} copy-done((f32[96]{0:T(128)S(1)}, f32[96]{0:T(128)}, u32[]{:S(2)}) %copy-start.2) | copy-done | bytes 408
  1.3 0.0 copy-start.1
  1.3 0.8 %copy-done.1 = bf16[96,256]{1,0:T(8,128)(2,1)S(1)} copy-done((bf16[96,256]{1,0:T(8,128)(2,1)S(1)}, bf16[96,256]{1,0:T(8,128)(2,1)}, u32[]{:S(2)}) %copy-start.1) | copy-done | bytes 49176
  2.1 0.2 shard_map.51
  2.2 3.1 %collective-permute-start.1 = (bf16[112,256]{1,0:T(8,128)(2,1)S(1)}, bf16[112,256]{1,0:T(8,128)(2,1)S(1)}, u32[]{:S(2)}, u32[]{:S(2)}) collective-permute-start(bf16[112,256]{1,0:T(8,128)(2,1)S(1)} %get-tuple-element.24), channel_id=1, source_target_pairs={{0,8},{4,12},{8,0},{12,4},{16,24},{20,28},{24,16},{28,20},{1,9},{5... | collective-permute-start | bytes 172040 | tf_op jit(solution)/shard_map/ppermute | solution.py:28
  5.3 2.5 %collective-permute-start.3 = (bf16[112,256]{1,0:T(8,128)(2,1)S(1)}, bf16[112,256]{1,0:T(8,128)(2,1)S(1)}, u32[]{:S(2)}, u32[]{:S(2)}) collective-permute-start(bf16[112,256]{1,0:T(8,128)(2,1)S(1)} %get-tuple-element.24), channel_id=1, source_target_pairs={{0,24},{4,28},{8,16},{12,20},{16,8},{20,12},{24,0},{28,4},{1,25},{... | collective-permute-start | bytes 172040 | tf_op jit(solution)/shard_map/ppermute | solution.py:28
  7.8 0.1 collective-permute-start.2
  7.9 1.5 %collective-permute-start = (bf16[1024,256]{1,0:T(8,128)(2,1)}, bf16[1024,256]{1,0:T(8,128)(2,1)S(1)}, u32[]{:S(2)}, u32[]{:S(2)}) collective-permute-start(bf16[1024,256]{1,0:T(8,128)(2,1)} %x_ref.1), channel_id=1, source_target_pairs={{0,2},{1,3},{2,0},{3,1},{4,6},{5,7},{6,4},{7,5},{8,10},{9,11},{10,... | collective-permute-start | bytes 1572872 | tf_op jit(solution)/shard_map/ppermute | solution.py:28
  9.4 0.0 collective-permute-done.1
  9.4 4.2 %collective-permute-done.2 = bf16[112,256]{1,0:T(8,128)(2,1)S(1)} collective-permute-done((bf16[112,256]{1,0:T(8,128)(2,1)S(1)}, bf16[112,256]{1,0:T(8,128)(2,1)S(1)}, u32[]{:S(2)}, u32[]{:S(2)}) %collective-permute-start.2) | collective-permute-done | bytes 57376 | tf_op jit(solution)/shard_map/ppermute | solution.py:28
  13.6 0.0 collective-permute-done.3
  13.7 0.1 collective-permute-start.5
  13.7 1.6 %collective-permute-start.4 = (bf16[448,256]{1,0:T(8,128)(2,1)S(1)}, bf16[448,256]{1,0:T(8,128)(2,1)S(1)}, u32[]{:S(2)}, u32[]{:S(2)}) collective-permute-start(bf16[448,256]{1,0:T(8,128)(2,1)S(1)} %constant_dynamic-update-slice_fusion.refs_2_), channel_id=1, source_target_pairs={{0,4},{4,0},{8,12},{12,8},{16,20},{20,16},{24,28},{28,24},{1,5},{5... | collective-permute-start | bytes 688136 | tf_op jit(solution)/shard_map/ppermute | solution.py:28
  15.3 0.0 copy-start
  15.3 1.0 %copy-done = bf16[1024,256]{1,0:T(8,128)(2,1)S(1)} copy-done((bf16[1024,256]{1,0:T(8,128)(2,1)S(1)}, bf16[1024,256]{1,0:T(8,128)(2,1)}, u32[]{:S(2)}) %copy-start) | copy-done | bytes 524312
  16.4 0.4 shard_map.50
  16.8 0.0 collective-permute-done.5.refs_3_
  16.8 4.4 %collective-permute-done.refs_1_ = bf16[1024,256]{1,0:T(8,128)(2,1)S(1)} collective-permute-done((bf16[1024,256]{1,0:T(8,128)(2,1)}, bf16[1024,256]{1,0:T(8,128)(2,1)S(1)}, u32[]{:S(2)}, u32[]{:S(2)}) %collective-permute-start) | collective-permute-done | bytes 524320 | tf_op jit(solution)/shard_map/ppermute | solution.py:28
  21.2 2.7 %shard_map.52 = (f32[16,128]{1,0:T(8,128)S(1)}, bf16[768,256]{1,0:T(8,128)(2,1)S(1)}, f32[768,128]{1,0:T(8,128)S(1)}) custom-call(bf16[1024,256]{1,0:T(8,128)(2,1)S(1)} %get-tuple-element.22.refs_0_, bf16[1024,256]{1,0:T(8,128)(2,1)S(1)} %collective-permute-done.refs_1_, bf16[448,256]{1,0:T(8,128)(2,1)S(1)} %constant_dynamic-update-slice_fusion.refs_2_, ...), custom_call_target="tpu_custom_call" | custom-call | flops 805306368 | bytes 1441792 | tf_op jit(solution)/shard_map/pallas_call | solution.py:294
  24.0 0.0 collective-permute-done.4.refs_2_
  24.0 0.1 collective-permute-start.6
  24.1 1.9 %shard_map.53 = (f32[16,128]{1,0:T(8,128)S(1)}, bf16[384,256]{1,0:T(8,128)(2,1)S(1)}, f32[384,128]{1,0:T(8,128)S(1)}) custom-call(bf16[1024,256]{1,0:T(8,128)(2,1)S(1)} %get-tuple-element.22.refs_0_, bf16[1024,256]{1,0:T(8,128)(2,1)S(1)} %collective-permute-done.refs_1_, bf16[448,256]{1,0:T(8,128)(2,1)S(1)} %collective-permute-done.4.refs_2_, ...), custom_call_target="tpu_custom_call" | custom-call | flops 402653184 | bytes 1245184 | tf_op jit(solution)/shard_map/pallas_call | solution.py:294
  26.0 0.0 collective-permute-done.6.refs_2_
  26.0 1.9 %shard_map.54 = (f32[16,128]{1,0:T(8,128)S(1)}, bf16[384,256]{1,0:T(8,128)(2,1)S(1)}, f32[384,128]{1,0:T(8,128)S(1)}) custom-call(bf16[1024,256]{1,0:T(8,128)(2,1)S(1)} %get-tuple-element.22.refs_0_, bf16[1024,256]{1,0:T(8,128)(2,1)S(1)} %collective-permute-done.refs_1_, bf16[448,256]{1,0:T(8,128)(2,1)S(1)} %collective-permute-done.6.refs_2_, ...), custom_call_target="tpu_custom_call" | custom-call | flops 402653184 | bytes 1245184 | tf_op jit(solution)/shard_map/pallas_call | solution.py:294
  27.8 1.6 %collective-permute-start.7 = (f32[16,128]{1,0:T(8,128)S(1)}, f32[16,128]{1,0:T(8,128)S(1)}, u32[]{:S(2)}, u32[]{:S(2)}) collective-permute-start(f32[16,128]{1,0:T(8,128)S(1)} %get-tuple-element.31.refs_2_), channel_id=1, source_target_pairs={{0,2},{1,3},{2,0},{3,1},{4,6},{5,7},{6,4},{7,5},{8,10},{9,11},{10,... | collective-permute-start | bytes 24584 | tf_op jit(solution)/shard_map/ppermute | solution.py:28
  29.4 2.2 %collective-permute-done.7.refs_3_ = f32[16,128]{1,0:T(8,128)S(1)} collective-permute-done((f32[16,128]{1,0:T(8,128)S(1)}, f32[16,128]{1,0:T(8,128)S(1)}, u32[]{:S(2)}, u32[]{:S(2)}) %collective-permute-start.7) | collective-permute-done | bytes 8224 | tf_op jit(solution)/shard_map/ppermute | solution.py:28
  31.6 11.2 %shard_map.55 = (f32[8,128]{1,0:T(8,128)}, f32[1,96]{1,0:T(1,128)S(1)}, f32[32,96]{1,0:T(8,128)S(1)}) custom-call(bf16[1024,256]{1,0:T(8,128)(2,1)S(1)} %get-tuple-element.22.refs_0_, bf16[1024,256]{1,0:T(8,128)(2,1)S(1)} %collective-permute-done.refs_1_, f32[16,128]{1,0:T(8,128)S(1)} %get-tuple-element.31.refs_2_, ...), custom_call_target="tpu_custom_call" | custom-call | flops 1610612736 | bytes 1835008 | tf_op jit(solution)/shard_map/pallas_call | solution.py:322
  42.8 11.8 %all_to_all.12 = f32[32,1,96]{2,1,0:T(1,128)S(1)} all-to-all(f32[32,1,96]{2,1,0:T(1,128)S(1)} %bitcast.10), channel_id=1, replica_groups=mesh['gen'=8,'dat'=4] {'dat','gen'}, dimensions={0} | all-to-all | bytes 24576 | tf_op jit(solution)/shard_map/all_to_all | solution.py:347
  54.6 0.1 reduce_max.9
  54.7 0.5 fusion
  (4 shorter events, 0.0 us)
Async XLA Ops:
  0.6 0.7 %copy-start.2 = (f32[96]{0:T(128)S(1)}, f32[96]{0:T(128)}, u32[]{:S(2)}) copy-start(f32[96]{0:T(128)} %param.5) | copy-start | bytes 1156
  1.3 0.8 %copy-start.1 = (bf16[96,256]{1,0:T(8,128)(2,1)S(1)}, bf16[96,256]{1,0:T(8,128)(2,1)}, u32[]{:S(2)}) copy-start(bf16[96,256]{1,0:T(8,128)(2,1)} %y_ref.1) | copy-start | bytes 147460
  2.2 7.2 %collective-permute-start.1 = (bf16[112,256]{1,0:T(8,128)(2,1)S(1)}, bf16[112,256]{1,0:T(8,128)(2,1)S(1)}, u32[]{:S(2)}, u32[]{:S(2)}) collective-permute-start(bf16[112,256]{1,0:T(8,128)(2,1)S(1)} %get-tuple-element.24), channel_id=1, source_target_pairs={{0,8},{4,12},{8,0},{12,4},{16,24},{20,28},{24,16},{28,20},{1,9},{5... | collective-permute-start | bytes 172040 | tf_op jit(solution)/shard_map/ppermute | solution.py:28
  5.3 8.3 %collective-permute-start.3 = (bf16[112,256]{1,0:T(8,128)(2,1)S(1)}, bf16[112,256]{1,0:T(8,128)(2,1)S(1)}, u32[]{:S(2)}, u32[]{:S(2)}) collective-permute-start(bf16[112,256]{1,0:T(8,128)(2,1)S(1)} %get-tuple-element.24), channel_id=1, source_target_pairs={{0,24},{4,28},{8,16},{12,20},{16,8},{20,12},{24,0},{28,4},{1,25},{... | collective-permute-start | bytes 172040 | tf_op jit(solution)/shard_map/ppermute | solution.py:28
  7.8 5.8 %collective-permute-start.2 = (bf16[112,256]{1,0:T(8,128)(2,1)S(1)}, bf16[112,256]{1,0:T(8,128)(2,1)S(1)}, u32[]{:S(2)}, u32[]{:S(2)}) collective-permute-start(bf16[112,256]{1,0:T(8,128)(2,1)S(1)} %get-tuple-element.24), channel_id=1, source_target_pairs={{0,16},{4,20},{8,24},{12,28},{16,0},{20,4},{24,8},{28,12},{1,17},{... | collective-permute-start | bytes 172040 | tf_op jit(solution)/shard_map/ppermute | solution.py:28
  7.9 13.3 %collective-permute-start = (bf16[1024,256]{1,0:T(8,128)(2,1)}, bf16[1024,256]{1,0:T(8,128)(2,1)S(1)}, u32[]{:S(2)}, u32[]{:S(2)}) collective-permute-start(bf16[1024,256]{1,0:T(8,128)(2,1)} %x_ref.1), channel_id=1, source_target_pairs={{0,2},{1,3},{2,0},{3,1},{4,6},{5,7},{6,4},{7,5},{8,10},{9,11},{10,... | collective-permute-start | bytes 1572872 | tf_op jit(solution)/shard_map/ppermute | solution.py:28
  13.7 3.1 %collective-permute-start.5 = (bf16[448,256]{1,0:T(8,128)(2,1)S(1)}, bf16[448,256]{1,0:T(8,128)(2,1)S(1)}, u32[]{:S(2)}, u32[]{:S(2)}) collective-permute-start(bf16[448,256]{1,0:T(8,128)(2,1)S(1)} %constant_dynamic-update-slice_fusion.refs_2_), channel_id=1, source_target_pairs={{0,1},{1,0},{2,3},{3,2},{4,5},{5,4},{6,7},{7,6},{8,9},{9,8},{10,11... | collective-permute-start | bytes 688136 | tf_op jit(solution)/shard_map/ppermute | solution.py:28
  13.7 10.2 %collective-permute-start.4 = (bf16[448,256]{1,0:T(8,128)(2,1)S(1)}, bf16[448,256]{1,0:T(8,128)(2,1)S(1)}, u32[]{:S(2)}, u32[]{:S(2)}) collective-permute-start(bf16[448,256]{1,0:T(8,128)(2,1)S(1)} %constant_dynamic-update-slice_fusion.refs_2_), channel_id=1, source_target_pairs={{0,4},{4,0},{8,12},{12,8},{16,20},{20,16},{24,28},{28,24},{1,5},{5... | collective-permute-start | bytes 688136 | tf_op jit(solution)/shard_map/ppermute | solution.py:28
  15.3 1.0 %copy-start = (bf16[1024,256]{1,0:T(8,128)(2,1)S(1)}, bf16[1024,256]{1,0:T(8,128)(2,1)}, u32[]{:S(2)}) copy-start(bf16[1024,256]{1,0:T(8,128)(2,1)} %x_ref.1) | copy-start | bytes 1572868
  24.0 2.0 %collective-permute-start.6 = (bf16[448,256]{1,0:T(8,128)(2,1)S(1)}, bf16[448,256]{1,0:T(8,128)(2,1)S(1)}, u32[]{:S(2)}, u32[]{:S(2)}) collective-permute-start(bf16[448,256]{1,0:T(8,128)(2,1)S(1)} %collective-permute-done.4.refs_2_), channel_id=1, source_target_pairs={{0,1},{1,0},{2,3},{3,2},{4,5},{5,4},{6,7},{7,6},{8,9},{9,8},{10,11... | collective-permute-start | bytes 688136 | tf_op jit(solution)/shard_map/ppermute | solution.py:28
  27.8 3.7 %collective-permute-start.7 = (f32[16,128]{1,0:T(8,128)S(1)}, f32[16,128]{1,0:T(8,128)S(1)}, u32[]{:S(2)}, u32[]{:S(2)}) collective-permute-start(f32[16,128]{1,0:T(8,128)S(1)} %get-tuple-element.31.refs_2_), channel_id=1, source_target_pairs={{0,2},{1,3},{2,0},{3,1},{4,6},{5,7},{6,4},{7,5},{8,10},{9,11},{10,... | collective-permute-start | bytes 24584 | tf_op jit(solution)/shard_map/ppermute | solution.py:28

commit v8 on v7

--- a/solution.py
+++ b/solution.py
@@ -45,7 +45,15 @@
     return column, [0, *far]
 
 
-def pack_kernel(y_ref, g_ref, packed_ref, column_ref):
+def pack_kernel(y_hbm_ref, g_hbm_ref, packed_ref, column_ref, y_ref, g_ref, sems):
+    copies = [
+        pltpu.make_async_copy(y_hbm_ref, y_ref, sems.at[0]),
+        pltpu.make_async_copy(g_hbm_ref, g_ref, sems.at[1]),
+    ]
+    for copy in copies:
+        copy.start()
+    for copy in copies:
+        copy.wait()
     share, width = y_ref.shape
     tall = packed_ref.shape[0] - TILE
     y = y_ref[...]
@@ -116,20 +124,14 @@
     return jnp.concatenate([values] * count, axis=1)
 
 
-def each_pair(xs, block, dots_ref, fill, visit):
+def each_pair(xs, dots_ref, fill, visit):
     rows = xs[0].shape[0]
-    pair = 2 if rows // block % 2 == 0 else 1
+    half = rows // 2
     for place, x_ref in enumerate(xs):
-
-        def step(index, carry, place=place, x_ref=x_ref):
-            firsts = [(index * pair + k) * block for k in range(pair)]
-            for k, first in enumerate(firsts):
-                fill(dots_ref.at[k], x_ref[pl.ds(pl.multiple_of(first, block), block), :])
-            for k, first in enumerate(firsts):
-                visit(dots_ref.at[k], (place * rows + first) // LANES)
-            return carry
-
-        lax.fori_loop(0, rows // block // pair, step, 0)
+        for k in range(2):
+            fill(dots_ref.at[k], x_ref[k * half : (k + 1) * half, :])
+        for k in range(2):
+            visit(dots_ref.at[k], (place * rows + k * half) // LANES)
 
 
 def eight(values, op):
@@ -144,14 +146,14 @@
     return out
 
 
-def row_kernel(*refs, count, share, block, tall, merge):
+def row_kernel(*refs, count, share, tall, merge):
     xs, refs = refs[:count], refs[count:]
     *parts, l_ref, y_ref, b_ref, t_ref = refs
     before = parts.pop() if merge else None
     unpack(parts, share, y_ref, b_ref)
     cols, width = y_ref.shape
     alpha = 2.0 * SCALE / width
-    repeat = block // LANES
+    repeat = t_ref.shape[2] // LANES
 
     def fill(slot, x):
         slot[...] = dots(y_ref[...], x)
@@ -173,7 +175,7 @@
         for k in range(repeat):
             l_ref[pl.ds(place + k, 1), :] = log_sum[:, k * LANES : (k + 1) * LANES]
 
-    each_pair(xs, block, t_ref, fill, visit)
+    each_pair(xs, t_ref, fill, visit)
     if merge:
         l_ref[...] = merged([before[...], l_ref[...]])
 
@@ -183,16 +185,16 @@
     return top + jnp.log2(sum(jnp.exp2(piece - top) for piece in pieces))
 
 
-def column_kernel(*refs, count, share, block, tall, orders, masks, log_cols):
+def column_kernel(*refs, count, share, tall, orders, masks, log_cols):
     xs, refs = refs[:count], refs[count:]
     logs, refs = refs[: len(orders)], refs[len(orders) :]
     sq_ref, g_ref, *data, f_ref, own_g_ref, col_ref, l_ref, sum_ref, top_ref, t_ref = refs
     ys, biases = data[::2], data[1::2]
     rows, width = xs[0].shape
     alpha = 2.0 * SCALE / width
-    repeat = block // LANES
-    tiles = rows // LANES
-    for k in range(count):
+    repeat = t_ref.shape[2] // LANES
+    tiles = f_ref.shape[0]
+    for k in range(len(orders)):
         pieces = [log[order[k] * tiles : (order[k] + 1) * tiles, :] for log, order in zip(logs, orders)]
         l_ref[k * tiles : (k + 1) * tiles, :] = merged(pieces)
     own_g_ref[...] = g_ref[...]
@@ -216,7 +218,7 @@
                     visit(here, alpha * slot[here, :] + bias - log_here)
                 offset += b_ref.shape[0]
 
-        each_pair(xs, block, t_ref, fill, visit_all)
+        each_pair(xs, t_ref, fill, visit_all)
 
     def add(here, values):
         sum_ref[here, :] += fold(jnp.exp2(values), jnp.add)
@@ -266,21 +268,25 @@
             jax.ShapeDtypeStruct((span, width), jnp.bfloat16),
             jax.ShapeDtypeStruct((span * (n_gen // 2), width), jnp.bfloat16),
         ),
+        in_specs=[pl.BlockSpec(memory_space=pltpu.HBM)] * 2,
+        scratch_shapes=[
+            pltpu.VMEM((share, width), jnp.bfloat16),
+            pltpu.VMEM((1, share), jnp.float32),
+            pltpu.SemaphoreType.DMA((2,)),
+        ],
         compiler_params=pltpu.CompilerParams(vmem_limit_bytes=4 * MIB),
-    )(data_samples, own_g)
+    )(*[pltpu.with_memory_space_constraint(array, pltpu.HBM) for array in (data_samples, own_g)])
     xs, order = gather_gen(gen_samples)
     column, far = gather_column(message, column)
     sq, xs[0] = pl.pallas_call(
         norm_kernel,
         out_shape=(
             jax.ShapeDtypeStruct((tiles, LANES), jnp.float32),
-            jax.ShapeDtypeStruct(gen_samples.shape, gen_samples.dtype),
+            jax.ShapeDtypeStruct((rows, width), gen_samples.dtype),
         ),
         compiler_params=pltpu.CompilerParams(vmem_limit_bytes=8 * MIB),
     )(gen_samples)
-    block = min(256, rows)
     tall = 64
-    pair = 2 if rows // block % 2 == 0 else 1
 
     def cost(count):
         return pl.CostEstimate(
@@ -293,21 +299,25 @@
         count = len(parts) * half // 2
         return pl.pallas_call(
             functools.partial(
-                row_kernel, count=len(xs), share=share, block=block, tall=tall, merge=bool(before)
+                row_kernel, count=len(xs), share=share, tall=tall, merge=bool(before)
             ),
             out_shape=(
-                jax.ShapeDtypeStruct((len(xs) * tiles, LANES), jnp.float32),
+                jax.ShapeDtypeStruct((len(order) * tiles, LANES), jnp.float32),
                 jax.ShapeDtypeStruct((count, width), jnp.bfloat16),
                 jax.ShapeDtypeStruct((count, LANES), jnp.float32),
             ),
-            scratch_shapes=[pltpu.VMEM((pair, count, block), jnp.float32)],
+            scratch_shapes=[pltpu.VMEM((2, count, rows // 2), jnp.float32)],
             compiler_params=pltpu.CompilerParams(vmem_limit_bytes=12 * MIB),
             cost_estimate=cost(count),
         )(*xs, *parts, *before)
 
     near = swap(column, "gen", 1)
-    twin = swap(column, "dat", 1)
-    log, *data = row_pass([column, twin], [])
+    xs[1:], held = lax.optimization_barrier((xs[1:], column))
+    twin = swap(held, "dat", 1)
+    log, *data = row_pass([column], [])
+    twin, log = lax.optimization_barrier((twin, log))
+    log, *more = row_pass([twin], [log])
+    data += more
     near, log = lax.optimization_barrier((near, log))
     near_twin = swap(near, "dat", 1)
     log, *more = row_pass([near], [log])
@@ -324,7 +334,6 @@
             column_kernel,
             count=len(xs),
             share=share,
-            block=block,
             tall=tall,
             orders=orders,
             masks=masks,
@@ -336,10 +345,10 @@
             jax.ShapeDtypeStruct((n_dat * n_gen, share), jnp.float32),
         ),
         scratch_shapes=[
-            pltpu.VMEM((len(xs) * tiles, LANES), jnp.float32),
+            pltpu.VMEM((len(order) * tiles, LANES), jnp.float32),
             pltpu.VMEM((cols, LANES), jnp.float32),
             pltpu.VMEM((cols, LANES), jnp.float32),
-            pltpu.VMEM((pair, cols, block), jnp.float32),
+            pltpu.VMEM((2, cols, rows // 2), jnp.float32),
         ],
         compiler_params=pltpu.CompilerParams(vmem_limit_bytes=16 * MIB),
         cost_estimate=cost(cols),

time: 55.5 us -> 54.7 us (0.986)
  Pallas kernels: 18.3 us -> 15.9 us
  blocking collectives: 11.8 us -> 13 us
  waiting for transfers between devices: 10.8 us -> 11.8 us
  local copies, waits for them, and re-layouts: 2.5 us -> 1.71 us
    pallas_call x3 -> x4, Pallas kernels: 6.5 us -> 4.44 us  [row_pass(): pl.pallas_call(functools.partial(row_kernel, count=len(xs), share=share,...]
    all_to_all x1, blocking collectives: 11.8 us -> 13 us  [per_device(): totals = lax.all_to_all(col, ('dat', 'gen'), 0, 0, tiled=True)]
    pallas_call x1, Pallas kernels: 11.2 us -> 10.1 us  [per_device(): pl.pallas_call(functools.partial(column_kernel, count=len(xs), share=shar...]
    ppermute x8, waiting for transfers between devices: 10.8 us -> 11.8 us  [swap(): lax.ppermute(value, axis, [(k, k ^ mask) for k in range(lax.axis_size(axi...]
    pallas_call x1, Pallas kernels: 0.15 us -> 0.98 us  [per_device(): pl.pallas_call(pack_kernel, out_shape=(jax.ShapeDtypeStruct((span, width)...]
    unnamed x6 -> x4, local copies, waits for them, and re-layouts: 2.49 us -> 1.7 us
  transfers between devices with their start and end apart: 8 -> 8, of which waited for: 3 -> 5; matrix products, arithmetic and copies ran while one was open for 0% -> 0% of each run, Pallas kernels for 9% -> 9%
where the time goes in v8:
time: 54.7 us; the launch traced here: 54.5 us
  Pallas kernels  15.9 us (29%)
  blocking collectives  13 us (24%)
  waiting for transfers between devices  11.8 us (22%)
  starting transfers between devices  10.8 us (20%)
  local copies, waits for them, and re-layouts  1.71 us (3%)
  between operations  0.67 us (1%)
  other arithmetic  0.61 us (1%)
    all_to_all x1, blocking collectives, per_device(): totals = lax.all_to_all(col, ('dat', 'gen'), 0, 0, tiled=True)  13 us
    ppermute x8, waiting for transfers between devices, swap(): lax.ppermute(value, axis, [(k, k ^ mask) for k in range(lax.axis_size(axi...  11.8 us
    ppermute x8, starting transfers between devices, swap(): lax.ppermute(value, axis, [(k, k ^ mask) for k in range(lax.axis_size(axi...  10.8 us
    pallas_call x1, Pallas kernels, per_device(): pl.pallas_call(functools.partial(column_kernel, count=len(xs), share=shar...  10.1 us
    pallas_call x4, Pallas kernels, row_pass(): pl.pallas_call(functools.partial(row_kernel, count=len(xs), share=share,...  4.44 us
    unnamed x4, local copies, waits for them, and re-layouts  1.7 us
  transfers between devices with their start and end apart: 8, of which 5 were waited for; matrix products, arithmetic and copies ran while one was open for 0% of the time, Pallas kernels for 9%

profile of v8, /device:TPU:0, one launch (start us, length us, event | category | flops | bytes accessed | tf_op | source)
XLA Modules:
  0.0 54.5 jit_solution(16983706390379249529)
XLA Ops:
  0.6 3.0 %collective-permute-start = (bf16[1024,256]{1,0:T(8,128)(2,1)}, bf16[1024,256]{1,0:T(8,128)(2,1)S(1)}, u32[]{:S(2)}, u32[]{:S(2)}) collective-permute-start(bf16[1024,256]{1,0:T(8,128)(2,1)} %x_ref.1), channel_id=1, source_target_pairs={{0,2},{1,3},{2,0},{3,1},{4,6},{5,7},{6,4},{7,5},{8,10},{9,11},{10,... | collective-permute-start | bytes 1572872 | tf_op jit(solution)/shard_map/ppermute | solution.py:28
  3.6 1.0 %shard_map.51 = (bf16[112,256]{1,0:T(8,128)(2,1)S(1)}, bf16[448,256]{1,0:T(8,128)(2,1)S(1)}) custom-call(bf16[96,256]{1,0:T(8,128)(2,1)} %y_hbm_ref.1, f32[1,96]{1,0:T(1,128)} %bitcast.11), custom_call_target="tpu_custom_call" | custom-call | tf_op jit(solution)/shard_map/pallas_call | solution.py:265
  4.6 1.6 %collective-permute-start.1 = (bf16[112,256]{1,0:T(8,128)(2,1)S(1)}, bf16[112,256]{1,0:T(8,128)(2,1)S(1)}, u32[]{:S(2)}, u32[]{:S(2)}) collective-permute-start(bf16[112,256]{1,0:T(8,128)(2,1)S(1)} %get-tuple-element.31), channel_id=1, source_target_pairs={{0,8},{4,12},{8,0},{12,4},{16,24},{20,28},{24,16},{28,20},{1,9},{5... | collective-permute-start | bytes 172040 | tf_op jit(solution)/shard_map/ppermute | solution.py:28
  6.3 2.5 %collective-permute-start.3 = (bf16[112,256]{1,0:T(8,128)(2,1)S(1)}, bf16[112,256]{1,0:T(8,128)(2,1)S(1)}, u32[]{:S(2)}, u32[]{:S(2)}) collective-permute-start(bf16[112,256]{1,0:T(8,128)(2,1)S(1)} %get-tuple-element.31), channel_id=1, source_target_pairs={{0,24},{4,28},{8,16},{12,20},{16,8},{20,12},{24,0},{28,4},{1,25},{... | collective-permute-start | bytes 172040 | tf_op jit(solution)/shard_map/ppermute | solution.py:28
  8.7 0.1 collective-permute-start.2
  8.9 0.0 collective-permute-done.1
  8.9 5.6 %collective-permute-done.2 = bf16[112,256]{1,0:T(8,128)(2,1)S(1)} collective-permute-done((bf16[112,256]{1,0:T(8,128)(2,1)S(1)}, bf16[112,256]{1,0:T(8,128)(2,1)S(1)}, u32[]{:S(2)}, u32[]{:S(2)}) %collective-permute-start.2) | collective-permute-done | bytes 57376 | tf_op jit(solution)/shard_map/ppermute | solution.py:28
  14.4 0.0 collective-permute-done.3
  14.5 1.3 %collective-permute-done.refs_1_ = bf16[1024,256]{1,0:T(8,128)(2,1)S(1)} collective-permute-done((bf16[1024,256]{1,0:T(8,128)(2,1)}, bf16[1024,256]{1,0:T(8,128)(2,1)S(1)}, u32[]{:S(2)}, u32[]{:S(2)}) %collective-permute-start) | collective-permute-done | bytes 524320 | tf_op jit(solution)/shard_map/ppermute | solution.py:28
  15.8 0.0 collective-permute-start.5
  15.8 1.8 %collective-permute-start.4 = (bf16[448,256]{1,0:T(8,128)(2,1)S(1)}, bf16[448,256]{1,0:T(8,128)(2,1)S(1)}, u32[]{:S(2)}, u32[]{:S(2)}) collective-permute-start(bf16[448,256]{1,0:T(8,128)(2,1)S(1)} %constant_dynamic-update-slice_fusion.refs_2_), channel_id=1, source_target_pairs={{0,4},{4,0},{8,12},{12,8},{16,20},{20,16},{24,28},{28,24},{1,5},{5... | collective-permute-start | bytes 688136 | tf_op jit(solution)/shard_map/ppermute | solution.py:28
  17.5 0.0 copy-start
  17.5 1.0 %copy-done = bf16[1024,256]{1,0:T(8,128)(2,1)S(1)} copy-done((bf16[1024,256]{1,0:T(8,128)(2,1)S(1)}, bf16[1024,256]{1,0:T(8,128)(2,1)}, u32[]{:S(2)}) %copy-start) | copy-done | bytes 524312
  18.6 0.4 shard_map.50
  19.0 1.1 %shard_map.52 = (f32[16,128]{1,0:T(8,128)S(1)}, bf16[384,256]{1,0:T(8,128)(2,1)S(1)}, f32[384,128]{1,0:T(8,128)S(1)}) custom-call(bf16[1024,256]{1,0:T(8,128)(2,1)S(1)} %get-tuple-element.29.refs_0_, bf16[1024,256]{1,0:T(8,128)(2,1)S(1)} %collective-permute-done.refs_1_, bf16[448,256]{1,0:T(8,128)(2,1)S(1)} %constant_dynamic-update-slice_fusion.refs_2_), custom_call_target="tpu_custom_call" | custom-call | flops 402653184 | bytes 1245184 | tf_op jit(solution)/shard_map/pallas_call | solution.py:300
  20.1 0.0 collective-permute-done.5.refs_2_
  20.1 1.1 %shard_map.53 = (f32[16,128]{1,0:T(8,128)S(1)}, bf16[384,256]{1,0:T(8,128)(2,1)S(1)}, f32[384,128]{1,0:T(8,128)S(1)}) custom-call(bf16[1024,256]{1,0:T(8,128)(2,1)S(1)} %get-tuple-element.29.refs_0_, bf16[1024,256]{1,0:T(8,128)(2,1)S(1)} %collective-permute-done.refs_1_, bf16[448,256]{1,0:T(8,128)(2,1)S(1)} %collective-permute-done.5.refs_2_, ...), custom_call_target="tpu_custom_call" | custom-call | flops 402653184 | bytes 1245184 | tf_op jit(solution)/shard_map/pallas_call | solution.py:300
  21.2 2.6 %collective-permute-done.4.refs_2_ = bf16[448,256]{1,0:T(8,128)(2,1)S(1)} collective-permute-done((bf16[448,256]{1,0:T(8,128)(2,1)S(1)}, bf16[448,256]{1,0:T(8,128)(2,1)S(1)}, u32[]{:S(2)}, u32[]{:S(2)}) %collective-permute-start.4) | collective-permute-done | bytes 229408 | tf_op jit(solution)/shard_map/ppermute | solution.py:28
  23.8 0.0 collective-permute-start.6
  23.8 1.1 %shard_map.54 = (f32[16,128]{1,0:T(8,128)S(1)}, bf16[384,256]{1,0:T(8,128)(2,1)S(1)}, f32[384,128]{1,0:T(8,128)S(1)}) custom-call(bf16[1024,256]{1,0:T(8,128)(2,1)S(1)} %get-tuple-element.29.refs_0_, bf16[1024,256]{1,0:T(8,128)(2,1)S(1)} %collective-permute-done.refs_1_, bf16[448,256]{1,0:T(8,128)(2,1)S(1)} %collective-permute-done.4.refs_2_, ...), custom_call_target="tpu_custom_call" | custom-call | flops 402653184 | bytes 1245184 | tf_op jit(solution)/shard_map/pallas_call | solution.py:300
  24.9 0.4 collective-permute-done.6.refs_2_
  25.3 1.1 %shard_map.55 = (f32[16,128]{1,0:T(8,128)S(1)}, bf16[384,256]{1,0:T(8,128)(2,1)S(1)}, f32[384,128]{1,0:T(8,128)S(1)}) custom-call(bf16[1024,256]{1,0:T(8,128)(2,1)S(1)} %get-tuple-element.29.refs_0_, bf16[1024,256]{1,0:T(8,128)(2,1)S(1)} %collective-permute-done.refs_1_, bf16[448,256]{1,0:T(8,128)(2,1)S(1)} %collective-permute-done.6.refs_2_, ...), custom_call_target="tpu_custom_call" | custom-call | flops 402653184 | bytes 1245184 | tf_op jit(solution)/shard_map/pallas_call | solution.py:300
  26.4 1.8 %collective-permute-start.7 = (f32[16,128]{1,0:T(8,128)S(1)}, f32[16,128]{1,0:T(8,128)S(1)}, u32[]{:S(2)}, u32[]{:S(2)}) collective-permute-start(f32[16,128]{1,0:T(8,128)S(1)} %get-tuple-element.43.refs_2_), channel_id=1, source_target_pairs={{0,2},{1,3},{2,0},{3,1},{4,6},{5,7},{6,4},{7,5},{8,10},{9,11},{10,... | collective-permute-start | bytes 24584 | tf_op jit(solution)/shard_map/ppermute | solution.py:28
  28.2 1.9 %collective-permute-done.7.refs_3_ = f32[16,128]{1,0:T(8,128)S(1)} collective-permute-done((f32[16,128]{1,0:T(8,128)S(1)}, f32[16,128]{1,0:T(8,128)S(1)}, u32[]{:S(2)}, u32[]{:S(2)}) %collective-permute-start.7) | collective-permute-done | bytes 8224 | tf_op jit(solution)/shard_map/ppermute | solution.py:28
  30.1 0.0 copy-start.1
  30.1 0.7 %copy-done.1 = f32[96]{0:T(128)S(1)} copy-done((f32[96]{0:T(128)S(1)}, f32[96]{0:T(128)}, u32[]{:S(2)}) %copy-start.1) | copy-done | bytes 408
  30.8 10.1 %shard_map.56 = (f32[8,128]{1,0:T(8,128)}, f32[1,96]{1,0:T(1,128)S(1)}, f32[32,96]{1,0:T(8,128)S(1)}) custom-call(bf16[1024,256]{1,0:T(8,128)(2,1)S(1)} %get-tuple-element.29.refs_0_, bf16[1024,256]{1,0:T(8,128)(2,1)S(1)} %collective-permute-done.refs_1_, f32[16,128]{1,0:T(8,128)S(1)} %get-tuple-element.43.refs_2_, ...), custom_call_target="tpu_custom_call" | custom-call | flops 1610612736 | bytes 1835008 | tf_op jit(solution)/shard_map/pallas_call | solution.py:332
  40.9 13.0 %all_to_all.12 = f32[32,1,96]{2,1,0:T(1,128)S(1)} all-to-all(f32[32,1,96]{2,1,0:T(1,128)S(1)} %bitcast.10), channel_id=1, replica_groups=mesh['gen'=8,'dat'=4] {'dat','gen'}, dimensions={0} | all-to-all | bytes 24576 | tf_op jit(solution)/shard_map/all_to_all | solution.py:356
  53.9 0.1 reduce_max.9
  53.9 0.5 fusion
  (4 shorter events, 0.0 us)
Async XLA Ops:
  0.6 15.1 %collective-permute-start = (bf16[1024,256]{1,0:T(8,128)(2,1)}, bf16[1024,256]{1,0:T(8,128)(2,1)S(1)}, u32[]{:S(2)}, u32[]{:S(2)}) collective-permute-start(bf16[1024,256]{1,0:T(8,128)(2,1)} %x_ref.1), channel_id=1, source_target_pairs={{0,2},{1,3},{2,0},{3,1},{4,6},{5,7},{6,4},{7,5},{8,10},{9,11},{10,... | collective-permute-start | bytes 1572872 | tf_op jit(solution)/shard_map/ppermute | solution.py:28
  4.6 4.2 %collective-permute-start.1 = (bf16[112,256]{1,0:T(8,128)(2,1)S(1)}, bf16[112,256]{1,0:T(8,128)(2,1)S(1)}, u32[]{:S(2)}, u32[]{:S(2)}) collective-permute-start(bf16[112,256]{1,0:T(8,128)(2,1)S(1)} %get-tuple-element.31), channel_id=1, source_target_pairs={{0,8},{4,12},{8,0},{12,4},{16,24},{20,28},{24,16},{28,20},{1,9},{5... | collective-permute-start | bytes 172040 | tf_op jit(solution)/shard_map/ppermute | solution.py:28
  6.3 8.2 %collective-permute-start.3 = (bf16[112,256]{1,0:T(8,128)(2,1)S(1)}, bf16[112,256]{1,0:T(8,128)(2,1)S(1)}, u32[]{:S(2)}, u32[]{:S(2)}) collective-permute-start(bf16[112,256]{1,0:T(8,128)(2,1)S(1)} %get-tuple-element.31), channel_id=1, source_target_pairs={{0,24},{4,28},{8,16},{12,20},{16,8},{20,12},{24,0},{28,4},{1,25},{... | collective-permute-start | bytes 172040 | tf_op jit(solution)/shard_map/ppermute | solution.py:28
  8.7 5.7 %collective-permute-start.2 = (bf16[112,256]{1,0:T(8,128)(2,1)S(1)}, bf16[112,256]{1,0:T(8,128)(2,1)S(1)}, u32[]{:S(2)}, u32[]{:S(2)}) collective-permute-start(bf16[112,256]{1,0:T(8,128)(2,1)S(1)} %get-tuple-element.31), channel_id=1, source_target_pairs={{0,16},{4,20},{8,24},{12,28},{16,0},{20,4},{24,8},{28,12},{1,17},{... | collective-permute-start | bytes 172040 | tf_op jit(solution)/shard_map/ppermute | solution.py:28
  15.8 4.4 %collective-permute-start.5 = (bf16[448,256]{1,0:T(8,128)(2,1)S(1)}, bf16[448,256]{1,0:T(8,128)(2,1)S(1)}, u32[]{:S(2)}, u32[]{:S(2)}) collective-permute-start(bf16[448,256]{1,0:T(8,128)(2,1)S(1)} %constant_dynamic-update-slice_fusion.refs_2_), channel_id=1, source_target_pairs={{0,1},{1,0},{2,3},{3,2},{4,5},{5,4},{6,7},{7,6},{8,9},{9,8},{10,11... | collective-permute-start | bytes 688136 | tf_op jit(solution)/shard_map/ppermute | solution.py:28
  15.8 8.0 %collective-permute-start.4 = (bf16[448,256]{1,0:T(8,128)(2,1)S(1)}, bf16[448,256]{1,0:T(8,128)(2,1)S(1)}, u32[]{:S(2)}, u32[]{:S(2)}) collective-permute-start(bf16[448,256]{1,0:T(8,128)(2,1)S(1)} %constant_dynamic-update-slice_fusion.refs_2_), channel_id=1, source_target_pairs={{0,4},{4,0},{8,12},{12,8},{16,20},{20,16},{24,28},{28,24},{1,5},{5... | collective-permute-start | bytes 688136 | tf_op jit(solution)/shard_map/ppermute | solution.py:28
  17.5 1.0 %copy-start = (bf16[1024,256]{1,0:T(8,128)(2,1)S(1)}, bf16[1024,256]{1,0:T(8,128)(2,1)}, u32[]{:S(2)}) copy-start(bf16[1024,256]{1,0:T(8,128)(2,1)} %x_ref.1) | copy-start | bytes 1572868
  23.8 1.5 %collective-permute-start.6 = (bf16[448,256]{1,0:T(8,128)(2,1)S(1)}, bf16[448,256]{1,0:T(8,128)(2,1)S(1)}, u32[]{:S(2)}, u32[]{:S(2)}) collective-permute-start(bf16[448,256]{1,0:T(8,128)(2,1)S(1)} %collective-permute-done.4.refs_2_), channel_id=1, source_target_pairs={{0,1},{1,0},{2,3},{3,2},{4,5},{5,4},{6,7},{7,6},{8,9},{9,8},{10,11... | collective-permute-start | bytes 688136 | tf_op jit(solution)/shard_map/ppermute | solution.py:28
  26.4 3.7 %collective-permute-start.7 = (f32[16,128]{1,0:T(8,128)S(1)}, f32[16,128]{1,0:T(8,128)S(1)}, u32[]{:S(2)}, u32[]{:S(2)}) collective-permute-start(f32[16,128]{1,0:T(8,128)S(1)} %get-tuple-element.43.refs_2_), channel_id=1, source_target_pairs={{0,2},{1,3},{2,0},{3,1},{4,6},{5,7},{6,4},{7,5},{8,10},{9,11},{10,... | collective-permute-start | bytes 24584 | tf_op jit(solution)/shard_map/ppermute | solution.py:28
  30.1 0.7 %copy-start.1 = (f32[96]{0:T(128)S(1)}, f32[96]{0:T(128)}, u32[]{:S(2)}) copy-start(f32[96]{0:T(128)} %param.5) | copy-start | bytes 1156

commit v9 on v8

--- a/solution.py
+++ b/solution.py
@@ -14,8 +14,8 @@
 SCALE = LOG2E / EPS
 LANES = 128
 TILE = 16
-LIFT = 100.0
-FLOOR = 2.0**-90
+LIFT = 50.0
+FLOOR = 2.0**-41
 MIB = 1024 * 1024
 NOTHING = -1e30
 
@@ -45,7 +45,7 @@
     return column, [0, *far]
 
 
-def pack_kernel(y_hbm_ref, g_hbm_ref, packed_ref, column_ref, y_ref, g_ref, sems):
+def pack_kernel(y_hbm_ref, g_hbm_ref, packed_ref, column_ref, own_g_ref, y_ref, g_ref, sems):
     copies = [
         pltpu.make_async_copy(y_hbm_ref, y_ref, sems.at[0]),
         pltpu.make_async_copy(g_hbm_ref, g_ref, sems.at[1]),
@@ -56,6 +56,7 @@
         copy.wait()
     share, width = y_ref.shape
     tall = packed_ref.shape[0] - TILE
+    own_g_ref[...] = g_ref[...]
     y = y_ref[...]
     wide = y.astype(jnp.float32)
     sq = jnp.sum(wide * wide, axis=1, keepdims=True)
@@ -148,7 +149,7 @@
 
 def row_kernel(*refs, count, share, tall, merge):
     xs, refs = refs[:count], refs[count:]
-    *parts, l_ref, y_ref, b_ref, t_ref = refs
+    *parts, l_ref, top_ref, e_ref, y_ref, b_ref, t_ref = refs
     before = parts.pop() if merge else None
     unpack(parts, share, y_ref, b_ref)
     cols, width = y_ref.shape
@@ -166,14 +167,19 @@
             slot[here, :] = t
             part = eight(t, jnp.max)
             top = part if top is None else jnp.maximum(top, part)
-        top = jnp.max(top, axis=0, keepdims=True)
+        base = jnp.max(top, axis=0, keepdims=True) - LIFT
         total = None
         for start, size in spans(cols, tall):
-            part = eight(jnp.exp2(slot[start : start + size, :] - top), jnp.sum)
+            here = slice(start, start + size)
+            e = jnp.exp2(slot[here, :] - base)
+            e_ref[place // repeat, here, :] = e
+            part = eight(e, jnp.sum)
             total = part if total is None else total + part
-        log_sum = top + jnp.log2(jnp.sum(total, axis=0, keepdims=True))
+        log_sum = base + jnp.log2(jnp.sum(total, axis=0, keepdims=True))
         for k in range(repeat):
-            l_ref[pl.ds(place + k, 1), :] = log_sum[:, k * LANES : (k + 1) * LANES]
+            lanes = slice(k * LANES, (k + 1) * LANES)
+            l_ref[place + k : place + k + 1, :] = log_sum[:, lanes]
+            top_ref[place + k : place + k + 1, :] = base[:, lanes] + LIFT
 
     each_pair(xs, t_ref, fill, visit)
     if merge:
@@ -188,8 +194,8 @@
 def column_kernel(*refs, count, share, tall, orders, masks, log_cols):
     xs, refs = refs[:count], refs[count:]
     logs, refs = refs[: len(orders)], refs[len(orders) :]
-    sq_ref, g_ref, *data, f_ref, own_g_ref, col_ref, l_ref, sum_ref, top_ref, t_ref = refs
-    ys, biases = data[::2], data[1::2]
+    sq_ref, *data, f_ref, col_ref, l_ref, sum_ref, top_ref, t_ref = refs
+    tops, es, ys, biases = data[::4], data[1::4], data[2::4], data[3::4]
     rows, width = xs[0].shape
     alpha = 2.0 * SCALE / width
     repeat = t_ref.shape[2] // LANES
@@ -197,7 +203,6 @@
     for k in range(len(orders)):
         pieces = [log[order[k] * tiles : (order[k] + 1) * tiles, :] for log, order in zip(logs, orders)]
         l_ref[k * tiles : (k + 1) * tiles, :] = merged(pieces)
-    own_g_ref[...] = g_ref[...]
     f_ref[...] = sq_ref[...] / width - (EPS * LN2) * l_ref[:tiles, :] + EPS * log_cols
 
     def fill(slot, x):
@@ -207,9 +212,9 @@
             slot[offset : offset + cols, :] = dots(y_ref[...], x)
             offset += cols
 
-    def each(lift, visit):
+    def each(visit):
         def visit_all(slot, place):
-            log_here = jnp.concatenate([l_ref[pl.ds(place + k, 1), :] for k in range(repeat)], axis=1) - lift
+            log_here = jnp.concatenate([l_ref[place + k : place + k + 1, :] for k in range(repeat)], axis=1)
             offset = 0
             for b_ref in biases:
                 for start, size in spans(b_ref.shape[0], tall):
@@ -220,28 +225,40 @@
 
         each_pair(xs, t_ref, fill, visit_all)
 
-    def add(here, values):
-        sum_ref[here, :] += fold(jnp.exp2(values), jnp.add)
-
     def raise_top(here, values):
         top_ref[here, :] = jnp.maximum(top_ref[here, :], fold(values, jnp.maximum))
 
     def add_from_top(here, values):
         sum_ref[here, :] += fold(jnp.exp2(values - across(top_ref[here, :], repeat)), jnp.add)
 
-    sum_ref[...] = jnp.zeros(sum_ref.shape, jnp.float32)
-    each(LIFT, add)
+    offset = 0
+    for held_ref, e_ref in zip(tops, es):
+        weights = jnp.exp2(held_ref[...] - l_ref[...] + LIFT)
+        scale = [
+            jnp.concatenate([weights[k * repeat + i : k * repeat + i + 1, :] for i in range(repeat)], axis=1)
+            for k in range(e_ref.shape[0])
+        ]
+
+        def add(index, carry, e_ref=e_ref, scale=scale, offset=offset):
+            start = pl.multiple_of(index * tall, tall)
+            here = pl.ds(start, tall)
+            parts = [fold(e_ref[k, here, :] * scale[k], jnp.add) for k in range(len(scale))]
+            sum_ref[pl.ds(offset + start, tall), :] = functools.reduce(jnp.add, parts)
+            return carry
+
+        lax.fori_loop(0, e_ref.shape[1] // tall, add, 0)
+        offset += e_ref.shape[1]
     least = jnp.min(jnp.sum(sum_ref[...], axis=1, keepdims=True))
-    top_ref[...] = jnp.full(top_ref.shape, -LIFT, jnp.float32)
+    top_ref[...] = jnp.full(top_ref.shape, -2.0 * LIFT, jnp.float32)
 
     @pl.when(jnp.logical_not(least >= FLOOR))
     def _():
         top_ref[...] = jnp.full(top_ref.shape, -jnp.inf, jnp.float32)
-        each(0.0, raise_top)
+        each(raise_top)
         top = jnp.max(top_ref[...], axis=1, keepdims=True)
         top_ref[...] = jnp.broadcast_to(top, top_ref.shape)
         sum_ref[...] = jnp.zeros(sum_ref.shape, jnp.float32)
-        each(0.0, add_from_top)
+        each(add_from_top)
 
     gen, dat = lax.axis_index("gen"), lax.axis_index("dat")
     n_gen = lax.axis_size("gen")
@@ -262,11 +279,12 @@
     tiles = rows // LANES
     span = round_up(share, TILE) + TILE
     own_g = data_potential.reshape(1, share)
-    message, column = pl.pallas_call(
+    message, column, held_g = pl.pallas_call(
         pack_kernel,
         out_shape=(
             jax.ShapeDtypeStruct((span, width), jnp.bfloat16),
             jax.ShapeDtypeStruct((span * (n_gen // 2), width), jnp.bfloat16),
+            jax.ShapeDtypeStruct((1, share), jnp.float32),
         ),
         in_specs=[pl.BlockSpec(memory_space=pltpu.HBM)] * 2,
         scratch_shapes=[
@@ -303,6 +321,8 @@
             ),
             out_shape=(
                 jax.ShapeDtypeStruct((len(order) * tiles, LANES), jnp.float32),
+                jax.ShapeDtypeStruct((len(order) * tiles, LANES), jnp.float32),
+                jax.ShapeDtypeStruct((2 * len(xs), count, rows // 2), jnp.float32),
                 jax.ShapeDtypeStruct((count, width), jnp.bfloat16),
                 jax.ShapeDtypeStruct((count, LANES), jnp.float32),
             ),
@@ -315,21 +335,21 @@
     xs[1:], held = lax.optimization_barrier((xs[1:], column))
     twin = swap(held, "dat", 1)
     log, *data = row_pass([column], [])
-    twin, log = lax.optimization_barrier((twin, log))
-    log, *more = row_pass([twin], [log])
-    data += more
     near, log = lax.optimization_barrier((near, log))
     near_twin = swap(near, "dat", 1)
     log, *more = row_pass([near], [log])
     data += more
+    twin, log = lax.optimization_barrier((twin, log))
+    log, *more = row_pass([twin], [log])
+    data += more
     near_twin, log = lax.optimization_barrier((near_twin, log))
     log, *more = row_pass([near_twin], [log])
     data += more
-    masks = [(g ^ a, b) for a in (0, 1) for b in (0, 1) for g in far]
+    masks = [(g ^ a, b) for b in (0, 1) for a in (0, 1) for g in far]
     logs = [log]
     logs += [swap(logs[0], "dat", m) for m in order[1:]]
     orders = [[order.index(m ^ partner) for m in order] for partner in order]
-    f, own_g, col = pl.pallas_call(
+    f, col = pl.pallas_call(
         functools.partial(
             column_kernel,
             count=len(xs),
@@ -341,7 +361,6 @@
         ),
         out_shape=(
             jax.ShapeDtypeStruct((tiles, LANES), jnp.float32),
-            jax.ShapeDtypeStruct((1, share), jnp.float32),
             jax.ShapeDtypeStruct((n_dat * n_gen, share), jnp.float32),
         ),
         scratch_shapes=[
@@ -352,11 +371,11 @@
         ],
         compiler_params=pltpu.CompilerParams(vmem_limit_bytes=16 * MIB),
         cost_estimate=cost(cols),
-    )(*xs, *logs, sq, own_g, *data)
+    )(*xs, *logs, sq, *data)
     totals = lax.all_to_all(col, ("dat", "gen"), 0, 0, tiled=True)
     top = jnp.max(totals, axis=0)
     total = top + jnp.log2(jnp.sum(jnp.exp2(totals - top[None, :]), axis=0))
-    new_data = own_g[0] - (EPS * LN2) * total + EPS * math.log(rows * n_gen / half)
+    new_data = held_g[0] - (EPS * LN2) * total + EPS * math.log(rows * n_gen / half)
     return f.reshape(rows), new_data
 
 

time: 54.7 us -> 49.5 us (0.905)
  Pallas kernels: 15.9 us -> 13.3 us
  blocking collectives: 13 us -> 11.8 us
  waiting for transfers between devices: 11.8 us -> 10.9 us
  local copies, waits for them, and re-layouts: 1.71 us -> 1.06 us
    pallas_call x1, Pallas kernels: 10.1 us -> 7.13 us  [per_device(): pl.pallas_call(functools.partial(column_kernel, count=len(xs), share=shar...]
    all_to_all x1, blocking collectives: 13 us -> 11.8 us  [per_device(): totals = lax.all_to_all(col, ('dat', 'gen'), 0, 0, tiled=True)]
    ppermute x8, waiting for transfers between devices: 11.8 us -> 10.9 us  [swap(): lax.ppermute(value, axis, [(k, k ^ mask) for k in range(lax.axis_size(axi...]
    unnamed x4 -> x2, local copies, waits for them, and re-layouts: 1.7 us -> 1.04 us
  transfers between devices with their start and end apart: 8 -> 8, of which waited for: 5 -> 3; matrix products, arithmetic and copies ran while one was open for 0% -> 0% of each run, Pallas kernels for 9% -> 8%
where the time goes in v9:
time: 49.5 us; the launch traced here: 49.3 us
  Pallas kernels  13.3 us (27%)
  blocking collectives  11.8 us (24%)
  starting transfers between devices  10.9 us (22%)
  waiting for transfers between devices  10.9 us (22%)
  local copies, waits for them, and re-layouts  1.06 us (2%)
  between operations  0.69 us (1%)
  other arithmetic  0.61 us (1%)
    all_to_all x1, blocking collectives, per_device(): totals = lax.all_to_all(col, ('dat', 'gen'), 0, 0, tiled=True)  11.8 us
    ppermute x8, waiting for transfers between devices, swap(): lax.ppermute(value, axis, [(k, k ^ mask) for k in range(lax.axis_size(axi...  10.9 us
    ppermute x8, starting transfers between devices, swap(): lax.ppermute(value, axis, [(k, k ^ mask) for k in range(lax.axis_size(axi...  10.9 us
    pallas_call x1, Pallas kernels, per_device(): pl.pallas_call(functools.partial(column_kernel, count=len(xs), share=shar...  7.13 us
    pallas_call x4, Pallas kernels, row_pass(): pl.pallas_call(functools.partial(row_kernel, count=len(xs), share=share,...  4.8 us
    unnamed x2, local copies, waits for them, and re-layouts  1.04 us
  transfers between devices with their start and end apart: 8, of which 3 were waited for; matrix products, arithmetic and copies ran while one was open for 0% of the time, Pallas kernels for 8%

profile of v9, /device:TPU:0, one launch (start us, length us, event | category | flops | bytes accessed | tf_op | source)
XLA Modules:
  0.0 49.3 jit_solution(11424016012376620147)
XLA Ops:
  0.6 1.0 %shard_map.51 = (bf16[112,256]{1,0:T(8,128)(2,1)S(1)}, bf16[448,256]{1,0:T(8,128)(2,1)S(1)}, f32[1,96]{1,0:T(1,128)S(1)}) custom-call(bf16[96,256]{1,0:T(8,128)(2,1)} %y_hbm_ref.1, f32[1,96]{1,0:T(1,128)} %bitcast.12), custom_call_target="tpu_custom_call" | custom-call | tf_op jit(solution)/shard_map/pallas_call | solution.py:282
  1.6 3.1 %collective-permute-start.1 = (bf16[112,256]{1,0:T(8,128)(2,1)S(1)}, bf16[112,256]{1,0:T(8,128)(2,1)S(1)}, u32[]{:S(2)}, u32[]{:S(2)}) collective-permute-start(bf16[112,256]{1,0:T(8,128)(2,1)S(1)} %get-tuple-element.39), channel_id=1, source_target_pairs={{0,8},{4,12},{8,0},{12,4},{16,24},{20,28},{24,16},{28,20},{1,9},{5... | collective-permute-start | bytes 172040 | tf_op jit(solution)/shard_map/ppermute | solution.py:28
  4.7 2.5 %collective-permute-start.3 = (bf16[112,256]{1,0:T(8,128)(2,1)S(1)}, bf16[112,256]{1,0:T(8,128)(2,1)S(1)}, u32[]{:S(2)}, u32[]{:S(2)}) collective-permute-start(bf16[112,256]{1,0:T(8,128)(2,1)S(1)} %get-tuple-element.39), channel_id=1, source_target_pairs={{0,24},{4,28},{8,16},{12,20},{16,8},{20,12},{24,0},{28,4},{1,25},{... | collective-permute-start | bytes 172040 | tf_op jit(solution)/shard_map/ppermute | solution.py:28
  7.2 0.1 collective-permute-start.2
  7.3 1.5 %collective-permute-start = (bf16[1024,256]{1,0:T(8,128)(2,1)}, bf16[1024,256]{1,0:T(8,128)(2,1)S(1)}, u32[]{:S(2)}, u32[]{:S(2)}) collective-permute-start(bf16[1024,256]{1,0:T(8,128)(2,1)} %x_ref.1), channel_id=1, source_target_pairs={{0,2},{1,3},{2,0},{3,1},{4,6},{5,7},{6,4},{7,5},{8,10},{9,11},{10,... | collective-permute-start | bytes 1572872 | tf_op jit(solution)/shard_map/ppermute | solution.py:28
  8.8 0.0 collective-permute-done.1
  8.8 4.2 %collective-permute-done.2 = bf16[112,256]{1,0:T(8,128)(2,1)S(1)} collective-permute-done((bf16[112,256]{1,0:T(8,128)(2,1)S(1)}, bf16[112,256]{1,0:T(8,128)(2,1)S(1)}, u32[]{:S(2)}, u32[]{:S(2)}) %collective-permute-start.2) | collective-permute-done | bytes 57376 | tf_op jit(solution)/shard_map/ppermute | solution.py:28
  13.0 0.0 collective-permute-done.3
  13.1 1.6 %collective-permute-start.4 = (bf16[448,256]{1,0:T(8,128)(2,1)S(1)}, bf16[448,256]{1,0:T(8,128)(2,1)S(1)}, u32[]{:S(2)}, u32[]{:S(2)}) collective-permute-start(bf16[448,256]{1,0:T(8,128)(2,1)S(1)} %constant_dynamic-update-slice_fusion.refs_2_), channel_id=1, source_target_pairs={{0,4},{4,0},{8,12},{12,8},{16,20},{20,16},{24,28},{28,24},{1,5},{5... | collective-permute-start | bytes 688136 | tf_op jit(solution)/shard_map/ppermute | solution.py:28
  14.6 0.0 copy-start
  14.6 1.0 %copy-done = bf16[1024,256]{1,0:T(8,128)(2,1)S(1)} copy-done((bf16[1024,256]{1,0:T(8,128)(2,1)S(1)}, bf16[1024,256]{1,0:T(8,128)(2,1)}, u32[]{:S(2)}) %copy-start) | copy-done | bytes 524312
  15.7 0.4 shard_map.50
  16.1 4.5 %collective-permute-done.refs_1_ = bf16[1024,256]{1,0:T(8,128)(2,1)S(1)} collective-permute-done((bf16[1024,256]{1,0:T(8,128)(2,1)}, bf16[1024,256]{1,0:T(8,128)(2,1)S(1)}, u32[]{:S(2)}, u32[]{:S(2)}) %collective-permute-start) | collective-permute-done | bytes 524320 | tf_op jit(solution)/shard_map/ppermute | solution.py:28
  20.6 0.0 collective-permute-start.6
  20.6 1.2 %shard_map.52 = (f32[16,128]{1,0:T(8,128)S(1)}, f32[16,128]{1,0:T(8,128)S(1)}, f32[4,384,512]{2,1,0:T(8,128)S(1)}, bf16[384,256]{1,0:T(8,128)(2,1)S(1)}, f32[384,128]{1,0:T(8,128)S(1)}) custom-call(bf16[1024,256]{1,0:T(8,128)(2,1)S(1)} %get-tuple-element.37.refs_0_, bf16[1024,256]{1,0:T(8,128)(2,1)S(1)} %collective-permute-done.refs_1_, ...), custom_call_target="tpu_custom_call" | custom-call | flops 402653184 | bytes 1245184 | tf_op jit(solution)/shard_map/pallas_call | solution.py:318
  21.8 0.0 collective-permute-done.4.refs_2_
  21.8 0.6 %collective-permute-start.5 = (bf16[448,256]{1,0:T(8,128)(2,1)S(1)}, bf16[448,256]{1,0:T(8,128)(2,1)S(1)}, u32[]{:S(2)}, u32[]{:S(2)}) collective-permute-start(bf16[448,256]{1,0:T(8,128)(2,1)S(1)} %collective-permute-done.4.refs_2_), channel_id=1, source_target_pairs={{0,1},{1,0},{2,3},{3,2},{4,5},{5,4},{6,7},{7,6},{8,9},{9,8},{10,11... | collective-permute-start | bytes 688136 | tf_op jit(solution)/shard_map/ppermute | solution.py:28
  22.4 1.2 %shard_map.53 = (f32[16,128]{1,0:T(8,128)S(1)}, f32[16,128]{1,0:T(8,128)S(1)}, f32[4,384,512]{2,1,0:T(8,128)S(1)}, bf16[384,256]{1,0:T(8,128)(2,1)S(1)}, f32[384,128]{1,0:T(8,128)S(1)}) custom-call(bf16[1024,256]{1,0:T(8,128)(2,1)S(1)} %get-tuple-element.37.refs_0_, bf16[1024,256]{1,0:T(8,128)(2,1)S(1)} %collective-permute-done.refs_1_, ...), custom_call_target="tpu_custom_call" | custom-call | flops 402653184 | bytes 1245184 | tf_op jit(solution)/shard_map/pallas_call | solution.py:318
  23.6 0.0 collective-permute-done.6.refs_2_
  23.6 1.2 %shard_map.54 = (f32[16,128]{1,0:T(8,128)S(1)}, f32[16,128]{1,0:T(8,128)S(1)}, f32[4,384,512]{2,1,0:T(8,128)S(1)}, bf16[384,256]{1,0:T(8,128)(2,1)S(1)}, f32[384,128]{1,0:T(8,128)S(1)}) custom-call(bf16[1024,256]{1,0:T(8,128)(2,1)S(1)} %get-tuple-element.37.refs_0_, bf16[1024,256]{1,0:T(8,128)(2,1)S(1)} %collective-permute-done.refs_1_, ...), custom_call_target="tpu_custom_call" | custom-call | flops 402653184 | bytes 1245184 | tf_op jit(solution)/shard_map/pallas_call | solution.py:318
  24.8 0.0 collective-permute-done.5.refs_2_
  24.8 1.2 %shard_map.55 = (f32[16,128]{1,0:T(8,128)S(1)}, f32[16,128]{1,0:T(8,128)S(1)}, f32[4,384,512]{2,1,0:T(8,128)S(1)}, bf16[384,256]{1,0:T(8,128)(2,1)S(1)}, f32[384,128]{1,0:T(8,128)S(1)}) custom-call(bf16[1024,256]{1,0:T(8,128)(2,1)S(1)} %get-tuple-element.37.refs_0_, bf16[1024,256]{1,0:T(8,128)(2,1)S(1)} %collective-permute-done.refs_1_, ...), custom_call_target="tpu_custom_call" | custom-call | flops 402653184 | bytes 1245184 | tf_op jit(solution)/shard_map/pallas_call | solution.py:318
  26.0 1.6 %collective-permute-start.7 = (f32[16,128]{1,0:T(8,128)S(1)}, f32[16,128]{1,0:T(8,128)S(1)}, u32[]{:S(2)}, u32[]{:S(2)}) collective-permute-start(f32[16,128]{1,0:T(8,128)S(1)} %get-tuple-element.51.refs_2_), channel_id=1, source_target_pairs={{0,2},{1,3},{2,0},{3,1},{4,6},{5,7},{6,4},{7,5},{8,10},{9,11},{10,... | collective-permute-start | bytes 24584 | tf_op jit(solution)/shard_map/ppermute | solution.py:28
  27.6 2.2 %collective-permute-done.7.refs_3_ = f32[16,128]{1,0:T(8,128)S(1)} collective-permute-done((f32[16,128]{1,0:T(8,128)S(1)}, f32[16,128]{1,0:T(8,128)S(1)}, u32[]{:S(2)}, u32[]{:S(2)}) %collective-permute-start.7) | collective-permute-done | bytes 8224 | tf_op jit(solution)/shard_map/ppermute | solution.py:28
  29.7 7.1 %shard_map.56 = (f32[8,128]{1,0:T(8,128)}, f32[32,96]{1,0:T(8,128)S(1)}) custom-call(bf16[1024,256]{1,0:T(8,128)(2,1)S(1)} %get-tuple-element.37.refs_0_, bf16[1024,256]{1,0:T(8,128)(2,1)S(1)} %collective-permute-done.refs_1_, f32[16,128]{1,0:T(8,128)S(1)} %get-tuple-element.51.refs_2_, f32[16,128]{1,0:T(8,128)S(1)} %collective-permute-done.7.refs_3_, ...), custom_call_target="tpu_custom_call" | custom-call | flops 1610612736 | bytes 1835008 | tf_op jit(solution)/shard_map/pallas_call | solution.py:352
  36.9 11.8 %all_to_all.12 = f32[32,1,96]{2,1,0:T(1,128)S(1)} all-to-all(f32[32,1,96]{2,1,0:T(1,128)S(1)} %bitcast.10), channel_id=1, replica_groups=mesh['gen'=8,'dat'=4] {'dat','gen'}, dimensions={0} | all-to-all | bytes 24576 | tf_op jit(solution)/shard_map/all_to_all | solution.py:375
  48.7 0.1 reduce_max.9
  48.8 0.5 %fusion = f32[96]{0:T(128)} fusion(f32[1,96]{1,0:T(1,128)S(1)} %get-tuple-element.70, f32[96]{0:T(128)S(1)} %reduce_max.9, f32[96]{0:T(128)S(1)} %exponential_reduce_fusion), kind=kLoop, calls=%fused_computation.5 | loop fusion | flops 480 | bytes 1536 | tf_op jit(solution)/shard_map/add | solution.py:378
  (4 shorter events, 0.0 us)
Async XLA Ops:
  1.6 7.2 %collective-permute-start.1 = (bf16[112,256]{1,0:T(8,128)(2,1)S(1)}, bf16[112,256]{1,0:T(8,128)(2,1)S(1)}, u32[]{:S(2)}, u32[]{:S(2)}) collective-permute-start(bf16[112,256]{1,0:T(8,128)(2,1)S(1)} %get-tuple-element.39), channel_id=1, source_target_pairs={{0,8},{4,12},{8,0},{12,4},{16,24},{20,28},{24,16},{28,20},{1,9},{5... | collective-permute-start | bytes 172040 | tf_op jit(solution)/shard_map/ppermute | solution.py:28
  4.7 8.3 %collective-permute-start.3 = (bf16[112,256]{1,0:T(8,128)(2,1)S(1)}, bf16[112,256]{1,0:T(8,128)(2,1)S(1)}, u32[]{:S(2)}, u32[]{:S(2)}) collective-permute-start(bf16[112,256]{1,0:T(8,128)(2,1)S(1)} %get-tuple-element.39), channel_id=1, source_target_pairs={{0,24},{4,28},{8,16},{12,20},{16,8},{20,12},{24,0},{28,4},{1,25},{... | collective-permute-start | bytes 172040 | tf_op jit(solution)/shard_map/ppermute | solution.py:28
  7.2 5.8 %collective-permute-start.2 = (bf16[112,256]{1,0:T(8,128)(2,1)S(1)}, bf16[112,256]{1,0:T(8,128)(2,1)S(1)}, u32[]{:S(2)}, u32[]{:S(2)}) collective-permute-start(bf16[112,256]{1,0:T(8,128)(2,1)S(1)} %get-tuple-element.39), channel_id=1, source_target_pairs={{0,16},{4,20},{8,24},{12,28},{16,0},{20,4},{24,8},{28,12},{1,17},{... | collective-permute-start | bytes 172040 | tf_op jit(solution)/shard_map/ppermute | solution.py:28
  7.3 13.3 %collective-permute-start = (bf16[1024,256]{1,0:T(8,128)(2,1)}, bf16[1024,256]{1,0:T(8,128)(2,1)S(1)}, u32[]{:S(2)}, u32[]{:S(2)}) collective-permute-start(bf16[1024,256]{1,0:T(8,128)(2,1)} %x_ref.1), channel_id=1, source_target_pairs={{0,2},{1,3},{2,0},{3,1},{4,6},{5,7},{6,4},{7,5},{8,10},{9,11},{10,... | collective-permute-start | bytes 1572872 | tf_op jit(solution)/shard_map/ppermute | solution.py:28
  13.1 8.8 %collective-permute-start.4 = (bf16[448,256]{1,0:T(8,128)(2,1)S(1)}, bf16[448,256]{1,0:T(8,128)(2,1)S(1)}, u32[]{:S(2)}, u32[]{:S(2)}) collective-permute-start(bf16[448,256]{1,0:T(8,128)(2,1)S(1)} %constant_dynamic-update-slice_fusion.refs_2_), channel_id=1, source_target_pairs={{0,4},{4,0},{8,12},{12,8},{16,20},{20,16},{24,28},{28,24},{1,5},{5... | collective-permute-start | bytes 688136 | tf_op jit(solution)/shard_map/ppermute | solution.py:28
  14.6 1.0 %copy-start = (bf16[1024,256]{1,0:T(8,128)(2,1)S(1)}, bf16[1024,256]{1,0:T(8,128)(2,1)}, u32[]{:S(2)}) copy-start(bf16[1024,256]{1,0:T(8,128)(2,1)} %x_ref.1) | copy-start | bytes 1572868
  20.6 3.0 %collective-permute-start.6 = (bf16[448,256]{1,0:T(8,128)(2,1)S(1)}, bf16[448,256]{1,0:T(8,128)(2,1)S(1)}, u32[]{:S(2)}, u32[]{:S(2)}) collective-permute-start(bf16[448,256]{1,0:T(8,128)(2,1)S(1)} %constant_dynamic-update-slice_fusion.refs_2_), channel_id=1, source_target_pairs={{0,1},{1,0},{2,3},{3,2},{4,5},{5,4},{6,7},{7,6},{8,9},{9,8},{10,11... | collective-permute-start | bytes 688136 | tf_op jit(solution)/shard_map/ppermute | solution.py:28
  21.8 3.0 %collective-permute-start.5 = (bf16[448,256]{1,0:T(8,128)(2,1)S(1)}, bf16[448,256]{1,0:T(8,128)(2,1)S(1)}, u32[]{:S(2)}, u32[]{:S(2)}) collective-permute-start(bf16[448,256]{1,0:T(8,128)(2,1)S(1)} %collective-permute-done.4.refs_2_), channel_id=1, source_target_pairs={{0,1},{1,0},{2,3},{3,2},{4,5},{5,4},{6,7},{7,6},{8,9},{9,8},{10,11... | collective-permute-start | bytes 688136 | tf_op jit(solution)/shard_map/ppermute | solution.py:28
  26.0 3.7 %collective-permute-start.7 = (f32[16,128]{1,0:T(8,128)S(1)}, f32[16,128]{1,0:T(8,128)S(1)}, u32[]{:S(2)}, u32[]{:S(2)}) collective-permute-start(f32[16,128]{1,0:T(8,128)S(1)} %get-tuple-element.51.refs_2_), channel_id=1, source_target_pairs={{0,2},{1,3},{2,0},{3,1},{4,6},{5,7},{6,4},{7,5},{8,10},{9,11},{10,... | collective-permute-start | bytes 24584 | tf_op jit(solution)/shard_map/ppermute | solution.py:28

commit v10 on v9

--- a/solution.py
+++ b/solution.py
@@ -147,11 +147,14 @@
     return out
 
 
-def row_kernel(*refs, count, share, tall, merge):
+def row_kernel(*refs, count, share, tall, merge, unpacked):
     xs, refs = refs[:count], refs[count:]
-    *parts, l_ref, top_ref, e_ref, y_ref, b_ref, t_ref = refs
-    before = parts.pop() if merge else None
-    unpack(parts, share, y_ref, b_ref)
+    before, refs = refs[:merge], refs[merge:]
+    if unpacked:
+        y_ref, b_ref, l_ref, top_ref, e_ref, t_ref = refs
+    else:
+        *parts, l_ref, top_ref, e_ref, y_ref, b_ref, t_ref = refs
+        unpack(parts, share, y_ref, b_ref)
     cols, width = y_ref.shape
     alpha = 2.0 * SCALE / width
     repeat = t_ref.shape[2] // LANES
@@ -183,7 +186,7 @@
 
     each_pair(xs, t_ref, fill, visit)
     if merge:
-        l_ref[...] = merged([before[...], l_ref[...]])
+        l_ref[...] = merged([jnp.concatenate([log[...] for log in before], axis=0), l_ref[...]])
 
 
 def merged(pieces):
@@ -191,11 +194,13 @@
     return top + jnp.log2(sum(jnp.exp2(piece - top) for piece in pieces))
 
 
-def column_kernel(*refs, count, share, tall, orders, masks, log_cols):
+def column_kernel(*refs, count, share, tall, orders, masks, log_cols, segments):
     xs, refs = refs[:count], refs[count:]
     logs, refs = refs[: len(orders)], refs[len(orders) :]
     sq_ref, *data, f_ref, col_ref, l_ref, sum_ref, top_ref, t_ref = refs
-    tops, es, ys, biases = data[::4], data[1::4], data[2::4], data[3::4]
+    calls = sum(len(segment) for segment in segments)
+    held, data = data[: 2 * calls], data[2 * calls :]
+    ys, biases = data[::2], data[1::2]
     rows, width = xs[0].shape
     alpha = 2.0 * SCALE / width
     repeat = t_ref.shape[2] // LANES
@@ -232,17 +237,20 @@
         sum_ref[here, :] += fold(jnp.exp2(values - across(top_ref[here, :], repeat)), jnp.add)
 
     offset = 0
-    for held_ref, e_ref in zip(tops, es):
-        weights = jnp.exp2(held_ref[...] - l_ref[...] + LIFT)
-        scale = [
-            jnp.concatenate([weights[k * repeat + i : k * repeat + i + 1, :] for i in range(repeat)], axis=1)
-            for k in range(e_ref.shape[0])
-        ]
-
-        def add(index, carry, e_ref=e_ref, scale=scale, offset=offset):
+    for segment in segments:
+        pieces = []
+        for first in segment:
+            held_ref, e_ref, *held = held
+            logs_here = l_ref[first * tiles : first * tiles + held_ref.shape[0], :]
+            weights = jnp.exp2(held_ref[...] - logs_here + LIFT)
+            for k in range(e_ref.shape[0]):
+                scale = [weights[k * repeat + i : k * repeat + i + 1, :] for i in range(repeat)]
+                pieces.append((e_ref, k, jnp.concatenate(scale, axis=1)))
+
+        def add(index, carry, pieces=pieces, offset=offset):
             start = pl.multiple_of(index * tall, tall)
             here = pl.ds(start, tall)
-            parts = [fold(e_ref[k, here, :] * scale[k], jnp.add) for k in range(len(scale))]
+            parts = [fold(e_ref[k, here, :] * scale, jnp.add) for e_ref, k, scale in pieces]
             sum_ref[pl.ds(offset + start, tall), :] = functools.reduce(jnp.add, parts)
             return carry
 
@@ -313,39 +321,49 @@
             transcendentals=rows * len(xs) * count,
         )
 
-    def row_pass(parts, before):
-        count = len(parts) * half // 2
-        return pl.pallas_call(
+    def row_pass(rows_of, parts, before=(), unpacked=None):
+        count = unpacked[0].shape[0] if unpacked else len(parts) * half // 2
+        logs_shape = jax.ShapeDtypeStruct((len(rows_of) * tiles, LANES), jnp.float32)
+        unpacked_shapes = (
+            jax.ShapeDtypeStruct((count, width), jnp.bfloat16),
+            jax.ShapeDtypeStruct((count, LANES), jnp.float32),
+        )
+        log, top, e, *rest = pl.pallas_call(
             functools.partial(
-                row_kernel, count=len(xs), share=share, tall=tall, merge=bool(before)
+                row_kernel,
+                count=len(rows_of),
+                share=share,
+                tall=tall,
+                merge=len(before),
+                unpacked=unpacked is not None,
             ),
             out_shape=(
-                jax.ShapeDtypeStruct((len(order) * tiles, LANES), jnp.float32),
-                jax.ShapeDtypeStruct((len(order) * tiles, LANES), jnp.float32),
-                jax.ShapeDtypeStruct((2 * len(xs), count, rows // 2), jnp.float32),
-                jax.ShapeDtypeStruct((count, width), jnp.bfloat16),
-                jax.ShapeDtypeStruct((count, LANES), jnp.float32),
-            ),
+                logs_shape,
+                logs_shape,
+                jax.ShapeDtypeStruct((2 * len(rows_of), count, rows // 2), jnp.float32),
+            )
+            + (() if unpacked else unpacked_shapes),
             scratch_shapes=[pltpu.VMEM((2, count, rows // 2), jnp.float32)],
             compiler_params=pltpu.CompilerParams(vmem_limit_bytes=12 * MIB),
             cost_estimate=cost(count),
-        )(*xs, *parts, *before)
+        )(*rows_of, *before, *(unpacked or parts))
+        return log, [top, e], rest
 
     near = swap(column, "gen", 1)
-    xs[1:], held = lax.optimization_barrier((xs[1:], column))
-    twin = swap(held, "dat", 1)
-    log, *data = row_pass([column], [])
-    near, log = lax.optimization_barrier((near, log))
+    twin = swap(column, "dat", 1)
+    log_own, held_own, data = row_pass(xs[:1], [column, twin])
+    near, log_own = lax.optimization_barrier((near, log_own))
     near_twin = swap(near, "dat", 1)
-    log, *more = row_pass([near], [log])
-    data += more
-    twin, log = lax.optimization_barrier((twin, log))
-    log, *more = row_pass([twin], [log])
-    data += more
+    xs[1:], near = lax.optimization_barrier((xs[1:], near))
+    log_others, held_others, _ = row_pass(xs[1:], [], unpacked=data)
+    log, held_near, more = row_pass(xs, [near], [log_own, log_others])
+    data = data + more
     near_twin, log = lax.optimization_barrier((near_twin, log))
-    log, *more = row_pass([near_twin], [log])
-    data += more
-    masks = [(g ^ a, b) for b in (0, 1) for a in (0, 1) for g in far]
+    log, held_last, more = row_pass(xs, [near_twin], [log])
+    data = data + more
+    held = held_own + held_others + held_near + held_last
+    segments = [[0, 1], [0], [0]]
+    masks = [(g ^ a, b) for a in (0, 1) for b in (0, 1) for g in far]
     logs = [log]
     logs += [swap(logs[0], "dat", m) for m in order[1:]]
     orders = [[order.index(m ^ partner) for m in order] for partner in order]
@@ -358,6 +376,7 @@
             orders=orders,
             masks=masks,
             log_cols=math.log(half * n_dat),
+            segments=segments,
         ),
         out_shape=(
             jax.ShapeDtypeStruct((tiles, LANES), jnp.float32),
@@ -371,7 +390,7 @@
         ],
         compiler_params=pltpu.CompilerParams(vmem_limit_bytes=16 * MIB),
         cost_estimate=cost(cols),
-    )(*xs, *logs, sq, *data)
+    )(*xs, *logs, sq, *held, *data)
     totals = lax.all_to_all(col, ("dat", "gen"), 0, 0, tiled=True)
     top = jnp.max(totals, axis=0)
     total = top + jnp.log2(jnp.sum(jnp.exp2(totals - top[None, :]), axis=0))

time: 49.5 us -> 47.7 us (0.964)
  waiting for transfers between devices: 10.9 us -> 10.2 us
  starting transfers between devices: 10.9 us -> 10.4 us
    ppermute x8, waiting for transfers between devices: 10.9 us -> 10.2 us  [swap(): lax.ppermute(value, axis, [(k, k ^ mask) for k in range(lax.axis_size(axi...]
    ppermute x8, starting transfers between devices: 10.9 us -> 10.4 us  [swap(): lax.ppermute(value, axis, [(k, k ^ mask) for k in range(lax.axis_size(axi...]
where the time goes in v10:
time: 47.7 us; the launch traced here: 47.5 us
  Pallas kernels  13 us (27%)
  blocking collectives  11.6 us (24%)
  starting transfers between devices  10.4 us (22%)
  waiting for transfers between devices  10.2 us (21%)
  local copies, waits for them, and re-layouts  1.06 us (2%)
  between operations  0.68 us (1%)
  other arithmetic  0.61 us (1%)
    all_to_all x1, blocking collectives, per_device(): totals = lax.all_to_all(col, ('dat', 'gen'), 0, 0, tiled=True)  11.6 us
    ppermute x8, starting transfers between devices, swap(): lax.ppermute(value, axis, [(k, k ^ mask) for k in range(lax.axis_size(axi...  10.4 us
    ppermute x8, waiting for transfers between devices, swap(): lax.ppermute(value, axis, [(k, k ^ mask) for k in range(lax.axis_size(axi...  10.2 us
    pallas_call x1, Pallas kernels, per_device(): pl.pallas_call(functools.partial(column_kernel, count=len(xs), share=shar...  6.87 us
    pallas_call x4, Pallas kernels, row_pass(): pl.pallas_call(functools.partial(row_kernel, count=len(rows_of), share=sh...  4.73 us
    unnamed x2, local copies, waits for them, and re-layouts  1.04 us
    pallas_call x1, Pallas kernels, per_device(): pl.pallas_call(pack_kernel, out_shape=(jax.ShapeDtypeStruct((span, width)...  0.99 us
  transfers between devices with their start and end apart: 8, of which 3 were waited for; matrix products, arithmetic and copies ran while one was open for 0% of the time, Pallas kernels for 8%

profile of v10, /device:TPU:0, one launch (start us, length us, event | category | flops | bytes accessed | tf_op | source)
XLA Modules:
  0.0 47.5 jit_solution(3533506542069867941)
XLA Ops:
  0.6 1.0 %shard_map.51 = (bf16[112,256]{1,0:T(8,128)(2,1)S(1)}, bf16[448,256]{1,0:T(8,128)(2,1)S(1)}, f32[1,96]{1,0:T(1,128)S(1)}) custom-call(bf16[96,256]{1,0:T(8,128)(2,1)} %y_hbm_ref.1, f32[1,96]{1,0:T(1,128)} %bitcast.12), custom_call_target="tpu_custom_call" | custom-call | tf_op jit(solution)/shard_map/pallas_call | solution.py:290
  1.6 3.1 %collective-permute-start.1 = (bf16[112,256]{1,0:T(8,128)(2,1)S(1)}, bf16[112,256]{1,0:T(8,128)(2,1)S(1)}, u32[]{:S(2)}, u32[]{:S(2)}) collective-permute-start(bf16[112,256]{1,0:T(8,128)(2,1)S(1)} %get-tuple-element.35), channel_id=1, source_target_pairs={{0,8},{4,12},{8,0},{12,4},{16,24},{20,28},{24,16},{28,20},{1,9},{5... | collective-permute-start | bytes 172040 | tf_op jit(solution)/shard_map/ppermute | solution.py:28
  4.7 2.5 %collective-permute-start.3 = (bf16[112,256]{1,0:T(8,128)(2,1)S(1)}, bf16[112,256]{1,0:T(8,128)(2,1)S(1)}, u32[]{:S(2)}, u32[]{:S(2)}) collective-permute-start(bf16[112,256]{1,0:T(8,128)(2,1)S(1)} %get-tuple-element.35), channel_id=1, source_target_pairs={{0,24},{4,28},{8,16},{12,20},{16,8},{20,12},{24,0},{28,4},{1,25},{... | collective-permute-start | bytes 172040 | tf_op jit(solution)/shard_map/ppermute | solution.py:28
  7.2 0.1 collective-permute-start.2
  7.3 1.5 %collective-permute-start = (bf16[1024,256]{1,0:T(8,128)(2,1)}, bf16[1024,256]{1,0:T(8,128)(2,1)S(1)}, u32[]{:S(2)}, u32[]{:S(2)}) collective-permute-start(bf16[1024,256]{1,0:T(8,128)(2,1)} %x_ref.1), channel_id=1, source_target_pairs={{0,2},{1,3},{2,0},{3,1},{4,6},{5,7},{6,4},{7,5},{8,10},{9,11},{10,... | collective-permute-start | bytes 1572872 | tf_op jit(solution)/shard_map/ppermute | solution.py:28
  8.8 0.0 collective-permute-done.1
  8.8 4.2 %collective-permute-done.2 = bf16[112,256]{1,0:T(8,128)(2,1)S(1)} collective-permute-done((bf16[112,256]{1,0:T(8,128)(2,1)S(1)}, bf16[112,256]{1,0:T(8,128)(2,1)S(1)}, u32[]{:S(2)}, u32[]{:S(2)}) %collective-permute-start.2) | collective-permute-done | bytes 57376 | tf_op jit(solution)/shard_map/ppermute | solution.py:28
  13.0 0.0 collective-permute-done.3
  13.1 0.1 collective-permute-start.5
  13.1 1.6 %collective-permute-start.4 = (bf16[448,256]{1,0:T(8,128)(2,1)S(1)}, bf16[448,256]{1,0:T(8,128)(2,1)S(1)}, u32[]{:S(2)}, u32[]{:S(2)}) collective-permute-start(bf16[448,256]{1,0:T(8,128)(2,1)S(1)} %constant_dynamic-update-slice_fusion.refs_1_), channel_id=1, source_target_pairs={{0,4},{4,0},{8,12},{12,8},{16,20},{20,16},{24,28},{28,24},{1,5},{5... | collective-permute-start | bytes 688136 | tf_op jit(solution)/shard_map/ppermute | solution.py:28
  14.7 0.0 copy-start
  14.7 1.0 %copy-done = bf16[1024,256]{1,0:T(8,128)(2,1)S(1)} copy-done((bf16[1024,256]{1,0:T(8,128)(2,1)S(1)}, bf16[1024,256]{1,0:T(8,128)(2,1)}, u32[]{:S(2)}) %copy-start) | copy-done | bytes 524312
  15.8 0.4 shard_map.50
  16.2 0.0 collective-permute-done.5.refs_2_
  16.2 1.2 %shard_map.52 = (f32[8,128]{1,0:T(8,128)S(1)}, f32[8,128]{1,0:T(8,128)S(1)}, f32[2,768,512]{2,1,0:T(8,128)S(1)}, bf16[768,256]{1,0:T(8,128)(2,1)S(1)}, f32[768,128]{1,0:T(8,128)S(1)}) custom-call(bf16[1024,256]{1,0:T(8,128)(2,1)S(1)} %get-tuple-element.33.refs_0_, bf16[448,256]{1,0:T(8,128)(2,1)S(1)} %constant_dynamic-update-slice_fusion.refs_1_, ...), custom_call_target="tpu_custom_call" | custom-call | flops 805306368 | bytes 1441792 | tf_op jit(solution)/shard_map/pallas_call | solution.py:331
  17.4 3.8 %collective-permute-done.4.refs_4_ = bf16[448,256]{1,0:T(8,128)(2,1)S(1)} collective-permute-done((bf16[448,256]{1,0:T(8,128)(2,1)S(1)}, bf16[448,256]{1,0:T(8,128)(2,1)S(1)}, u32[]{:S(2)}, u32[]{:S(2)}) %collective-permute-start.4) | collective-permute-done | bytes 229408 | tf_op jit(solution)/shard_map/ppermute | solution.py:28
  21.2 0.0 collective-permute-start.6
  21.2 0.0 collective-permute-done.refs_0_.refs_1_
  21.2 1.1 %shard_map.53 = (f32[8,128]{1,0:T(8,128)S(1)}, f32[8,128]{1,0:T(8,128)S(1)}, f32[2,768,512]{2,1,0:T(8,128)S(1)}) custom-call(bf16[1024,256]{1,0:T(8,128)(2,1)S(1)} %collective-permute-done.refs_0_.refs_1_, bf16[768,256]{1,0:T(8,128)(2,1)S(1)} %get-tuple-element.40.refs_1_.refs_13_, f32[768,128]{1,0:T(8,128)S(1)} %get-tuple-element.41.refs_2_.refs_14_), custom_call_target="tpu_custom_call" | custom-call | flops 805306368 | bytes 1441792 | tf_op jit(solution)/shard_map/pallas_call | solution.py:331
  22.3 1.2 %shard_map.54 = (f32[16,128]{1,0:T(8,128)S(1)}, f32[16,128]{1,0:T(8,128)S(1)}, f32[4,384,512]{2,1,0:T(8,128)S(1)}, bf16[384,256]{1,0:T(8,128)(2,1)S(1)}, f32[384,128]{1,0:T(8,128)S(1)}) custom-call(bf16[1024,256]{1,0:T(8,128)(2,1)S(1)} %get-tuple-element.33.refs_0_, bf16[1024,256]{1,0:T(8,128)(2,1)S(1)} %collective-permute-done.refs_0_.refs_1_, ...), custom_call_target="tpu_custom_call" | custom-call | flops 402653184 | bytes 1245184 | tf_op jit(solution)/shard_map/pallas_call | solution.py:331
  23.5 0.0 collective-permute-done.6.refs_3_
  23.5 1.2 %shard_map.55 = (f32[16,128]{1,0:T(8,128)S(1)}, f32[16,128]{1,0:T(8,128)S(1)}, f32[4,384,512]{2,1,0:T(8,128)S(1)}, bf16[384,256]{1,0:T(8,128)(2,1)S(1)}, f32[384,128]{1,0:T(8,128)S(1)}) custom-call(bf16[1024,256]{1,0:T(8,128)(2,1)S(1)} %get-tuple-element.33.refs_0_, bf16[1024,256]{1,0:T(8,128)(2,1)S(1)} %collective-permute-done.refs_0_.refs_1_, ...), custom_call_target="tpu_custom_call" | custom-call | flops 402653184 | bytes 1245184 | tf_op jit(solution)/shard_map/pallas_call | solution.py:331
  24.7 1.6 %collective-permute-start.7 = (f32[16,128]{1,0:T(8,128)S(1)}, f32[16,128]{1,0:T(8,128)S(1)}, u32[]{:S(2)}, u32[]{:S(2)}) collective-permute-start(f32[16,128]{1,0:T(8,128)S(1)} %get-tuple-element.47.refs_2_), channel_id=1, source_target_pairs={{0,2},{1,3},{2,0},{3,1},{4,6},{5,7},{6,4},{7,5},{8,10},{9,11},{10,... | collective-permute-start | bytes 24584 | tf_op jit(solution)/shard_map/ppermute | solution.py:28
  26.3 2.2 %collective-permute-done.7.refs_3_ = f32[16,128]{1,0:T(8,128)S(1)} collective-permute-done((f32[16,128]{1,0:T(8,128)S(1)}, f32[16,128]{1,0:T(8,128)S(1)}, u32[]{:S(2)}, u32[]{:S(2)}) %collective-permute-start.7) | collective-permute-done | bytes 8224 | tf_op jit(solution)/shard_map/ppermute | solution.py:28
  28.4 6.9 %shard_map.56 = (f32[8,128]{1,0:T(8,128)}, f32[32,96]{1,0:T(8,128)S(1)}) custom-call(bf16[1024,256]{1,0:T(8,128)(2,1)S(1)} %get-tuple-element.33.refs_0_, bf16[1024,256]{1,0:T(8,128)(2,1)S(1)} %collective-permute-done.refs_0_.refs_1_, f32[16,128]{1,0:T(8,128)S(1)} %get-tuple-element.47.refs_2_, f32[16,128]{1,0:T(8,128)S(1)} %collective-permute-done.7.refs_3_, ...), custom_call_target="tpu_custom_call" | custom-call | flops 1610612736 | bytes 1835008 | tf_op jit(solution)/shard_map/pallas_call | solution.py:370
  35.3 11.6 %all_to_all.12 = f32[32,1,96]{2,1,0:T(1,128)S(1)} all-to-all(f32[32,1,96]{2,1,0:T(1,128)S(1)} %bitcast.10), channel_id=1, replica_groups=mesh['gen'=8,'dat'=4] {'dat','gen'}, dimensions={0} | all-to-all | bytes 24576 | tf_op jit(solution)/shard_map/all_to_all | solution.py:394
  46.9 0.1 reduce_max.9
  47.0 0.5 %fusion = f32[96]{0:T(128)} fusion(f32[1,96]{1,0:T(1,128)S(1)} %get-tuple-element.62, f32[96]{0:T(128)S(1)} %reduce_max.9, f32[96]{0:T(128)S(1)} %exponential_reduce_fusion), kind=kLoop, calls=%fused_computation.5 | loop fusion | flops 480 | bytes 1536 | tf_op jit(solution)/shard_map/add | solution.py:397
  (4 shorter events, 0.0 us)
Async XLA Ops:
  1.6 7.2 %collective-permute-start.1 = (bf16[112,256]{1,0:T(8,128)(2,1)S(1)}, bf16[112,256]{1,0:T(8,128)(2,1)S(1)}, u32[]{:S(2)}, u32[]{:S(2)}) collective-permute-start(bf16[112,256]{1,0:T(8,128)(2,1)S(1)} %get-tuple-element.35), channel_id=1, source_target_pairs={{0,8},{4,12},{8,0},{12,4},{16,24},{20,28},{24,16},{28,20},{1,9},{5... | collective-permute-start | bytes 172040 | tf_op jit(solution)/shard_map/ppermute | solution.py:28
  4.7 8.3 %collective-permute-start.3 = (bf16[112,256]{1,0:T(8,128)(2,1)S(1)}, bf16[112,256]{1,0:T(8,128)(2,1)S(1)}, u32[]{:S(2)}, u32[]{:S(2)}) collective-permute-start(bf16[112,256]{1,0:T(8,128)(2,1)S(1)} %get-tuple-element.35), channel_id=1, source_target_pairs={{0,24},{4,28},{8,16},{12,20},{16,8},{20,12},{24,0},{28,4},{1,25},{... | collective-permute-start | bytes 172040 | tf_op jit(solution)/shard_map/ppermute | solution.py:28
  7.2 5.8 %collective-permute-start.2 = (bf16[112,256]{1,0:T(8,128)(2,1)S(1)}, bf16[112,256]{1,0:T(8,128)(2,1)S(1)}, u32[]{:S(2)}, u32[]{:S(2)}) collective-permute-start(bf16[112,256]{1,0:T(8,128)(2,1)S(1)} %get-tuple-element.35), channel_id=1, source_target_pairs={{0,16},{4,20},{8,24},{12,28},{16,0},{20,4},{24,8},{28,12},{1,17},{... | collective-permute-start | bytes 172040 | tf_op jit(solution)/shard_map/ppermute | solution.py:28
  7.3 13.9 %collective-permute-start = (bf16[1024,256]{1,0:T(8,128)(2,1)}, bf16[1024,256]{1,0:T(8,128)(2,1)S(1)}, u32[]{:S(2)}, u32[]{:S(2)}) collective-permute-start(bf16[1024,256]{1,0:T(8,128)(2,1)} %x_ref.1), channel_id=1, source_target_pairs={{0,2},{1,3},{2,0},{3,1},{4,6},{5,7},{6,4},{7,5},{8,10},{9,11},{10,... | collective-permute-start | bytes 1572872 | tf_op jit(solution)/shard_map/ppermute | solution.py:28
  13.1 3.1 %collective-permute-start.5 = (bf16[448,256]{1,0:T(8,128)(2,1)S(1)}, bf16[448,256]{1,0:T(8,128)(2,1)S(1)}, u32[]{:S(2)}, u32[]{:S(2)}) collective-permute-start(bf16[448,256]{1,0:T(8,128)(2,1)S(1)} %constant_dynamic-update-slice_fusion.refs_1_), channel_id=1, source_target_pairs={{0,1},{1,0},{2,3},{3,2},{4,5},{5,4},{6,7},{7,6},{8,9},{9,8},{10,11... | collective-permute-start | bytes 688136 | tf_op jit(solution)/shard_map/ppermute | solution.py:28
  13.1 8.0 %collective-permute-start.4 = (bf16[448,256]{1,0:T(8,128)(2,1)S(1)}, bf16[448,256]{1,0:T(8,128)(2,1)S(1)}, u32[]{:S(2)}, u32[]{:S(2)}) collective-permute-start(bf16[448,256]{1,0:T(8,128)(2,1)S(1)} %constant_dynamic-update-slice_fusion.refs_1_), channel_id=1, source_target_pairs={{0,4},{4,0},{8,12},{12,8},{16,20},{20,16},{24,28},{28,24},{1,5},{5... | collective-permute-start | bytes 688136 | tf_op jit(solution)/shard_map/ppermute | solution.py:28
  14.7 1.0 %copy-start = (bf16[1024,256]{1,0:T(8,128)(2,1)S(1)}, bf16[1024,256]{1,0:T(8,128)(2,1)}, u32[]{:S(2)}) copy-start(bf16[1024,256]{1,0:T(8,128)(2,1)} %x_ref.1) | copy-start | bytes 1572868
  21.2 2.3 %collective-permute-start.6 = (bf16[448,256]{1,0:T(8,128)(2,1)S(1)}, bf16[448,256]{1,0:T(8,128)(2,1)S(1)}, u32[]{:S(2)}, u32[]{:S(2)}) collective-permute-start(bf16[448,256]{1,0:T(8,128)(2,1)S(1)} %collective-permute-done.4.refs_4_), channel_id=1, source_target_pairs={{0,1},{1,0},{2,3},{3,2},{4,5},{5,4},{6,7},{7,6},{8,9},{9,8},{10,11... | collective-permute-start | bytes 688136 | tf_op jit(solution)/shard_map/ppermute | solution.py:28
  24.7 3.7 %collective-permute-start.7 = (f32[16,128]{1,0:T(8,128)S(1)}, f32[16,128]{1,0:T(8,128)S(1)}, u32[]{:S(2)}, u32[]{:S(2)}) collective-permute-start(f32[16,128]{1,0:T(8,128)S(1)} %get-tuple-element.47.refs_2_), channel_id=1, source_target_pairs={{0,2},{1,3},{2,0},{3,1},{4,6},{5,7},{6,4},{7,5},{8,10},{9,11},{10,... | collective-permute-start | bytes 24584 | tf_op jit(solution)/shard_map/ppermute | solution.py:28

commit v11 on v10

--- a/solution.py
+++ b/solution.py
@@ -38,21 +38,29 @@
 
 
 def gather_column(message, column):
-    span = message.shape[0]
-    far = range(2, lax.axis_size("gen"), 2)
-    for k, mask in enumerate(far):
-        column = lax.dynamic_update_slice(column, swap(message, "gen", mask), ((k + 1) * span, 0))
-    return column, [0, *far]
-
-
-def pack_kernel(y_hbm_ref, g_hbm_ref, packed_ref, column_ref, own_g_ref, y_ref, g_ref, sems):
+    masks = [0]
+    bit = lax.axis_size("gen") // 2
+    while bit > 1:
+        held = message.shape[0]
+        other = swap(message, "gen", bit)
+        column = lax.dynamic_update_slice(column, other, (held, 0))
+        masks += [mask ^ bit for mask in masks]
+        bit //= 2
+        message = column[: 2 * held] if bit > 1 else column
+    return column, masks
+
+
+def pack_kernel(
+    y_hbm_ref, g_hbm_ref, x_hbm_ref, packed_ref, column_ref, own_g_ref, own_x_ref, y_ref, g_ref, sems
+):
     copies = [
         pltpu.make_async_copy(y_hbm_ref, y_ref, sems.at[0]),
         pltpu.make_async_copy(g_hbm_ref, g_ref, sems.at[1]),
+        pltpu.make_async_copy(x_hbm_ref, own_x_ref, sems.at[2]),
     ]
     for copy in copies:
         copy.start()
-    for copy in copies:
+    for copy in copies[:2]:
         copy.wait()
     share, width = y_ref.shape
     tall = packed_ref.shape[0] - TILE
@@ -75,6 +83,7 @@
     packed_ref[:share, :] = y
     packed_ref[tall:, :share] = pieces.astype(jnp.bfloat16)
     column_ref[: packed_ref.shape[0], :] = packed_ref[...]
+    copies[2].wait()
 
 
 def unpack(parts, share, y_ref, b_ref):
@@ -99,8 +108,7 @@
             k += 1
 
 
-def norm_kernel(x_ref, sq_ref, copy_ref):
-    copy_ref[...] = x_ref[...]
+def norm_kernel(x_ref, sq_ref):
     x = x_ref[...].astype(jnp.float32)
     square = x * x
     high = square.astype(jnp.bfloat16)
@@ -287,31 +295,31 @@
     tiles = rows // LANES
     span = round_up(share, TILE) + TILE
     own_g = data_potential.reshape(1, share)
-    message, column, held_g = pl.pallas_call(
+    message, column, held_g, held_x = pl.pallas_call(
         pack_kernel,
         out_shape=(
             jax.ShapeDtypeStruct((span, width), jnp.bfloat16),
             jax.ShapeDtypeStruct((span * (n_gen // 2), width), jnp.bfloat16),
             jax.ShapeDtypeStruct((1, share), jnp.float32),
+            jax.ShapeDtypeStruct((rows, width), gen_samples.dtype),
         ),
-        in_specs=[pl.BlockSpec(memory_space=pltpu.HBM)] * 2,
+        in_specs=[pl.BlockSpec(memory_space=pltpu.HBM)] * 3,
         scratch_shapes=[
             pltpu.VMEM((share, width), jnp.bfloat16),
             pltpu.VMEM((1, share), jnp.float32),
-            pltpu.SemaphoreType.DMA((2,)),
+            pltpu.SemaphoreType.DMA((3,)),
         ],
         compiler_params=pltpu.CompilerParams(vmem_limit_bytes=4 * MIB),
-    )(*[pltpu.with_memory_space_constraint(array, pltpu.HBM) for array in (data_samples, own_g)])
+    )(*[pltpu.with_memory_space_constraint(array, pltpu.HBM) for array in (data_samples, own_g, gen_samples)])
     xs, order = gather_gen(gen_samples)
     column, far = gather_column(message, column)
-    sq, xs[0] = pl.pallas_call(
+    xs[1:], xs[0] = lax.optimization_barrier((xs[1:], held_x))
+    sq = pl.pallas_call(
         norm_kernel,
-        out_shape=(
-            jax.ShapeDtypeStruct((tiles, LANES), jnp.float32),
-            jax.ShapeDtypeStruct((rows, width), gen_samples.dtype),
-        ),
+        out_shape=jax.ShapeDtypeStruct((tiles, LANES), jnp.float32),
         compiler_params=pltpu.CompilerParams(vmem_limit_bytes=8 * MIB),
-    )(gen_samples)
+        cost_estimate=pl.CostEstimate(flops=8 * rows * width * width, bytes_accessed=16 * MIB, transcendentals=0),
+    )(xs[0])
     tall = 64
 
     def cost(count):
@@ -352,9 +360,7 @@
     near = swap(column, "gen", 1)
     twin = swap(column, "dat", 1)
     log_own, held_own, data = row_pass(xs[:1], [column, twin])
-    near, log_own = lax.optimization_barrier((near, log_own))
     near_twin = swap(near, "dat", 1)
-    xs[1:], near = lax.optimization_barrier((xs[1:], near))
     log_others, held_others, _ = row_pass(xs[1:], [], unpacked=data)
     log, held_near, more = row_pass(xs, [near], [log_own, log_others])
     data = data + more

time: 47.7 us -> 48.7 us (1.021)
  blocking collectives: 11.6 us -> 13.1 us
  local copies, waits for them, and re-layouts: 1.06 us -> 0.02 us
    all_to_all x1, blocking collectives: 11.6 us -> 13.1 us  [per_device(): totals = lax.all_to_all(col, ('dat', 'gen'), 0, 0, tiled=True)]
    unnamed x2 -> x0, local copies, waits for them, and re-layouts: 1.04 us -> none
    ppermute x8 -> x7, waiting for transfers between devices: 10.2 us -> 10.6 us  [swap(): lax.ppermute(value, axis, [(k, k ^ mask) for k in range(lax.axis_size(axi...]
    ppermute x8 -> x7, starting transfers between devices: 10.4 us -> 10.5 us  [swap(): lax.ppermute(value, axis, [(k, k ^ mask) for k in range(lax.axis_size(axi...]
  transfers between devices with their start and end apart: 8 -> 7, of which waited for: 3 -> 4; matrix products, arithmetic and copies ran while one was open for 0% -> 0% of each run, Pallas kernels for 8% -> 8%
where the time goes in v11:
time: 48.7 us; the launch traced here: 48.5 us
  blocking collectives  13.1 us (27%)
  Pallas kernels  13 us (27%)
  waiting for transfers between devices  10.6 us (22%)
  starting transfers between devices  10.5 us (22%)
  between operations  0.67 us (1%)
  other arithmetic  0.61 us (1%)
    all_to_all x1, blocking collectives, per_device(): totals = lax.all_to_all(col, ('dat', 'gen'), 0, 0, tiled=True)  13.1 us
    ppermute x7, waiting for transfers between devices, swap(): lax.ppermute(value, axis, [(k, k ^ mask) for k in range(lax.axis_size(axi...  10.6 us
    ppermute x7, starting transfers between devices, swap(): lax.ppermute(value, axis, [(k, k ^ mask) for k in range(lax.axis_size(axi...  10.5 us
    pallas_call x1, Pallas kernels, per_device(): pl.pallas_call(functools.partial(column_kernel, count=len(xs), share=shar...  6.84 us
    pallas_call x4, Pallas kernels, row_pass(): pl.pallas_call(functools.partial(row_kernel, count=len(rows_of), share=sh...  4.64 us
    pallas_call x1, Pallas kernels, per_device(): pl.pallas_call(pack_kernel, out_shape=(jax.ShapeDtypeStruct((span, width)...  1.11 us
  transfers between devices with their start and end apart: 7, of which 4 were waited for; matrix products, arithmetic and copies ran while one was open for 0% of the time, Pallas kernels for 8%

profile of v11, /device:TPU:0, one launch (start us, length us, event | category | flops | bytes accessed | tf_op | source)
XLA Modules:
  0.0 48.5 jit_solution(10199748449205597270)
XLA Ops:
  0.6 1.1 %shard_map.50 = (bf16[112,256]{1,0:T(8,128)(2,1)S(1)}, bf16[448,256]{1,0:T(8,128)(2,1)S(1)}, f32[1,96]{1,0:T(1,128)S(1)}, bf16[1024,256]{1,0:T(8,128)(2,1)S(1)}) custom-call(bf16[96,256]{1,0:T(8,128)(2,1)} %y_hbm_ref.1, f32[1,96]{1,0:T(1,128)} %bitcast.12, bf16[1024,256]{1,0:T(8,128)(2,1)} %x_hbm_ref.1), custom_call_target="tpu_custom_call" | custom-call | tf_op jit(solution)/shard_map/pallas_call | solution.py:298
  1.8 4.1 %collective-permute-start.1 = (bf16[112,256]{1,0:T(8,128)(2,1)S(1)}, bf16[112,256]{1,0:T(8,128)(2,1)S(1)}, u32[]{:S(2)}, u32[]{:S(2)}) collective-permute-start(bf16[112,256]{1,0:T(8,128)(2,1)S(1)} %get-tuple-element.34), channel_id=1, source_target_pairs={{0,16},{4,20},{8,24},{12,28},{16,0},{20,4},{24,8},{28,12},{1,17},{... | collective-permute-start | bytes 172040 | tf_op jit(solution)/shard_map/ppermute | solution.py:28
  5.9 1.5 %collective-permute-start = (bf16[1024,256]{1,0:T(8,128)(2,1)}, bf16[1024,256]{1,0:T(8,128)(2,1)S(1)}, u32[]{:S(2)}, u32[]{:S(2)}) collective-permute-start(bf16[1024,256]{1,0:T(8,128)(2,1)} %x_hbm_ref.1), channel_id=1, source_target_pairs={{0,2},{1,3},{2,0},{3,1},{4,6},{5,7},{6,4},{7,5},{8,10},{9,11},{10,... | collective-permute-start | bytes 1572872 | tf_op jit(solution)/shard_map/ppermute | solution.py:28
  7.3 1.3 %collective-permute-done.1 = bf16[112,256]{1,0:T(8,128)(2,1)S(1)} collective-permute-done((bf16[112,256]{1,0:T(8,128)(2,1)S(1)}, bf16[112,256]{1,0:T(8,128)(2,1)S(1)}, u32[]{:S(2)}, u32[]{:S(2)}) %collective-permute-start.1) | collective-permute-done | bytes 57376 | tf_op jit(solution)/shard_map/ppermute | solution.py:28
  8.6 1.4 %collective-permute-start.2 = (bf16[224,256]{1,0:T(8,128)(2,1)S(1)}, bf16[224,256]{1,0:T(8,128)(2,1)S(1)}, u32[]{:S(2)}, u32[]{:S(2)}) collective-permute-start(bf16[224,256]{1,0:T(8,128)(2,1)S(1)} %slice.4), channel_id=1, source_target_pairs={{0,8},{4,12},{8,0},{12,4},{16,24},{20,28},{24,16},{28,20},{1,9},{5... | collective-permute-start | bytes 344072 | tf_op jit(solution)/shard_map/ppermute | solution.py:28
  10.0 3.5 %collective-permute-done.2 = bf16[224,256]{1,0:T(8,128)(2,1)S(1)} collective-permute-done((bf16[224,256]{1,0:T(8,128)(2,1)S(1)}, bf16[224,256]{1,0:T(8,128)(2,1)S(1)}, u32[]{:S(2)}, u32[]{:S(2)}) %collective-permute-start.2) | collective-permute-done | bytes 114720 | tf_op jit(solution)/shard_map/ppermute | solution.py:28
  13.5 1.8 %collective-permute-start.3 = (bf16[448,256]{1,0:T(8,128)(2,1)S(1)}, bf16[448,256]{1,0:T(8,128)(2,1)S(1)}, u32[]{:S(2)}, u32[]{:S(2)}) collective-permute-start(bf16[448,256]{1,0:T(8,128)(2,1)S(1)} %constant_dynamic-update-slice_fusion.refs_1_), channel_id=1, source_target_pairs={{0,4},{4,0},{8,12},{12,8},{16,20},{20,16},{24,28},{28,24},{1,5},{5... | collective-permute-start | bytes 688136 | tf_op jit(solution)/shard_map/ppermute | solution.py:28
  15.3 0.0 collective-permute-start.5
  15.3 4.3 %collective-permute-done.3.refs_4_ = bf16[448,256]{1,0:T(8,128)(2,1)S(1)} collective-permute-done((bf16[448,256]{1,0:T(8,128)(2,1)S(1)}, bf16[448,256]{1,0:T(8,128)(2,1)S(1)}, u32[]{:S(2)}, u32[]{:S(2)}) %collective-permute-start.3) | collective-permute-done | bytes 229408 | tf_op jit(solution)/shard_map/ppermute | solution.py:28
  19.6 0.0 collective-permute-start.4
  19.6 0.0 collective-permute-done.refs_0_.refs_1_
  19.6 0.0 collective-permute-done.5.refs_2_
  19.6 1.2 %shard_map.51 = (f32[8,128]{1,0:T(8,128)S(1)}, f32[8,128]{1,0:T(8,128)S(1)}, f32[2,768,512]{2,1,0:T(8,128)S(1)}, bf16[768,256]{1,0:T(8,128)(2,1)S(1)}, f32[768,128]{1,0:T(8,128)S(1)}) custom-call(bf16[1024,256]{1,0:T(8,128)(2,1)S(1)} %get-tuple-element.31.refs_0_.x_ref, bf16[448,256]{1,0:T(8,128)(2,1)S(1)} %constant_dynamic-update-slice_fusion.refs_1_, ...), custom_call_target="tpu_custom_call" | custom-call | flops 805306368 | bytes 1441792 | tf_op jit(solution)/shard_map/pallas_call | solution.py:339
  20.8 1.1 %shard_map.52 = (f32[8,128]{1,0:T(8,128)S(1)}, f32[8,128]{1,0:T(8,128)S(1)}, f32[2,768,512]{2,1,0:T(8,128)S(1)}) custom-call(bf16[1024,256]{1,0:T(8,128)(2,1)S(1)} %collective-permute-done.refs_0_.refs_1_, bf16[768,256]{1,0:T(8,128)(2,1)S(1)} %get-tuple-element.36.refs_1_.refs_13_, f32[768,128]{1,0:T(8,128)S(1)} %get-tuple-element.37.refs_2_.refs_14_), custom_call_target="tpu_custom_call" | custom-call | flops 805306368 | bytes 1441792 | tf_op jit(solution)/shard_map/pallas_call | solution.py:339
  21.9 1.2 %shard_map.53 = (f32[16,128]{1,0:T(8,128)S(1)}, f32[16,128]{1,0:T(8,128)S(1)}, f32[4,384,512]{2,1,0:T(8,128)S(1)}, bf16[384,256]{1,0:T(8,128)(2,1)S(1)}, f32[384,128]{1,0:T(8,128)S(1)}) custom-call(bf16[1024,256]{1,0:T(8,128)(2,1)S(1)} %get-tuple-element.31.refs_0_.x_ref, bf16[1024,256]{1,0:T(8,128)(2,1)S(1)} %collective-permute-done.refs_0_.refs_1_, ...), custom_call_target="tpu_custom_call" | custom-call | flops 402653184 | bytes 1245184 | tf_op jit(solution)/shard_map/pallas_call | solution.py:339
  23.1 0.0 collective-permute-done.4.refs_3_
  23.1 1.2 %shard_map.54 = (f32[16,128]{1,0:T(8,128)S(1)}, f32[16,128]{1,0:T(8,128)S(1)}, f32[4,384,512]{2,1,0:T(8,128)S(1)}, bf16[384,256]{1,0:T(8,128)(2,1)S(1)}, f32[384,128]{1,0:T(8,128)S(1)}) custom-call(bf16[1024,256]{1,0:T(8,128)(2,1)S(1)} %get-tuple-element.31.refs_0_.x_ref, bf16[1024,256]{1,0:T(8,128)(2,1)S(1)} %collective-permute-done.refs_0_.refs_1_, ...), custom_call_target="tpu_custom_call" | custom-call | flops 402653184 | bytes 1245184 | tf_op jit(solution)/shard_map/pallas_call | solution.py:339
  24.3 1.8 %collective-permute-start.6 = (f32[16,128]{1,0:T(8,128)S(1)}, f32[16,128]{1,0:T(8,128)S(1)}, u32[]{:S(2)}, u32[]{:S(2)}) collective-permute-start(f32[16,128]{1,0:T(8,128)S(1)} %get-tuple-element.42.refs_2_), channel_id=1, source_target_pairs={{0,2},{1,3},{2,0},{3,1},{4,6},{5,7},{6,4},{7,5},{8,10},{9,11},{10,... | collective-permute-start | bytes 24584 | tf_op jit(solution)/shard_map/ppermute | solution.py:28
  26.0 0.4 shard_map.55.refs_4_
  26.4 1.5 %collective-permute-done.6.refs_3_ = f32[16,128]{1,0:T(8,128)S(1)} collective-permute-done((f32[16,128]{1,0:T(8,128)S(1)}, f32[16,128]{1,0:T(8,128)S(1)}, u32[]{:S(2)}, u32[]{:S(2)}) %collective-permute-start.6) | collective-permute-done | bytes 8224 | tf_op jit(solution)/shard_map/ppermute | solution.py:28
  28.0 6.8 %shard_map.56 = (f32[8,128]{1,0:T(8,128)}, f32[32,96]{1,0:T(8,128)S(1)}) custom-call(bf16[1024,256]{1,0:T(8,128)(2,1)S(1)} %get-tuple-element.31.refs_0_.x_ref, bf16[1024,256]{1,0:T(8,128)(2,1)S(1)} %collective-permute-done.refs_0_.refs_1_, f32[16,128]{1,0:T(8,128)S(1)} %get-tuple-element.42.refs_2_, f32[16,128]{1,0:T(8,128)S(1)} %collective-permute-done.6.refs_3_, ...), custom_call_target="tpu_custom_call" | custom-call | flops 1610612736 | bytes 1835008 | tf_op jit(solution)/shard_map/pallas_call | solution.py:376
  34.8 13.1 %all_to_all.12 = f32[32,1,96]{2,1,0:T(1,128)S(1)} all-to-all(f32[32,1,96]{2,1,0:T(1,128)S(1)} %bitcast.10), channel_id=1, replica_groups=mesh['gen'=8,'dat'=4] {'dat','gen'}, dimensions={0} | all-to-all | bytes 24576 | tf_op jit(solution)/shard_map/all_to_all | solution.py:400
  47.9 0.1 reduce_max.9
  48.0 0.5 %fusion = f32[96]{0:T(128)} fusion(f32[1,96]{1,0:T(1,128)S(1)} %get-tuple-element.56, f32[96]{0:T(128)S(1)} %reduce_max.9, f32[96]{0:T(128)S(1)} %exponential_reduce_fusion), kind=kLoop, calls=%fused_computation.4 | loop fusion | flops 480 | bytes 1536 | tf_op jit(solution)/shard_map/add | solution.py:403
  (4 shorter events, 0.1 us)
Async XLA Ops:
  1.8 6.9 %collective-permute-start.1 = (bf16[112,256]{1,0:T(8,128)(2,1)S(1)}, bf16[112,256]{1,0:T(8,128)(2,1)S(1)}, u32[]{:S(2)}, u32[]{:S(2)}) collective-permute-start(bf16[112,256]{1,0:T(8,128)(2,1)S(1)} %get-tuple-element.34), channel_id=1, source_target_pairs={{0,16},{4,20},{8,24},{12,28},{16,0},{20,4},{24,8},{28,12},{1,17},{... | collective-permute-start | bytes 172040 | tf_op jit(solution)/shard_map/ppermute | solution.py:28
  5.9 13.8 %collective-permute-start = (bf16[1024,256]{1,0:T(8,128)(2,1)}, bf16[1024,256]{1,0:T(8,128)(2,1)S(1)}, u32[]{:S(2)}, u32[]{:S(2)}) collective-permute-start(bf16[1024,256]{1,0:T(8,128)(2,1)} %x_hbm_ref.1), channel_id=1, source_target_pairs={{0,2},{1,3},{2,0},{3,1},{4,6},{5,7},{6,4},{7,5},{8,10},{9,11},{10,... | collective-permute-start | bytes 1572872 | tf_op jit(solution)/shard_map/ppermute | solution.py:28
  8.6 4.9 %collective-permute-start.2 = (bf16[224,256]{1,0:T(8,128)(2,1)S(1)}, bf16[224,256]{1,0:T(8,128)(2,1)S(1)}, u32[]{:S(2)}, u32[]{:S(2)}) collective-permute-start(bf16[224,256]{1,0:T(8,128)(2,1)S(1)} %slice.4), channel_id=1, source_target_pairs={{0,8},{4,12},{8,0},{12,4},{16,24},{20,28},{24,16},{28,20},{1,9},{5... | collective-permute-start | bytes 344072 | tf_op jit(solution)/shard_map/ppermute | solution.py:28
  13.5 6.1 %collective-permute-start.3 = (bf16[448,256]{1,0:T(8,128)(2,1)S(1)}, bf16[448,256]{1,0:T(8,128)(2,1)S(1)}, u32[]{:S(2)}, u32[]{:S(2)}) collective-permute-start(bf16[448,256]{1,0:T(8,128)(2,1)S(1)} %constant_dynamic-update-slice_fusion.refs_1_), channel_id=1, source_target_pairs={{0,4},{4,0},{8,12},{12,8},{16,20},{20,16},{24,28},{28,24},{1,5},{5... | collective-permute-start | bytes 688136 | tf_op jit(solution)/shard_map/ppermute | solution.py:28
  15.3 4.3 %collective-permute-start.5 = (bf16[448,256]{1,0:T(8,128)(2,1)S(1)}, bf16[448,256]{1,0:T(8,128)(2,1)S(1)}, u32[]{:S(2)}, u32[]{:S(2)}) collective-permute-start(bf16[448,256]{1,0:T(8,128)(2,1)S(1)} %constant_dynamic-update-slice_fusion.refs_1_), channel_id=1, source_target_pairs={{0,1},{1,0},{2,3},{3,2},{4,5},{5,4},{6,7},{7,6},{8,9},{9,8},{10,11... | collective-permute-start | bytes 688136 | tf_op jit(solution)/shard_map/ppermute | solution.py:28
  19.6 3.5 %collective-permute-start.4 = (bf16[448,256]{1,0:T(8,128)(2,1)S(1)}, bf16[448,256]{1,0:T(8,128)(2,1)S(1)}, u32[]{:S(2)}, u32[]{:S(2)}) collective-permute-start(bf16[448,256]{1,0:T(8,128)(2,1)S(1)} %collective-permute-done.3.refs_4_), channel_id=1, source_target_pairs={{0,1},{1,0},{2,3},{3,2},{4,5},{5,4},{6,7},{7,6},{8,9},{9,8},{10,11... | collective-permute-start | bytes 688136 | tf_op jit(solution)/shard_map/ppermute | solution.py:28
  24.3 3.7 %collective-permute-start.6 = (f32[16,128]{1,0:T(8,128)S(1)}, f32[16,128]{1,0:T(8,128)S(1)}, u32[]{:S(2)}, u32[]{:S(2)}) collective-permute-start(f32[16,128]{1,0:T(8,128)S(1)} %get-tuple-element.42.refs_2_), channel_id=1, source_target_pairs={{0,2},{1,3},{2,0},{3,1},{4,6},{5,7},{6,4},{7,5},{8,10},{9,11},{10,... | collective-permute-start | bytes 24584 | tf_op jit(solution)/shard_map/ppermute | solution.py:28

commit v12 on v11

--- a/solution.py
+++ b/solution.py
@@ -38,16 +38,11 @@
 
 
 def gather_column(message, column):
-    masks = [0]
-    bit = lax.axis_size("gen") // 2
-    while bit > 1:
-        held = message.shape[0]
-        other = swap(message, "gen", bit)
-        column = lax.dynamic_update_slice(column, other, (held, 0))
-        masks += [mask ^ bit for mask in masks]
-        bit //= 2
-        message = column[: 2 * held] if bit > 1 else column
-    return column, masks
+    span = message.shape[0]
+    far = range(2, lax.axis_size("gen"), 2)
+    for k, mask in enumerate(far):
+        column = lax.dynamic_update_slice(column, swap(message, "gen", mask), ((k + 1) * span, 0))
+    return column, [0, *far]
 
 
 def pack_kernel(
@@ -313,13 +308,15 @@
     )(*[pltpu.with_memory_space_constraint(array, pltpu.HBM) for array in (data_samples, own_g, gen_samples)])
     xs, order = gather_gen(gen_samples)
     column, far = gather_column(message, column)
-    xs[1:], xs[0] = lax.optimization_barrier((xs[1:], held_x))
+    xs[0] = held_x
+    xs[1:], norm_x = lax.optimization_barrier((xs[1:], held_x))
     sq = pl.pallas_call(
         norm_kernel,
         out_shape=jax.ShapeDtypeStruct((tiles, LANES), jnp.float32),
         compiler_params=pltpu.CompilerParams(vmem_limit_bytes=8 * MIB),
-        cost_estimate=pl.CostEstimate(flops=8 * rows * width * width, bytes_accessed=16 * MIB, transcendentals=0),
-    )(xs[0])
+        cost_estimate=pl.CostEstimate(flops=8 * rows * width * width, bytes_accessed=4 * MIB, transcendentals=0),
+    )(norm_x)
+    xs[1:], sq = lax.optimization_barrier((xs[1:], sq))
     tall = 64
 
     def cost(count):
@@ -359,17 +356,19 @@
 
     near = swap(column, "gen", 1)
     twin = swap(column, "dat", 1)
-    log_own, held_own, data = row_pass(xs[:1], [column, twin])
+    log_own, held_own, data = row_pass(xs[:1], [column])
+    near, log_own = lax.optimization_barrier((near, log_own))
     near_twin = swap(near, "dat", 1)
+    twin, near = lax.optimization_barrier((twin, near))
     log_others, held_others, _ = row_pass(xs[1:], [], unpacked=data)
-    log, held_near, more = row_pass(xs, [near], [log_own, log_others])
+    log, held_both, more = row_pass(xs, [near, twin], [log_own, log_others])
     data = data + more
     near_twin, log = lax.optimization_barrier((near_twin, log))
     log, held_last, more = row_pass(xs, [near_twin], [log])
     data = data + more
-    held = held_own + held_others + held_near + held_last
+    held = held_own + held_others + held_both + held_last
     segments = [[0, 1], [0], [0]]
-    masks = [(g ^ a, b) for a in (0, 1) for b in (0, 1) for g in far]
+    masks = [(g ^ a, b) for a, b in ((0, 0), (1, 0), (0, 1), (1, 1)) for g in far]
     logs = [log]
     logs += [swap(logs[0], "dat", m) for m in order[1:]]
     orders = [[order.index(m ^ partner) for m in order] for partner in order]

time: 48.7 us -> 47.5 us (0.975)
  blocking collectives: 13.1 us -> 11.1 us
  waiting for transfers between devices: 10.6 us -> 12.4 us
  starting transfers between devices: 10.5 us -> 9.47 us
    all_to_all x1, blocking collectives: 13.1 us -> 11.1 us  [per_device(): totals = lax.all_to_all(col, ('dat', 'gen'), 0, 0, tiled=True)]
    ppermute x7 -> x8, waiting for transfers between devices: 10.6 us -> 12.4 us  [swap(): lax.ppermute(value, axis, [(k, k ^ mask) for k in range(lax.axis_size(axi...]
    ppermute x7 -> x8, starting transfers between devices: 10.5 us -> 9.47 us  [swap(): lax.ppermute(value, axis, [(k, k ^ mask) for k in range(lax.axis_size(axi...]
  transfers between devices with their start and end apart: 7 -> 8, of which waited for: 4 -> 3; matrix products, arithmetic and copies ran while one was open for 0% -> 0% of each run, Pallas kernels for 8% -> 8%
where the time goes in v12:
time: 47.5 us; the launch traced here: 47.4 us
  Pallas kernels  13.1 us (28%)
  waiting for transfers between devices  12.4 us (26%)
  blocking collectives  11.1 us (23%)
  starting transfers between devices  9.47 us (20%)
  between operations  0.68 us (1%)
  other arithmetic  0.61 us (1%)
    ppermute x8, waiting for transfers between devices, swap(): lax.ppermute(value, axis, [(k, k ^ mask) for k in range(lax.axis_size(axi...  12.4 us
    all_to_all x1, blocking collectives, per_device(): totals = lax.all_to_all(col, ('dat', 'gen'), 0, 0, tiled=True)  11.1 us
    ppermute x8, starting transfers between devices, swap(): lax.ppermute(value, axis, [(k, k ^ mask) for k in range(lax.axis_size(axi...  9.47 us
    pallas_call x1, Pallas kernels, per_device(): pl.pallas_call(functools.partial(column_kernel, count=len(xs), share=shar...  6.9 us
    pallas_call x4, Pallas kernels, row_pass(): pl.pallas_call(functools.partial(row_kernel, count=len(rows_of), share=sh...  4.65 us
    pallas_call x1, Pallas kernels, per_device(): pl.pallas_call(pack_kernel, out_shape=(jax.ShapeDtypeStruct((span, width)...  1.11 us
  transfers between devices with their start and end apart: 8, of which 3 were waited for; matrix products, arithmetic and copies ran while one was open for 0% of the time, Pallas kernels for 8%

profile of v12, /device:TPU:0, one launch (start us, length us, event | category | flops | bytes accessed | tf_op | source)
XLA Modules:
  0.0 47.4 jit_solution(4831165571839877118)
XLA Ops:
  0.6 1.1 %shard_map.50 = (bf16[112,256]{1,0:T(8,128)(2,1)S(1)}, bf16[448,256]{1,0:T(8,128)(2,1)S(1)}, f32[1,96]{1,0:T(1,128)S(1)}, bf16[1024,256]{1,0:T(8,128)(2,1)S(1)}) custom-call(bf16[96,256]{1,0:T(8,128)(2,1)} %y_hbm_ref.1, f32[1,96]{1,0:T(1,128)} %bitcast.12, bf16[1024,256]{1,0:T(8,128)(2,1)} %x_hbm_ref.1), custom_call_target="tpu_custom_call" | custom-call | tf_op jit(solution)/shard_map/pallas_call | solution.py:293
  1.8 3.1 %collective-permute-start.1 = (bf16[112,256]{1,0:T(8,128)(2,1)S(1)}, bf16[112,256]{1,0:T(8,128)(2,1)S(1)}, u32[]{:S(2)}, u32[]{:S(2)}) collective-permute-start(bf16[112,256]{1,0:T(8,128)(2,1)S(1)} %get-tuple-element.41), channel_id=1, source_target_pairs={{0,8},{4,12},{8,0},{12,4},{16,24},{20,28},{24,16},{28,20},{1,9},{5... | collective-permute-start | bytes 172040 | tf_op jit(solution)/shard_map/ppermute | solution.py:28
  4.8 1.5 %collective-permute-start = (bf16[1024,256]{1,0:T(8,128)(2,1)}, bf16[1024,256]{1,0:T(8,128)(2,1)S(1)}, u32[]{:S(2)}, u32[]{:S(2)}) collective-permute-start(bf16[1024,256]{1,0:T(8,128)(2,1)} %x_hbm_ref.1), channel_id=1, source_target_pairs={{0,2},{1,3},{2,0},{3,1},{4,6},{5,7},{6,4},{7,5},{8,10},{9,11},{10,... | collective-permute-start | bytes 1572872 | tf_op jit(solution)/shard_map/ppermute | solution.py:28
  6.3 2.5 %collective-permute-start.3 = (bf16[112,256]{1,0:T(8,128)(2,1)S(1)}, bf16[112,256]{1,0:T(8,128)(2,1)S(1)}, u32[]{:S(2)}, u32[]{:S(2)}) collective-permute-start(bf16[112,256]{1,0:T(8,128)(2,1)S(1)} %get-tuple-element.41), channel_id=1, source_target_pairs={{0,24},{4,28},{8,16},{12,20},{16,8},{20,12},{24,0},{28,4},{1,25},{... | collective-permute-start | bytes 172040 | tf_op jit(solution)/shard_map/ppermute | solution.py:28
  8.8 0.1 collective-permute-start.2
  8.9 0.0 collective-permute-done.1
  8.9 5.6 %collective-permute-done.2 = bf16[112,256]{1,0:T(8,128)(2,1)S(1)} collective-permute-done((bf16[112,256]{1,0:T(8,128)(2,1)S(1)}, bf16[112,256]{1,0:T(8,128)(2,1)S(1)}, u32[]{:S(2)}, u32[]{:S(2)}) %collective-permute-start.2) | collective-permute-done | bytes 57376 | tf_op jit(solution)/shard_map/ppermute | solution.py:28
  14.5 0.0 collective-permute-done.3
  14.5 1.6 %collective-permute-start.4 = (bf16[448,256]{1,0:T(8,128)(2,1)S(1)}, bf16[448,256]{1,0:T(8,128)(2,1)S(1)}, u32[]{:S(2)}, u32[]{:S(2)}) collective-permute-start(bf16[448,256]{1,0:T(8,128)(2,1)S(1)} %constant_dynamic-update-slice_fusion.refs_1_), channel_id=1, source_target_pairs={{0,4},{4,0},{8,12},{12,8},{16,20},{20,16},{24,28},{28,24},{1,5},{5... | collective-permute-start | bytes 688136 | tf_op jit(solution)/shard_map/ppermute | solution.py:28
  16.1 0.0 collective-permute-start.6
  16.1 0.7 %shard_map.52 = (f32[8,128]{1,0:T(8,128)S(1)}, f32[8,128]{1,0:T(8,128)S(1)}, f32[2,384,512]{2,1,0:T(8,128)S(1)}, bf16[384,256]{1,0:T(8,128)(2,1)S(1)}, f32[384,128]{1,0:T(8,128)S(1)}) custom-call(bf16[1024,256]{1,0:T(8,128)(2,1)S(1)} %get-tuple-element.38.x_ref.refs_0_, bf16[448,256]{1,0:T(8,128)(2,1)S(1)} %constant_dynamic-update-slice_fusion.refs_1_), custom_call_target="tpu_custom_call" | custom-call | flops 402653184 | bytes 1245184 | tf_op jit(solution)/shard_map/pallas_call | solution.py:336
  16.8 3.8 %collective-permute-done.4.refs_4_ = bf16[448,256]{1,0:T(8,128)(2,1)S(1)} collective-permute-done((bf16[448,256]{1,0:T(8,128)(2,1)S(1)}, bf16[448,256]{1,0:T(8,128)(2,1)S(1)}, u32[]{:S(2)}, u32[]{:S(2)}) %collective-permute-start.4) | collective-permute-done | bytes 229408 | tf_op jit(solution)/shard_map/ppermute | solution.py:28
  20.6 0.0 collective-permute-start.5
  20.6 0.0 collective-permute-done.6.refs_5_
  20.6 0.0 collective-permute-done.refs_0_.refs_1_
  20.6 0.4 shard_map.51.refs_4_
  21.0 0.7 %shard_map.53 = (f32[8,128]{1,0:T(8,128)S(1)}, f32[8,128]{1,0:T(8,128)S(1)}, f32[2,384,512]{2,1,0:T(8,128)S(1)}) custom-call(bf16[1024,256]{1,0:T(8,128)(2,1)S(1)} %collective-permute-done.refs_0_.refs_1_, bf16[384,256]{1,0:T(8,128)(2,1)S(1)} %get-tuple-element.45.refs_1_.refs_13_, f32[384,128]{1,0:T(8,128)S(1)} %get-tuple-element.46.refs_2_.refs_14_), custom_call_target="tpu_custom_call" | custom-call | flops 402653184 | bytes 1245184 | tf_op jit(solution)/shard_map/pallas_call | solution.py:336
  21.7 2.1 %shard_map.54 = (f32[16,128]{1,0:T(8,128)S(1)}, f32[16,128]{1,0:T(8,128)S(1)}, f32[4,768,512]{2,1,0:T(8,128)S(1)}, bf16[768,256]{1,0:T(8,128)(2,1)S(1)}, f32[768,128]{1,0:T(8,128)S(1)}) custom-call(bf16[1024,256]{1,0:T(8,128)(2,1)S(1)} %get-tuple-element.38.x_ref.refs_0_, bf16[1024,256]{1,0:T(8,128)(2,1)S(1)} %collective-permute-done.refs_0_.refs_1_, ...), custom_call_target="tpu_custom_call" | custom-call | flops 805306368 | bytes 1441792 | tf_op jit(solution)/shard_map/pallas_call | solution.py:336
  23.8 0.0 collective-permute-done.5.refs_3_
  23.8 1.2 %shard_map.55 = (f32[16,128]{1,0:T(8,128)S(1)}, f32[16,128]{1,0:T(8,128)S(1)}, f32[4,384,512]{2,1,0:T(8,128)S(1)}, bf16[384,256]{1,0:T(8,128)(2,1)S(1)}, f32[384,128]{1,0:T(8,128)S(1)}) custom-call(bf16[1024,256]{1,0:T(8,128)(2,1)S(1)} %get-tuple-element.38.x_ref.refs_0_, bf16[1024,256]{1,0:T(8,128)(2,1)S(1)} %collective-permute-done.refs_0_.refs_1_, ...), custom_call_target="tpu_custom_call" | custom-call | flops 402653184 | bytes 1245184 | tf_op jit(solution)/shard_map/pallas_call | solution.py:336
  25.0 0.7 %collective-permute-start.7 = (f32[16,128]{1,0:T(8,128)S(1)}, f32[16,128]{1,0:T(8,128)S(1)}, u32[]{:S(2)}, u32[]{:S(2)}) collective-permute-start(f32[16,128]{1,0:T(8,128)S(1)} %get-tuple-element.53.refs_2_), channel_id=1, source_target_pairs={{0,2},{1,3},{2,0},{3,1},{4,6},{5,7},{6,4},{7,5},{8,10},{9,11},{10,... | collective-permute-start | bytes 24584 | tf_op jit(solution)/shard_map/ppermute | solution.py:28
  25.7 3.0 %collective-permute-done.7.refs_3_ = f32[16,128]{1,0:T(8,128)S(1)} collective-permute-done((f32[16,128]{1,0:T(8,128)S(1)}, f32[16,128]{1,0:T(8,128)S(1)}, u32[]{:S(2)}, u32[]{:S(2)}) %collective-permute-start.7) | collective-permute-done | bytes 8224 | tf_op jit(solution)/shard_map/ppermute | solution.py:28
  28.7 6.9 %shard_map.56 = (f32[8,128]{1,0:T(8,128)}, f32[32,96]{1,0:T(8,128)S(1)}) custom-call(bf16[1024,256]{1,0:T(8,128)(2,1)S(1)} %get-tuple-element.38.x_ref.refs_0_, bf16[1024,256]{1,0:T(8,128)(2,1)S(1)} %collective-permute-done.refs_0_.refs_1_, f32[16,128]{1,0:T(8,128)S(1)} %get-tuple-element.53.refs_2_, f32[16,128]{1,0:T(8,128)S(1)} %collective-permute-done.7.refs_3_, ...), custom_call_target="tpu_custom_call" | custom-call | flops 1610612736 | bytes 1835008 | tf_op jit(solution)/shard_map/pallas_call | solution.py:375
  35.6 11.1 %all_to_all.12 = f32[32,1,96]{2,1,0:T(1,128)S(1)} all-to-all(f32[32,1,96]{2,1,0:T(1,128)S(1)} %bitcast.10), channel_id=1, replica_groups=mesh['gen'=8,'dat'=4] {'dat','gen'}, dimensions={0} | all-to-all | bytes 24576 | tf_op jit(solution)/shard_map/all_to_all | solution.py:399
  46.8 0.1 reduce_max.9
  46.9 0.5 %fusion = f32[96]{0:T(128)} fusion(f32[1,96]{1,0:T(1,128)S(1)} %get-tuple-element.68, f32[96]{0:T(128)S(1)} %reduce_max.9, f32[96]{0:T(128)S(1)} %exponential_reduce_fusion), kind=kLoop, calls=%fused_computation.5 | loop fusion | flops 480 | bytes 1536 | tf_op jit(solution)/shard_map/add | solution.py:402
  (4 shorter events, 0.0 us)
Async XLA Ops:
  1.8 7.2 %collective-permute-start.1 = (bf16[112,256]{1,0:T(8,128)(2,1)S(1)}, bf16[112,256]{1,0:T(8,128)(2,1)S(1)}, u32[]{:S(2)}, u32[]{:S(2)}) collective-permute-start(bf16[112,256]{1,0:T(8,128)(2,1)S(1)} %get-tuple-element.41), channel_id=1, source_target_pairs={{0,8},{4,12},{8,0},{12,4},{16,24},{20,28},{24,16},{28,20},{1,9},{5... | collective-permute-start | bytes 172040 | tf_op jit(solution)/shard_map/ppermute | solution.py:28
  4.8 15.8 %collective-permute-start = (bf16[1024,256]{1,0:T(8,128)(2,1)}, bf16[1024,256]{1,0:T(8,128)(2,1)S(1)}, u32[]{:S(2)}, u32[]{:S(2)}) collective-permute-start(bf16[1024,256]{1,0:T(8,128)(2,1)} %x_hbm_ref.1), channel_id=1, source_target_pairs={{0,2},{1,3},{2,0},{3,1},{4,6},{5,7},{6,4},{7,5},{8,10},{9,11},{10,... | collective-permute-start | bytes 1572872 | tf_op jit(solution)/shard_map/ppermute | solution.py:28
  6.3 8.2 %collective-permute-start.3 = (bf16[112,256]{1,0:T(8,128)(2,1)S(1)}, bf16[112,256]{1,0:T(8,128)(2,1)S(1)}, u32[]{:S(2)}, u32[]{:S(2)}) collective-permute-start(bf16[112,256]{1,0:T(8,128)(2,1)S(1)} %get-tuple-element.41), channel_id=1, source_target_pairs={{0,24},{4,28},{8,16},{12,20},{16,8},{20,12},{24,0},{28,4},{1,25},{... | collective-permute-start | bytes 172040 | tf_op jit(solution)/shard_map/ppermute | solution.py:28
  8.8 5.7 %collective-permute-start.2 = (bf16[112,256]{1,0:T(8,128)(2,1)S(1)}, bf16[112,256]{1,0:T(8,128)(2,1)S(1)}, u32[]{:S(2)}, u32[]{:S(2)}) collective-permute-start(bf16[112,256]{1,0:T(8,128)(2,1)S(1)} %get-tuple-element.41), channel_id=1, source_target_pairs={{0,16},{4,20},{8,24},{12,28},{16,0},{20,4},{24,8},{28,12},{1,17},{... | collective-permute-start | bytes 172040 | tf_op jit(solution)/shard_map/ppermute | solution.py:28
  14.5 6.1 %collective-permute-start.4 = (bf16[448,256]{1,0:T(8,128)(2,1)S(1)}, bf16[448,256]{1,0:T(8,128)(2,1)S(1)}, u32[]{:S(2)}, u32[]{:S(2)}) collective-permute-start(bf16[448,256]{1,0:T(8,128)(2,1)S(1)} %constant_dynamic-update-slice_fusion.refs_1_), channel_id=1, source_target_pairs={{0,4},{4,0},{8,12},{12,8},{16,20},{20,16},{24,28},{28,24},{1,5},{5... | collective-permute-start | bytes 688136 | tf_op jit(solution)/shard_map/ppermute | solution.py:28
  16.1 4.5 %collective-permute-start.6 = (bf16[448,256]{1,0:T(8,128)(2,1)S(1)}, bf16[448,256]{1,0:T(8,128)(2,1)S(1)}, u32[]{:S(2)}, u32[]{:S(2)}) collective-permute-start(bf16[448,256]{1,0:T(8,128)(2,1)S(1)} %constant_dynamic-update-slice_fusion.refs_1_), channel_id=1, source_target_pairs={{0,1},{1,0},{2,3},{3,2},{4,5},{5,4},{6,7},{7,6},{8,9},{9,8},{10,11... | collective-permute-start | bytes 688136 | tf_op jit(solution)/shard_map/ppermute | solution.py:28
  20.6 3.2 %collective-permute-start.5 = (bf16[448,256]{1,0:T(8,128)(2,1)S(1)}, bf16[448,256]{1,0:T(8,128)(2,1)S(1)}, u32[]{:S(2)}, u32[]{:S(2)}) collective-permute-start(bf16[448,256]{1,0:T(8,128)(2,1)S(1)} %collective-permute-done.4.refs_4_), channel_id=1, source_target_pairs={{0,1},{1,0},{2,3},{3,2},{4,5},{5,4},{6,7},{7,6},{8,9},{9,8},{10,11... | collective-permute-start | bytes 688136 | tf_op jit(solution)/shard_map/ppermute | solution.py:28
  25.0 3.7 %collective-permute-start.7 = (f32[16,128]{1,0:T(8,128)S(1)}, f32[16,128]{1,0:T(8,128)S(1)}, u32[]{:S(2)}, u32[]{:S(2)}) collective-permute-start(f32[16,128]{1,0:T(8,128)S(1)} %get-tuple-element.53.refs_2_), channel_id=1, source_target_pairs={{0,2},{1,3},{2,0},{3,1},{4,6},{5,7},{6,4},{7,5},{8,10},{9,11},{10,... | collective-permute-start | bytes 24584 | tf_op jit(solution)/shard_map/ppermute | solution.py:28

commit v13 on v12

--- a/solution.py
+++ b/solution.py
@@ -357,10 +357,10 @@
     near = swap(column, "gen", 1)
     twin = swap(column, "dat", 1)
     log_own, held_own, data = row_pass(xs[:1], [column])
-    near, log_own = lax.optimization_barrier((near, log_own))
+    log_others, held_others, _ = row_pass(xs[1:], [], unpacked=data)
+    near, log_own, log_others = lax.optimization_barrier((near, log_own, log_others))
     near_twin = swap(near, "dat", 1)
     twin, near = lax.optimization_barrier((twin, near))
-    log_others, held_others, _ = row_pass(xs[1:], [], unpacked=data)
     log, held_both, more = row_pass(xs, [near, twin], [log_own, log_others])
     data = data + more
     near_twin, log = lax.optimization_barrier((near_twin, log))

time: 47.5 us -> 46.4 us (0.977)
  waiting for transfers between devices: 12.4 us -> 11.3 us
    ppermute x8, waiting for transfers between devices: 12.4 us -> 11.3 us  [swap(): lax.ppermute(value, axis, [(k, k ^ mask) for k in range(lax.axis_size(axi...]
  transfers between devices with their start and end apart: 8 -> 8, of which waited for: 3 -> 4; matrix products, arithmetic and copies ran while one was open for 0% -> 0% of each run, Pallas kernels for 8% -> 8%
where the time goes in v13:
time: 46.4 us; the launch traced here: 46.3 us
  Pallas kernels  13.1 us (28%)
  waiting for transfers between devices  11.3 us (24%)
  blocking collectives  11.1 us (24%)
  starting transfers between devices  9.48 us (20%)
  between operations  0.67 us (1%)
  other arithmetic  0.61 us (1%)
    ppermute x8, waiting for transfers between devices, swap(): lax.ppermute(value, axis, [(k, k ^ mask) for k in range(lax.axis_size(axi...  11.3 us
    all_to_all x1, blocking collectives, per_device(): totals = lax.all_to_all(col, ('dat', 'gen'), 0, 0, tiled=True)  11.1 us
    ppermute x8, starting transfers between devices, swap(): lax.ppermute(value, axis, [(k, k ^ mask) for k in range(lax.axis_size(axi...  9.48 us
    pallas_call x1, Pallas kernels, per_device(): pl.pallas_call(functools.partial(column_kernel, count=len(xs), share=shar...  6.9 us
    pallas_call x4, Pallas kernels, row_pass(): pl.pallas_call(functools.partial(row_kernel, count=len(rows_of), share=sh...  4.64 us
    pallas_call x1, Pallas kernels, per_device(): pl.pallas_call(pack_kernel, out_shape=(jax.ShapeDtypeStruct((span, width)...  1.11 us
  transfers between devices with their start and end apart: 8, of which 4 were waited for; matrix products, arithmetic and copies ran while one was open for 0% of the time, Pallas kernels for 8%

profile of v13, /device:TPU:0, one launch (start us, length us, event | category | flops | bytes accessed | tf_op | source)
XLA Modules:
  0.0 46.3 jit_solution(16866573218829672277)
XLA Ops:
  0.6 1.1 %shard_map.50 = (bf16[112,256]{1,0:T(8,128)(2,1)S(1)}, bf16[448,256]{1,0:T(8,128)(2,1)S(1)}, f32[1,96]{1,0:T(1,128)S(1)}, bf16[1024,256]{1,0:T(8,128)(2,1)S(1)}) custom-call(bf16[96,256]{1,0:T(8,128)(2,1)} %y_hbm_ref.1, f32[1,96]{1,0:T(1,128)} %bitcast.12, bf16[1024,256]{1,0:T(8,128)(2,1)} %x_hbm_ref.1), custom_call_target="tpu_custom_call" | custom-call | tf_op jit(solution)/shard_map/pallas_call | solution.py:293
  1.8 3.1 %collective-permute-start.1 = (bf16[112,256]{1,0:T(8,128)(2,1)S(1)}, bf16[112,256]{1,0:T(8,128)(2,1)S(1)}, u32[]{:S(2)}, u32[]{:S(2)}) collective-permute-start(bf16[112,256]{1,0:T(8,128)(2,1)S(1)} %get-tuple-element.42), channel_id=1, source_target_pairs={{0,8},{4,12},{8,0},{12,4},{16,24},{20,28},{24,16},{28,20},{1,9},{5... | collective-permute-start | bytes 172040 | tf_op jit(solution)/shard_map/ppermute | solution.py:28
  4.8 1.5 %collective-permute-start = (bf16[1024,256]{1,0:T(8,128)(2,1)}, bf16[1024,256]{1,0:T(8,128)(2,1)S(1)}, u32[]{:S(2)}, u32[]{:S(2)}) collective-permute-start(bf16[1024,256]{1,0:T(8,128)(2,1)} %x_hbm_ref.1), channel_id=1, source_target_pairs={{0,2},{1,3},{2,0},{3,1},{4,6},{5,7},{6,4},{7,5},{8,10},{9,11},{10,... | collective-permute-start | bytes 1572872 | tf_op jit(solution)/shard_map/ppermute | solution.py:28
  6.3 2.5 %collective-permute-start.3 = (bf16[112,256]{1,0:T(8,128)(2,1)S(1)}, bf16[112,256]{1,0:T(8,128)(2,1)S(1)}, u32[]{:S(2)}, u32[]{:S(2)}) collective-permute-start(bf16[112,256]{1,0:T(8,128)(2,1)S(1)} %get-tuple-element.42), channel_id=1, source_target_pairs={{0,24},{4,28},{8,16},{12,20},{16,8},{20,12},{24,0},{28,4},{1,25},{... | collective-permute-start | bytes 172040 | tf_op jit(solution)/shard_map/ppermute | solution.py:28
  8.8 0.1 collective-permute-start.2
  8.9 0.0 collective-permute-done.1
  8.9 5.6 %collective-permute-done.2 = bf16[112,256]{1,0:T(8,128)(2,1)S(1)} collective-permute-done((bf16[112,256]{1,0:T(8,128)(2,1)S(1)}, bf16[112,256]{1,0:T(8,128)(2,1)S(1)}, u32[]{:S(2)}, u32[]{:S(2)}) %collective-permute-start.2) | collective-permute-done | bytes 57376 | tf_op jit(solution)/shard_map/ppermute | solution.py:28
  14.5 0.0 collective-permute-done.3
  14.5 1.6 %collective-permute-start.4 = (bf16[448,256]{1,0:T(8,128)(2,1)S(1)}, bf16[448,256]{1,0:T(8,128)(2,1)S(1)}, u32[]{:S(2)}, u32[]{:S(2)}) collective-permute-start(bf16[448,256]{1,0:T(8,128)(2,1)S(1)} %constant_dynamic-update-slice_fusion.refs_1_), channel_id=1, source_target_pairs={{0,4},{4,0},{8,12},{12,8},{16,20},{20,16},{24,28},{28,24},{1,5},{5... | collective-permute-start | bytes 688136 | tf_op jit(solution)/shard_map/ppermute | solution.py:28
  16.1 0.0 collective-permute-start.6
  16.1 0.7 %shard_map.52 = (f32[8,128]{1,0:T(8,128)S(1)}, f32[8,128]{1,0:T(8,128)S(1)}, f32[2,384,512]{2,1,0:T(8,128)S(1)}, bf16[384,256]{1,0:T(8,128)(2,1)S(1)}, f32[384,128]{1,0:T(8,128)S(1)}) custom-call(bf16[1024,256]{1,0:T(8,128)(2,1)S(1)} %get-tuple-element.39.x_ref.refs_0_, bf16[448,256]{1,0:T(8,128)(2,1)S(1)} %constant_dynamic-update-slice_fusion.refs_1_), custom_call_target="tpu_custom_call" | custom-call | flops 402653184 | bytes 1245184 | tf_op jit(solution)/shard_map/pallas_call | solution.py:336
  16.8 1.7 %collective-permute-done.refs_0_.refs_1_ = bf16[1024,256]{1,0:T(8,128)(2,1)S(1)} collective-permute-done((bf16[1024,256]{1,0:T(8,128)(2,1)}, bf16[1024,256]{1,0:T(8,128)(2,1)S(1)}, u32[]{:S(2)}, u32[]{:S(2)}) %collective-permute-start) | collective-permute-done | bytes 524320 | tf_op jit(solution)/shard_map/ppermute | solution.py:28
  18.4 0.4 shard_map.51.refs_4_
  18.8 0.7 %shard_map.53 = (f32[8,128]{1,0:T(8,128)S(1)}, f32[8,128]{1,0:T(8,128)S(1)}, f32[2,384,512]{2,1,0:T(8,128)S(1)}) custom-call(bf16[1024,256]{1,0:T(8,128)(2,1)S(1)} %collective-permute-done.refs_0_.refs_1_, bf16[384,256]{1,0:T(8,128)(2,1)S(1)} %get-tuple-element.44.refs_1_.refs_13_, f32[384,128]{1,0:T(8,128)S(1)} %get-tuple-element.45.refs_2_.refs_14_), custom_call_target="tpu_custom_call" | custom-call | flops 402653184 | bytes 1245184 | tf_op jit(solution)/shard_map/pallas_call | solution.py:336
  19.5 1.1 %collective-permute-done.4.refs_4_ = bf16[448,256]{1,0:T(8,128)(2,1)S(1)} collective-permute-done((bf16[448,256]{1,0:T(8,128)(2,1)S(1)}, bf16[448,256]{1,0:T(8,128)(2,1)S(1)}, u32[]{:S(2)}, u32[]{:S(2)}) %collective-permute-start.4) | collective-permute-done | bytes 229408 | tf_op jit(solution)/shard_map/ppermute | solution.py:28
  20.6 0.0 collective-permute-start.5
  20.6 0.0 collective-permute-done.6.refs_5_
  20.6 2.1 %shard_map.54 = (f32[16,128]{1,0:T(8,128)S(1)}, f32[16,128]{1,0:T(8,128)S(1)}, f32[4,768,512]{2,1,0:T(8,128)S(1)}, bf16[768,256]{1,0:T(8,128)(2,1)S(1)}, f32[768,128]{1,0:T(8,128)S(1)}) custom-call(bf16[1024,256]{1,0:T(8,128)(2,1)S(1)} %get-tuple-element.39.x_ref.refs_0_, bf16[1024,256]{1,0:T(8,128)(2,1)S(1)} %collective-permute-done.refs_0_.refs_1_, ...), custom_call_target="tpu_custom_call" | custom-call | flops 805306368 | bytes 1441792 | tf_op jit(solution)/shard_map/pallas_call | solution.py:336
  22.7 0.0 collective-permute-done.5.refs_3_
  22.7 1.2 %shard_map.55 = (f32[16,128]{1,0:T(8,128)S(1)}, f32[16,128]{1,0:T(8,128)S(1)}, f32[4,384,512]{2,1,0:T(8,128)S(1)}, bf16[384,256]{1,0:T(8,128)(2,1)S(1)}, f32[384,128]{1,0:T(8,128)S(1)}) custom-call(bf16[1024,256]{1,0:T(8,128)(2,1)S(1)} %get-tuple-element.39.x_ref.refs_0_, bf16[1024,256]{1,0:T(8,128)(2,1)S(1)} %collective-permute-done.refs_0_.refs_1_, ...), custom_call_target="tpu_custom_call" | custom-call | flops 402653184 | bytes 1245184 | tf_op jit(solution)/shard_map/pallas_call | solution.py:336
  23.9 0.7 %collective-permute-start.7 = (f32[16,128]{1,0:T(8,128)S(1)}, f32[16,128]{1,0:T(8,128)S(1)}, u32[]{:S(2)}, u32[]{:S(2)}) collective-permute-start(f32[16,128]{1,0:T(8,128)S(1)} %get-tuple-element.55.refs_2_), channel_id=1, source_target_pairs={{0,2},{1,3},{2,0},{3,1},{4,6},{5,7},{6,4},{7,5},{8,10},{9,11},{10,... | collective-permute-start | bytes 24584 | tf_op jit(solution)/shard_map/ppermute | solution.py:28
  24.6 3.0 %collective-permute-done.7.refs_3_ = f32[16,128]{1,0:T(8,128)S(1)} collective-permute-done((f32[16,128]{1,0:T(8,128)S(1)}, f32[16,128]{1,0:T(8,128)S(1)}, u32[]{:S(2)}, u32[]{:S(2)}) %collective-permute-start.7) | collective-permute-done | bytes 8224 | tf_op jit(solution)/shard_map/ppermute | solution.py:28
  27.6 6.9 %shard_map.56 = (f32[8,128]{1,0:T(8,128)}, f32[32,96]{1,0:T(8,128)S(1)}) custom-call(bf16[1024,256]{1,0:T(8,128)(2,1)S(1)} %get-tuple-element.39.x_ref.refs_0_, bf16[1024,256]{1,0:T(8,128)(2,1)S(1)} %collective-permute-done.refs_0_.refs_1_, f32[16,128]{1,0:T(8,128)S(1)} %get-tuple-element.55.refs_2_, f32[16,128]{1,0:T(8,128)S(1)} %collective-permute-done.7.refs_3_, ...), custom_call_target="tpu_custom_call" | custom-call | flops 1610612736 | bytes 1835008 | tf_op jit(solution)/shard_map/pallas_call | solution.py:375
  34.5 11.1 %all_to_all.12 = f32[32,1,96]{2,1,0:T(1,128)S(1)} all-to-all(f32[32,1,96]{2,1,0:T(1,128)S(1)} %bitcast.10), channel_id=1, replica_groups=mesh['gen'=8,'dat'=4] {'dat','gen'}, dimensions={0} | all-to-all | bytes 24576 | tf_op jit(solution)/shard_map/all_to_all | solution.py:399
  45.7 0.1 reduce_max.9
  45.7 0.5 %fusion = f32[96]{0:T(128)} fusion(f32[1,96]{1,0:T(1,128)S(1)} %get-tuple-element.70, f32[96]{0:T(128)S(1)} %reduce_max.9, f32[96]{0:T(128)S(1)} %exponential_reduce_fusion), kind=kLoop, calls=%fused_computation.5 | loop fusion | flops 480 | bytes 1536 | tf_op jit(solution)/shard_map/add | solution.py:402
  (4 shorter events, 0.0 us)
Async XLA Ops:
  1.8 7.2 %collective-permute-start.1 = (bf16[112,256]{1,0:T(8,128)(2,1)S(1)}, bf16[112,256]{1,0:T(8,128)(2,1)S(1)}, u32[]{:S(2)}, u32[]{:S(2)}) collective-permute-start(bf16[112,256]{1,0:T(8,128)(2,1)S(1)} %get-tuple-element.42), channel_id=1, source_target_pairs={{0,8},{4,12},{8,0},{12,4},{16,24},{20,28},{24,16},{28,20},{1,9},{5... | collective-permute-start | bytes 172040 | tf_op jit(solution)/shard_map/ppermute | solution.py:28
  4.8 13.6 %collective-permute-start = (bf16[1024,256]{1,0:T(8,128)(2,1)}, bf16[1024,256]{1,0:T(8,128)(2,1)S(1)}, u32[]{:S(2)}, u32[]{:S(2)}) collective-permute-start(bf16[1024,256]{1,0:T(8,128)(2,1)} %x_hbm_ref.1), channel_id=1, source_target_pairs={{0,2},{1,3},{2,0},{3,1},{4,6},{5,7},{6,4},{7,5},{8,10},{9,11},{10,... | collective-permute-start | bytes 1572872 | tf_op jit(solution)/shard_map/ppermute | solution.py:28
  6.3 8.2 %collective-permute-start.3 = (bf16[112,256]{1,0:T(8,128)(2,1)S(1)}, bf16[112,256]{1,0:T(8,128)(2,1)S(1)}, u32[]{:S(2)}, u32[]{:S(2)}) collective-permute-start(bf16[112,256]{1,0:T(8,128)(2,1)S(1)} %get-tuple-element.42), channel_id=1, source_target_pairs={{0,24},{4,28},{8,16},{12,20},{16,8},{20,12},{24,0},{28,4},{1,25},{... | collective-permute-start | bytes 172040 | tf_op jit(solution)/shard_map/ppermute | solution.py:28
  8.8 5.7 %collective-permute-start.2 = (bf16[112,256]{1,0:T(8,128)(2,1)S(1)}, bf16[112,256]{1,0:T(8,128)(2,1)S(1)}, u32[]{:S(2)}, u32[]{:S(2)}) collective-permute-start(bf16[112,256]{1,0:T(8,128)(2,1)S(1)} %get-tuple-element.42), channel_id=1, source_target_pairs={{0,16},{4,20},{8,24},{12,28},{16,0},{20,4},{24,8},{28,12},{1,17},{... | collective-permute-start | bytes 172040 | tf_op jit(solution)/shard_map/ppermute | solution.py:28
  14.5 6.1 %collective-permute-start.4 = (bf16[448,256]{1,0:T(8,128)(2,1)S(1)}, bf16[448,256]{1,0:T(8,128)(2,1)S(1)}, u32[]{:S(2)}, u32[]{:S(2)}) collective-permute-start(bf16[448,256]{1,0:T(8,128)(2,1)S(1)} %constant_dynamic-update-slice_fusion.refs_1_), channel_id=1, source_target_pairs={{0,4},{4,0},{8,12},{12,8},{16,20},{20,16},{24,28},{28,24},{1,5},{5... | collective-permute-start | bytes 688136 | tf_op jit(solution)/shard_map/ppermute | solution.py:28
  16.1 4.5 %collective-permute-start.6 = (bf16[448,256]{1,0:T(8,128)(2,1)S(1)}, bf16[448,256]{1,0:T(8,128)(2,1)S(1)}, u32[]{:S(2)}, u32[]{:S(2)}) collective-permute-start(bf16[448,256]{1,0:T(8,128)(2,1)S(1)} %constant_dynamic-update-slice_fusion.refs_1_), channel_id=1, source_target_pairs={{0,1},{1,0},{2,3},{3,2},{4,5},{5,4},{6,7},{7,6},{8,9},{9,8},{10,11... | collective-permute-start | bytes 688136 | tf_op jit(solution)/shard_map/ppermute | solution.py:28
  20.6 2.1 %collective-permute-start.5 = (bf16[448,256]{1,0:T(8,128)(2,1)S(1)}, bf16[448,256]{1,0:T(8,128)(2,1)S(1)}, u32[]{:S(2)}, u32[]{:S(2)}) collective-permute-start(bf16[448,256]{1,0:T(8,128)(2,1)S(1)} %collective-permute-done.4.refs_4_), channel_id=1, source_target_pairs={{0,1},{1,0},{2,3},{3,2},{4,5},{5,4},{6,7},{7,6},{8,9},{9,8},{10,11... | collective-permute-start | bytes 688136 | tf_op jit(solution)/shard_map/ppermute | solution.py:28
  23.9 3.7 %collective-permute-start.7 = (f32[16,128]{1,0:T(8,128)S(1)}, f32[16,128]{1,0:T(8,128)S(1)}, u32[]{:S(2)}, u32[]{:S(2)}) collective-permute-start(f32[16,128]{1,0:T(8,128)S(1)} %get-tuple-element.55.refs_2_), channel_id=1, source_target_pairs={{0,2},{1,3},{2,0},{3,1},{4,6},{5,7},{6,4},{7,5},{8,10},{9,11},{10,... | collective-permute-start | bytes 24584 | tf_op jit(solution)/shard_map/ppermute | solution.py:28

commit v14 on v13

--- a/solution.py
+++ b/solution.py
@@ -250,14 +250,16 @@
                 scale = [weights[k * repeat + i : k * repeat + i + 1, :] for i in range(repeat)]
                 pieces.append((e_ref, k, jnp.concatenate(scale, axis=1)))
 
-        def add(index, carry, pieces=pieces, offset=offset):
-            start = pl.multiple_of(index * tall, tall)
-            here = pl.ds(start, tall)
+        stride = math.gcd(e_ref.shape[1], 3 * tall)
+
+        def add(index, carry, pieces=pieces, offset=offset, stride=stride):
+            start = pl.multiple_of(index * stride, stride)
+            here = pl.ds(start, stride)
             parts = [fold(e_ref[k, here, :] * scale, jnp.add) for e_ref, k, scale in pieces]
-            sum_ref[pl.ds(offset + start, tall), :] = functools.reduce(jnp.add, parts)
+            sum_ref[pl.ds(offset + start, stride), :] = functools.reduce(jnp.add, parts)
             return carry
 
-        lax.fori_loop(0, e_ref.shape[1] // tall, add, 0)
+        lax.fori_loop(0, e_ref.shape[1] // stride, add, 0)
         offset += e_ref.shape[1]
     least = jnp.min(jnp.sum(sum_ref[...], axis=1, keepdims=True))
     top_ref[...] = jnp.full(top_ref.shape, -2.0 * LIFT, jnp.float32)

time: 46.4 us -> 46.3 us (level)
  no operation moved by 1% of the time
where the time goes in v14:
time: 46.3 us; the launch traced here: 46.1 us
  Pallas kernels  12.9 us (28%)
  waiting for transfers between devices  11.3 us (24%)
  blocking collectives  11.1 us (24%)
  starting transfers between devices  9.48 us (20%)
  between operations  0.67 us (1%)
  other arithmetic  0.61 us (1%)
    ppermute x8, waiting for transfers between devices, swap(): lax.ppermute(value, axis, [(k, k ^ mask) for k in range(lax.axis_size(axi...  11.3 us
    all_to_all x1, blocking collectives, per_device(): totals = lax.all_to_all(col, ('dat', 'gen'), 0, 0, tiled=True)  11.1 us
    ppermute x8, starting transfers between devices, swap(): lax.ppermute(value, axis, [(k, k ^ mask) for k in range(lax.axis_size(axi...  9.48 us
    pallas_call x1, Pallas kernels, per_device(): pl.pallas_call(functools.partial(column_kernel, count=len(xs), share=shar...  6.78 us
    pallas_call x4, Pallas kernels, row_pass(): pl.pallas_call(functools.partial(row_kernel, count=len(rows_of), share=sh...  4.64 us
    pallas_call x1, Pallas kernels, per_device(): pl.pallas_call(pack_kernel, out_shape=(jax.ShapeDtypeStruct((span, width)...  1.11 us
  transfers between devices with their start and end apart: 8, of which 4 were waited for; matrix products, arithmetic and copies ran while one was open for 0% of the time, Pallas kernels for 8%

profile of v14, /device:TPU:0, one launch (start us, length us, event | category | flops | bytes accessed | tf_op | source)
XLA Modules:
  0.0 46.1 jit_solution(12733494739059848955)
XLA Ops:
  0.6 1.1 %shard_map.50 = (bf16[112,256]{1,0:T(8,128)(2,1)S(1)}, bf16[448,256]{1,0:T(8,128)(2,1)S(1)}, f32[1,96]{1,0:T(1,128)S(1)}, bf16[1024,256]{1,0:T(8,128)(2,1)S(1)}) custom-call(bf16[96,256]{1,0:T(8,128)(2,1)} %y_hbm_ref.1, f32[1,96]{1,0:T(1,128)} %bitcast.12, bf16[1024,256]{1,0:T(8,128)(2,1)} %x_hbm_ref.1), custom_call_target="tpu_custom_call" | custom-call | tf_op jit(solution)/shard_map/pallas_call | solution.py:295
  1.8 3.1 %collective-permute-start.1 = (bf16[112,256]{1,0:T(8,128)(2,1)S(1)}, bf16[112,256]{1,0:T(8,128)(2,1)S(1)}, u32[]{:S(2)}, u32[]{:S(2)}) collective-permute-start(bf16[112,256]{1,0:T(8,128)(2,1)S(1)} %get-tuple-element.42), channel_id=1, source_target_pairs={{0,8},{4,12},{8,0},{12,4},{16,24},{20,28},{24,16},{28,20},{1,9},{5... | collective-permute-start | bytes 172040 | tf_op jit(solution)/shard_map/ppermute | solution.py:28
  4.8 1.5 %collective-permute-start = (bf16[1024,256]{1,0:T(8,128)(2,1)}, bf16[1024,256]{1,0:T(8,128)(2,1)S(1)}, u32[]{:S(2)}, u32[]{:S(2)}) collective-permute-start(bf16[1024,256]{1,0:T(8,128)(2,1)} %x_hbm_ref.1), channel_id=1, source_target_pairs={{0,2},{1,3},{2,0},{3,1},{4,6},{5,7},{6,4},{7,5},{8,10},{9,11},{10,... | collective-permute-start | bytes 1572872 | tf_op jit(solution)/shard_map/ppermute | solution.py:28
  6.3 2.5 %collective-permute-start.3 = (bf16[112,256]{1,0:T(8,128)(2,1)S(1)}, bf16[112,256]{1,0:T(8,128)(2,1)S(1)}, u32[]{:S(2)}, u32[]{:S(2)}) collective-permute-start(bf16[112,256]{1,0:T(8,128)(2,1)S(1)} %get-tuple-element.42), channel_id=1, source_target_pairs={{0,24},{4,28},{8,16},{12,20},{16,8},{20,12},{24,0},{28,4},{1,25},{... | collective-permute-start | bytes 172040 | tf_op jit(solution)/shard_map/ppermute | solution.py:28
  8.8 0.1 collective-permute-start.2
  8.9 0.0 collective-permute-done.1
  8.9 5.6 %collective-permute-done.2 = bf16[112,256]{1,0:T(8,128)(2,1)S(1)} collective-permute-done((bf16[112,256]{1,0:T(8,128)(2,1)S(1)}, bf16[112,256]{1,0:T(8,128)(2,1)S(1)}, u32[]{:S(2)}, u32[]{:S(2)}) %collective-permute-start.2) | collective-permute-done | bytes 57376 | tf_op jit(solution)/shard_map/ppermute | solution.py:28
  14.5 0.0 collective-permute-done.3
  14.5 1.6 %collective-permute-start.4 = (bf16[448,256]{1,0:T(8,128)(2,1)S(1)}, bf16[448,256]{1,0:T(8,128)(2,1)S(1)}, u32[]{:S(2)}, u32[]{:S(2)}) collective-permute-start(bf16[448,256]{1,0:T(8,128)(2,1)S(1)} %constant_dynamic-update-slice_fusion.refs_1_), channel_id=1, source_target_pairs={{0,4},{4,0},{8,12},{12,8},{16,20},{20,16},{24,28},{28,24},{1,5},{5... | collective-permute-start | bytes 688136 | tf_op jit(solution)/shard_map/ppermute | solution.py:28
  16.1 0.0 collective-permute-start.6
  16.1 0.7 %shard_map.52 = (f32[8,128]{1,0:T(8,128)S(1)}, f32[8,128]{1,0:T(8,128)S(1)}, f32[2,384,512]{2,1,0:T(8,128)S(1)}, bf16[384,256]{1,0:T(8,128)(2,1)S(1)}, f32[384,128]{1,0:T(8,128)S(1)}) custom-call(bf16[1024,256]{1,0:T(8,128)(2,1)S(1)} %get-tuple-element.39.x_ref.refs_0_, bf16[448,256]{1,0:T(8,128)(2,1)S(1)} %constant_dynamic-update-slice_fusion.refs_1_), custom_call_target="tpu_custom_call" | custom-call | flops 402653184 | bytes 1245184 | tf_op jit(solution)/shard_map/pallas_call | solution.py:338
  16.8 1.7 %collective-permute-done.refs_0_.refs_1_ = bf16[1024,256]{1,0:T(8,128)(2,1)S(1)} collective-permute-done((bf16[1024,256]{1,0:T(8,128)(2,1)}, bf16[1024,256]{1,0:T(8,128)(2,1)S(1)}, u32[]{:S(2)}, u32[]{:S(2)}) %collective-permute-start) | collective-permute-done | bytes 524320 | tf_op jit(solution)/shard_map/ppermute | solution.py:28
  18.4 0.4 shard_map.51.refs_4_
  18.8 0.7 %shard_map.53 = (f32[8,128]{1,0:T(8,128)S(1)}, f32[8,128]{1,0:T(8,128)S(1)}, f32[2,384,512]{2,1,0:T(8,128)S(1)}) custom-call(bf16[1024,256]{1,0:T(8,128)(2,1)S(1)} %collective-permute-done.refs_0_.refs_1_, bf16[384,256]{1,0:T(8,128)(2,1)S(1)} %get-tuple-element.44.refs_1_.refs_13_, f32[384,128]{1,0:T(8,128)S(1)} %get-tuple-element.45.refs_2_.refs_14_), custom_call_target="tpu_custom_call" | custom-call | flops 402653184 | bytes 1245184 | tf_op jit(solution)/shard_map/pallas_call | solution.py:338
  19.5 1.1 %collective-permute-done.4.refs_4_ = bf16[448,256]{1,0:T(8,128)(2,1)S(1)} collective-permute-done((bf16[448,256]{1,0:T(8,128)(2,1)S(1)}, bf16[448,256]{1,0:T(8,128)(2,1)S(1)}, u32[]{:S(2)}, u32[]{:S(2)}) %collective-permute-start.4) | collective-permute-done | bytes 229408 | tf_op jit(solution)/shard_map/ppermute | solution.py:28
  20.6 0.0 collective-permute-start.5
  20.6 0.0 collective-permute-done.6.refs_5_
  20.6 2.1 %shard_map.54 = (f32[16,128]{1,0:T(8,128)S(1)}, f32[16,128]{1,0:T(8,128)S(1)}, f32[4,768,512]{2,1,0:T(8,128)S(1)}, bf16[768,256]{1,0:T(8,128)(2,1)S(1)}, f32[768,128]{1,0:T(8,128)S(1)}) custom-call(bf16[1024,256]{1,0:T(8,128)(2,1)S(1)} %get-tuple-element.39.x_ref.refs_0_, bf16[1024,256]{1,0:T(8,128)(2,1)S(1)} %collective-permute-done.refs_0_.refs_1_, ...), custom_call_target="tpu_custom_call" | custom-call | flops 805306368 | bytes 1441792 | tf_op jit(solution)/shard_map/pallas_call | solution.py:338
  22.7 0.0 collective-permute-done.5.refs_3_
  22.7 1.2 %shard_map.55 = (f32[16,128]{1,0:T(8,128)S(1)}, f32[16,128]{1,0:T(8,128)S(1)}, f32[4,384,512]{2,1,0:T(8,128)S(1)}, bf16[384,256]{1,0:T(8,128)(2,1)S(1)}, f32[384,128]{1,0:T(8,128)S(1)}) custom-call(bf16[1024,256]{1,0:T(8,128)(2,1)S(1)} %get-tuple-element.39.x_ref.refs_0_, bf16[1024,256]{1,0:T(8,128)(2,1)S(1)} %collective-permute-done.refs_0_.refs_1_, ...), custom_call_target="tpu_custom_call" | custom-call | flops 402653184 | bytes 1245184 | tf_op jit(solution)/shard_map/pallas_call | solution.py:338
  23.9 0.7 %collective-permute-start.7 = (f32[16,128]{1,0:T(8,128)S(1)}, f32[16,128]{1,0:T(8,128)S(1)}, u32[]{:S(2)}, u32[]{:S(2)}) collective-permute-start(f32[16,128]{1,0:T(8,128)S(1)} %get-tuple-element.55.refs_2_), channel_id=1, source_target_pairs={{0,2},{1,3},{2,0},{3,1},{4,6},{5,7},{6,4},{7,5},{8,10},{9,11},{10,... | collective-permute-start | bytes 24584 | tf_op jit(solution)/shard_map/ppermute | solution.py:28
  24.6 3.0 %collective-permute-done.7.refs_3_ = f32[16,128]{1,0:T(8,128)S(1)} collective-permute-done((f32[16,128]{1,0:T(8,128)S(1)}, f32[16,128]{1,0:T(8,128)S(1)}, u32[]{:S(2)}, u32[]{:S(2)}) %collective-permute-start.7) | collective-permute-done | bytes 8224 | tf_op jit(solution)/shard_map/ppermute | solution.py:28
  27.6 6.8 %shard_map.56 = (f32[8,128]{1,0:T(8,128)}, f32[32,96]{1,0:T(8,128)S(1)}) custom-call(bf16[1024,256]{1,0:T(8,128)(2,1)S(1)} %get-tuple-element.39.x_ref.refs_0_, bf16[1024,256]{1,0:T(8,128)(2,1)S(1)} %collective-permute-done.refs_0_.refs_1_, f32[16,128]{1,0:T(8,128)S(1)} %get-tuple-element.55.refs_2_, f32[16,128]{1,0:T(8,128)S(1)} %collective-permute-done.7.refs_3_, ...), custom_call_target="tpu_custom_call" | custom-call | flops 1610612736 | bytes 1835008 | tf_op jit(solution)/shard_map/pallas_call | solution.py:377
  34.4 11.1 %all_to_all.12 = f32[32,1,96]{2,1,0:T(1,128)S(1)} all-to-all(f32[32,1,96]{2,1,0:T(1,128)S(1)} %bitcast.10), channel_id=1, replica_groups=mesh['gen'=8,'dat'=4] {'dat','gen'}, dimensions={0} | all-to-all | bytes 24576 | tf_op jit(solution)/shard_map/all_to_all | solution.py:401
  45.5 0.1 reduce_max.9
  45.6 0.5 %fusion = f32[96]{0:T(128)} fusion(f32[1,96]{1,0:T(1,128)S(1)} %get-tuple-element.70, f32[96]{0:T(128)S(1)} %reduce_max.9, f32[96]{0:T(128)S(1)} %exponential_reduce_fusion), kind=kLoop, calls=%fused_computation.5 | loop fusion | flops 480 | bytes 1536 | tf_op jit(solution)/shard_map/add | solution.py:404
  (4 shorter events, 0.0 us)
Async XLA Ops:
  1.8 7.2 %collective-permute-start.1 = (bf16[112,256]{1,0:T(8,128)(2,1)S(1)}, bf16[112,256]{1,0:T(8,128)(2,1)S(1)}, u32[]{:S(2)}, u32[]{:S(2)}) collective-permute-start(bf16[112,256]{1,0:T(8,128)(2,1)S(1)} %get-tuple-element.42), channel_id=1, source_target_pairs={{0,8},{4,12},{8,0},{12,4},{16,24},{20,28},{24,16},{28,20},{1,9},{5... | collective-permute-start | bytes 172040 | tf_op jit(solution)/shard_map/ppermute | solution.py:28
  4.8 13.6 %collective-permute-start = (bf16[1024,256]{1,0:T(8,128)(2,1)}, bf16[1024,256]{1,0:T(8,128)(2,1)S(1)}, u32[]{:S(2)}, u32[]{:S(2)}) collective-permute-start(bf16[1024,256]{1,0:T(8,128)(2,1)} %x_hbm_ref.1), channel_id=1, source_target_pairs={{0,2},{1,3},{2,0},{3,1},{4,6},{5,7},{6,4},{7,5},{8,10},{9,11},{10,... | collective-permute-start | bytes 1572872 | tf_op jit(solution)/shard_map/ppermute | solution.py:28
  6.3 8.2 %collective-permute-start.3 = (bf16[112,256]{1,0:T(8,128)(2,1)S(1)}, bf16[112,256]{1,0:T(8,128)(2,1)S(1)}, u32[]{:S(2)}, u32[]{:S(2)}) collective-permute-start(bf16[112,256]{1,0:T(8,128)(2,1)S(1)} %get-tuple-element.42), channel_id=1, source_target_pairs={{0,24},{4,28},{8,16},{12,20},{16,8},{20,12},{24,0},{28,4},{1,25},{... | collective-permute-start | bytes 172040 | tf_op jit(solution)/shard_map/ppermute | solution.py:28
  8.8 5.7 %collective-permute-start.2 = (bf16[112,256]{1,0:T(8,128)(2,1)S(1)}, bf16[112,256]{1,0:T(8,128)(2,1)S(1)}, u32[]{:S(2)}, u32[]{:S(2)}) collective-permute-start(bf16[112,256]{1,0:T(8,128)(2,1)S(1)} %get-tuple-element.42), channel_id=1, source_target_pairs={{0,16},{4,20},{8,24},{12,28},{16,0},{20,4},{24,8},{28,12},{1,17},{... | collective-permute-start | bytes 172040 | tf_op jit(solution)/shard_map/ppermute | solution.py:28
  14.5 6.1 %collective-permute-start.4 = (bf16[448,256]{1,0:T(8,128)(2,1)S(1)}, bf16[448,256]{1,0:T(8,128)(2,1)S(1)}, u32[]{:S(2)}, u32[]{:S(2)}) collective-permute-start(bf16[448,256]{1,0:T(8,128)(2,1)S(1)} %constant_dynamic-update-slice_fusion.refs_1_), channel_id=1, source_target_pairs={{0,4},{4,0},{8,12},{12,8},{16,20},{20,16},{24,28},{28,24},{1,5},{5... | collective-permute-start | bytes 688136 | tf_op jit(solution)/shard_map/ppermute | solution.py:28
  16.1 4.5 %collective-permute-start.6 = (bf16[448,256]{1,0:T(8,128)(2,1)S(1)}, bf16[448,256]{1,0:T(8,128)(2,1)S(1)}, u32[]{:S(2)}, u32[]{:S(2)}) collective-permute-start(bf16[448,256]{1,0:T(8,128)(2,1)S(1)} %constant_dynamic-update-slice_fusion.refs_1_), channel_id=1, source_target_pairs={{0,1},{1,0},{2,3},{3,2},{4,5},{5,4},{6,7},{7,6},{8,9},{9,8},{10,11... | collective-permute-start | bytes 688136 | tf_op jit(solution)/shard_map/ppermute | solution.py:28
  20.6 2.1 %collective-permute-start.5 = (bf16[448,256]{1,0:T(8,128)(2,1)S(1)}, bf16[448,256]{1,0:T(8,128)(2,1)S(1)}, u32[]{:S(2)}, u32[]{:S(2)}) collective-permute-start(bf16[448,256]{1,0:T(8,128)(2,1)S(1)} %collective-permute-done.4.refs_4_), channel_id=1, source_target_pairs={{0,1},{1,0},{2,3},{3,2},{4,5},{5,4},{6,7},{7,6},{8,9},{9,8},{10,11... | collective-permute-start | bytes 688136 | tf_op jit(solution)/shard_map/ppermute | solution.py:28
  23.9 3.7 %collective-permute-start.7 = (f32[16,128]{1,0:T(8,128)S(1)}, f32[16,128]{1,0:T(8,128)S(1)}, u32[]{:S(2)}, u32[]{:S(2)}) collective-permute-start(f32[16,128]{1,0:T(8,128)S(1)} %get-tuple-element.55.refs_2_), channel_id=1, source_target_pairs={{0,2},{1,3},{2,0},{3,1},{4,6},{5,7},{6,4},{7,5},{8,10},{9,11},{10,... | collective-permute-start | bytes 24584 | tf_op jit(solution)/shard_map/ppermute | solution.py:28
